TPU v7x, 256 devices: a whole 4x4x8 slice. The times are simulated.
256 devices in a mesh: pipe: 32 (over z, y), tensor: 8 (over x, core).
Axes of the slice: x: 4, y: 4, z: 8, core: 2. Of those that a mesh axis runs over, the one named last changes fastest.
Arguments:
- gate_pre: bfloat16 [256, 53248], P(None, 'pipe'), may hold values from -8 to 8
- up_pre: bfloat16 [256, 53248], P(None, 'pipe'), may hold values from -8 to 8
- down_codes: bfloat16 [53248, 16384], P('pipe', 'tensor'), may hold values from -6 to 6, as said below
- down_scales: bfloat16 [3328, 16384], P('pipe', 'tensor'), may hold values from 0.5 to 2
- weight_scale: float32 [1], replicated, may hold values from 0.0017334381 to 0.0043335953
- residual: bfloat16 [256, 16384], P('pipe', 'tensor'), may hold values from -17 to 17
- norm_gain: bfloat16 [16384], P('tensor'), may hold values from 0.5 to 1.5
Outputs:
- payload: bfloat16 [256, 53248], P(None, 'pipe')
- block_scales: float32 [256, 3328], P(None, 'pipe')
- new_residual: bfloat16 [256, 16384], P('pipe', 'tensor')
- normed: bfloat16 [256, 16384], P('pipe', 'tensor')
Inputs may be any that keep to these rules, and one draw needn't show every extreme that they name: Every entry of down_codes is 0 or plus or minus 0.5, 1, 1.5, 2, 3, 4 or 6.
All inputs are finite; a program needn't handle non-finite values. Where the computation divides by a largest or mean magnitude, that divisor is 1e-20 or more.
Results may differ from a plain program's by a relative error of at most 0.0085.
Values sent between devices are 32-bit elements; how exact they have to be, the bound alone decides.
No kernel may reach another device: no remote copies, remote signals or barrier semaphores. Data moves between devices by JAX's collectives and lax.ppermute only.
A program may use at most 128 MiB of HBM per device.

v0:
```python
import math

import jax
import jax.numpy as jnp
from jax import lax
from jax.sharding import PartitionSpec as P


def swapped(block, axis, bit):
    count = lax.axis_size(axis)
    route = []
    for low in range(count):
        high = low | 1 << bit
        if high != low and high < count:
            route += [(low, high), (high, low)]
    return lax.ppermute(block, axis, route)


def sylvester_signs(order_size):
    indices = jnp.arange(order_size, dtype=jnp.int32)
    intersection = jnp.bitwise_and(indices[:, None], indices[None, :])
    parity = jnp.zeros((order_size, order_size), jnp.int32)
    for level in range(order_size.bit_length() - 1):
        parity = parity + jnp.bitwise_and(jnp.right_shift(intersection, level), 1)
    return (1 - 2 * (parity % 2)).astype(jnp.float32)


def on_device(gate_pre, up_pre, down_codes, down_scales, weight_scale, residual, norm_gain):
    row_count, local_width = gate_pre.shape
    pipe_count = lax.axis_size("pipe")
    groups = local_width // 128
    hidden = (jax.nn.silu(gate_pre.astype(jnp.float32)) * up_pre.astype(jnp.float32)).astype(
        jnp.bfloat16
    )
    signs_inner = sylvester_signs(128).astype(jnp.bfloat16)
    inner = jnp.dot(
        hidden.reshape(row_count * groups, 128), signs_inner, preferred_element_type=jnp.float32
    ).reshape(row_count, groups, 128)
    mixed = inner
    position = lax.axis_index("pipe")
    for level in range(pipe_count.bit_length() - 1):
        partner = swapped(mixed, "pipe", level)
        upper_half = jnp.bitwise_and(jnp.right_shift(position, level), 1) == 1
        mixed = jnp.where(upper_half, partner - mixed, mixed + partner)
    rotated = mixed * (1.0 / math.sqrt(128 * pipe_count))
    peak_value = lax.pmax(jnp.max(jnp.abs(rotated)), "pipe")
    blocks = rotated.reshape(row_count, groups, 8, 16)
    block_bound = jnp.maximum(jnp.max(jnp.abs(blocks), axis=3), peak_value / 64.0)
    block_scales = (448.0 * block_bound / peak_value).reshape(row_count, groups * 8)
    payload = (6.0 * blocks / block_bound[..., None]).astype(jnp.bfloat16)
    dequant = (
        (payload.astype(jnp.float32) * block_bound[..., None] / 6.0)
        .astype(jnp.bfloat16)
        .reshape(row_count, local_width)
    )
    code_rows, model_cols = down_codes.shape
    weight = (
        (
            down_codes.reshape(code_rows // 16, 16, model_cols).astype(jnp.float32)
            * down_scales[:, None, :].astype(jnp.float32)
            * weight_scale[0]
        )
        .reshape(code_rows, model_cols)
        .astype(jnp.bfloat16)
    )
    row_share = row_count // pipe_count
    total_sum = lax.psum(jnp.dot(dequant, weight, preferred_element_type=jnp.float32), "pipe")
    own_rows = lax.dynamic_slice_in_dim(total_sum, lax.axis_index("pipe") * row_share, row_share, 0)
    summed = residual.astype(jnp.float32) + own_rows
    mean_square = lax.psum(jnp.sum(summed * summed, axis=1), "tensor") / (
        model_cols * lax.axis_size("tensor")
    )
    normed = (
        summed * lax.rsqrt(mean_square + 1e-05)[:, None] * norm_gain.astype(jnp.float32)
    ).astype(jnp.bfloat16)
    return (
        payload.reshape(row_count, local_width),
        block_scales,
        summed.astype(jnp.bfloat16),
        normed,
    )


def solution(mesh):
    in_specs = (
        P(None, "pipe"),
        P(None, "pipe"),
        P("pipe", "tensor"),
        P("pipe", "tensor"),
        P(),
        P("pipe", "tensor"),
        P("tensor"),
    )
    out_specs = (P(None, "pipe"), P(None, "pipe"), P("pipe", "tensor"), P("pipe", "tensor"))
    return jax.shard_map(
        on_device, mesh=mesh, in_specs=in_specs, out_specs=out_specs, check_vma=False
    )
```

profile of v0, /device:TPU:1, one launch (start us, length us, event | category | flops | bytes accessed | tf_op | source)
XLA Modules:
  0.0 548.8 jit_solution(8178520057315777336)
XLA Ops:
  7.2 0.0 copy-start
  7.2 0.0 all-reduce.2.cloned.1.call-start
  7.2 1.6 copy.14
  8.8 0.0 copy-done
  8.8 0.6 copy.15
  9.4 0.6 fusion.9
  10.0 0.4 fusion.17
  10.5 2.2 collective-permute-start
  12.7 35.7 %collective-permute-done = f32[256,13,128]{0,2,1:T(8,128)} collective-permute-done((f32[256,13,128]{0,2,1:T(8,128)S(1)}, f32[256,13,128]{0,2,1:T(8,128)}, u32[]{:S(2)}, u32[]{:S(2)}) %collective-permute-start) | collective-permute-done | bytes 1703968 | tf_op jit(solution)/shard_map/ppermute | solution.py:16
  48.4 1.7 add_select_fusion.4
  50.0 4.2 collective-permute-start.1
  54.2 35.9 %collective-permute-done.1 = f32[256,13,128]{0,2,1:T(8,128)} collective-permute-done((f32[256,13,128]{0,2,1:T(8,128)S(1)}, f32[256,13,128]{0,2,1:T(8,128)}, u32[]{:S(2)}, u32[]{:S(2)}) %collective-permute-start.1) | collective-permute-done | bytes 1703968 | tf_op jit(solution)/shard_map/ppermute | solution.py:16
  90.1 1.7 add_select_fusion.3
  91.8 1.7 collective-permute-start.2
  93.5 35.1 %collective-permute-done.2 = f32[256,13,128]{0,2,1:T(8,128)} collective-permute-done((f32[256,13,128]{0,2,1:T(8,128)S(1)}, f32[256,13,128]{0,2,1:T(8,128)}, u32[]{:S(2)}, u32[]{:S(2)}) %collective-permute-start.2) | collective-permute-done | bytes 1703968 | tf_op jit(solution)/shard_map/ppermute | solution.py:16
  128.6 1.7 add_select_fusion.2
  130.3 3.0 collective-permute-start.3
  133.3 73.2 %collective-permute-done.3 = f32[256,13,128]{0,2,1:T(8,128)} collective-permute-done((f32[256,13,128]{0,2,1:T(8,128)S(1)}, f32[256,13,128]{0,2,1:T(8,128)}, u32[]{:S(2)}, u32[]{:S(2)}) %collective-permute-start.3) | collective-permute-done | bytes 1703968 | tf_op jit(solution)/shard_map/ppermute | solution.py:16
  206.5 1.7 add_select_fusion.1
  208.2 6.6 %collective-permute-start.4 = (f32[256,13,128]{0,2,1:T(8,128)S(1)}, f32[256,13,128]{0,2,1:T(8,128)S(1)}, u32[]{:S(2)}, u32[]{:S(2)}) collective-permute-start(f32[256,13,128]{0,2,1:T(8,128)S(1)} %add_select_fusion.1), channel_id=1, source_target_pairs={{0,128},{128,0},{8,136},{136,8},{16,144},{144,16},{24,152},{152,24... | collective-permute-start | bytes 5111816 | tf_op jit(solution)/shard_map/ppermute | solution.py:16
  214.8 1.1 convert_element_type.61
  216.5 8.3 %fusion.1 = bf16[1664,2048]{1,0:T(8,128)(2,1)} fusion(bf16[1664,2048]{1,0:T(8,128)(2,1)} %param.9, f32[]{:T(128)} %bitcast.31, f32[104,2048]{1,0:T(8,128)S(1)} %convert_element_type.61), kind=kLoop, calls=%fused_computation.2 | loop fusion | flops 13631488 | bytes 14483460 | tf_op jit(solution)/shard_map/convert_element_type | solution.py:64
  224.9 63.4 %collective-permute-done.4 = f32[256,13,128]{0,2,1:T(8,128)S(1)} collective-permute-done((f32[256,13,128]{0,2,1:T(8,128)S(1)}, f32[256,13,128]{0,2,1:T(8,128)S(1)}, u32[]{:S(2)}, u32[]{:S(2)}) %collective-permute-start.4) | collective-permute-done | bytes 1703968 | tf_op jit(solution)/shard_map/ppermute | solution.py:16
  288.3 0.9 fusion.10
  289.2 0.2 broadcast_multiply_fusion
  289.4 0.3 bitcast_reduce_fusion
  289.7 61.9 %pmax.7 = f32[]{:T(128)} all-reduce(f32[]{:T(128)} %get-tuple-element.12), channel_id=1, replica_groups=mesh['pipe'=32,'tensor'=8] {'pipe'}, use_global_device_ids=true, to_apply=%region_2.3 | all-reduce | flops 1 | bytes 8 | tf_op jit(solution)/shard_map/pmax | solution.py:46
  352.3 1.3 divide_bitcast_fusion
  353.6 0.4 fusion.8
  354.0 6.4 %fusion.35 = f32[256,2048]{1,0:T(8,128)} fusion(bf16[256,1664]{0,1:T(8,128)(2,1)S(1)} %get-tuple-element.8, bf16[1664,2048]{1,0:T(8,128)(2,1)} %fusion.1), kind=kOutput, calls=%fused_computation.55 | convolution fusion | flops 1744830464 | bytes 9764864 | tf_op jit(solution)/shard_map/dot_general | solution.py:67
  360.4 0.0 copy-start.2
  360.4 0.0 copy-start.1
  360.4 0.0 all-reduce.2.cloned.1.call-update
  360.4 0.7 copy-done.2
  361.1 160.1 %all-reduce.2.cloned.1.call-done = f32[256,2048]{1,0:T(8,128)} async-done(((f32[256,2048]{1,0:T(8,128)}), f32[256,2048]{1,0:T(8,128)}) %all-reduce.2.cloned.1.call-update) | async-done | bytes 2097168 | tf_op jit(solution)/shard_map/psum | solution.py:67
  521.2 0.0 copy-done.1
  521.2 1.0 multiply_reduce_fusion
  522.1 1.3 copy.17
  523.5 16.9 %psum.15 = f32[8]{0:T(128)S(1)} all-reduce(f32[8]{0:T(128)S(1)} %multiply_reduce_fusion), channel_id=1, replica_groups=mesh['pipe'=32,'tensor'=8] {'tensor'}, use_global_device_ids=true, to_apply=%region_5.6 | all-reduce | flops 8 | bytes 64 | tf_op jit(solution)/shard_map/psum | solution.py:70
  540.4 1.5 multiply_convert_fusion
  (2 shorter events, 0.0 us)
Async XLA Ops:
  7.2 1.7 copy-start
  7.2 514.0 %all-reduce.2.cloned.1.call-start = ((), (), s32[]{:S(2)}) async-start(), calls=%async_computation | async-start | bytes 4194304 | tf_op jit(solution)/shard_map/psum | solution.py:67
  10.5 37.9 %collective-permute-start = (f32[256,13,128]{0,2,1:T(8,128)S(1)}, f32[256,13,128]{0,2,1:T(8,128)}, u32[]{:S(2)}, u32[]{:S(2)}) collective-permute-start(f32[256,13,128]{0,2,1:T(8,128)S(1)} %fusion.17), channel_id=1, source_target_pairs={{0,8},{8,0},{16,24},{24,16},{32,40},{40,32},{48,56},{56,48},{64,72... | collective-permute-start | bytes 5111816 | tf_op jit(solution)/shard_map/ppermute | solution.py:16
  50.0 40.1 %collective-permute-start.1 = (f32[256,13,128]{0,2,1:T(8,128)S(1)}, f32[256,13,128]{0,2,1:T(8,128)}, u32[]{:S(2)}, u32[]{:S(2)}) collective-permute-start(f32[256,13,128]{0,2,1:T(8,128)S(1)} %add_select_fusion.4), channel_id=1, source_target_pairs={{0,16},{16,0},{8,24},{24,8},{32,48},{48,32},{40,56},{56,40},{64,80... | collective-permute-start | bytes 5111816 | tf_op jit(solution)/shard_map/ppermute | solution.py:16
  91.8 36.8 %collective-permute-start.2 = (f32[256,13,128]{0,2,1:T(8,128)S(1)}, f32[256,13,128]{0,2,1:T(8,128)}, u32[]{:S(2)}, u32[]{:S(2)}) collective-permute-start(f32[256,13,128]{0,2,1:T(8,128)S(1)} %add_select_fusion.3), channel_id=1, source_target_pairs={{0,32},{32,0},{8,40},{40,8},{16,48},{48,16},{24,56},{56,24},{64,96... | collective-permute-start | bytes 5111816 | tf_op jit(solution)/shard_map/ppermute | solution.py:16
  130.3 76.2 %collective-permute-start.3 = (f32[256,13,128]{0,2,1:T(8,128)S(1)}, f32[256,13,128]{0,2,1:T(8,128)}, u32[]{:S(2)}, u32[]{:S(2)}) collective-permute-start(f32[256,13,128]{0,2,1:T(8,128)S(1)} %add_select_fusion.2), channel_id=1, source_target_pairs={{0,64},{64,0},{8,72},{72,8},{16,80},{80,16},{24,88},{88,24},{32,96... | collective-permute-start | bytes 5111816 | tf_op jit(solution)/shard_map/ppermute | solution.py:16
  208.2 80.1 %collective-permute-start.4 = (f32[256,13,128]{0,2,1:T(8,128)S(1)}, f32[256,13,128]{0,2,1:T(8,128)S(1)}, u32[]{:S(2)}, u32[]{:S(2)}) collective-permute-start(f32[256,13,128]{0,2,1:T(8,128)S(1)} %add_select_fusion.1), channel_id=1, source_target_pairs={{0,128},{128,0},{8,136},{136,8},{16,144},{144,16},{24,152},{152,24... | collective-permute-start | bytes 5111816 | tf_op jit(solution)/shard_map/ppermute | solution.py:16
  360.4 0.7 copy-start.2
  360.4 160.8 %copy-start.1 = (bf16[8,2048]{1,0:T(8,128)(2,1)S(1)}, bf16[8,2048]{1,0:T(8,128)(2,1)}, u32[]{:S(2)}) copy-start(bf16[8,2048]{1,0:T(8,128)(2,1)} %param.12) | copy-start | bytes 98308
Sparse Core Ops, SparseCore 0:
  360.5 160.5 all-reduce.1
where the time goes:
time: 549 us
  waiting for transfers between devices  403 us (73%)
  blocking collectives  78.8 us (14%)
  other arithmetic  22.4 us (4%)
  starting transfers between devices  17.7 us (3%)
  between operations  15.4 us (3%)
  matrix products  6.84 us (1%)
    ppermute x5, waiting for transfers between devices, swapped(): return lax.ppermute(block, axis, route)  243 us
    psum x1, waiting for transfers between devices, on_device(): lax.psum(jnp.dot(dequant, weight, preferred_element_type=jnp.float32), 'p...  160 us
    pmax x1, blocking collectives, on_device(): peak_value = lax.pmax(jnp.max(jnp.abs(rotated)), 'pipe')  61.9 us
    ppermute x5, starting transfers between devices, swapped(): return lax.ppermute(block, axis, route)  17.7 us
    psum x1, blocking collectives, on_device(): lax.psum(jnp.sum(summed * summed, axis=1), 'tensor')  16.9 us
  transfers between devices with their start and end apart: 6, of which 6 were waited for; matrix products, arithmetic and copies ran while one was open for 2% of the time, Pallas kernels for 0%

commit v1 on v0

v1 whole, which is shorter than its diff:
```python
import functools

import jax
import jax.numpy as jnp
import numpy as np
from jax import lax
from jax.experimental import pallas as pl
from jax.experimental.pallas import tpu as pltpu
from jax.sharding import Mesh
from jax.sharding import PartitionSpec as P

NZ, NY, NX, NC = 8, 4, 4, 2
N_PIPE, N_TENSOR = NZ * NY, NX * NC
ROWS, GROUPS, INNER = 256, 13, 128
WIDTH = GROUPS * INNER
COLS = 2048
WIDE = COLS + 128
SLAB = ROWS // N_TENSOR
OWN = ROWS // N_PIPE
SIZES = {"z": NZ, "y": NY, "x": NX, "c": NC}
VMEM = pl.BlockSpec(memory_space=pltpu.VMEM)
PARAMS = pltpu.CompilerParams(vmem_limit_bytes=48 * 1024 * 1024)


def signs(order):
    i = np.arange(order)
    parity = np.zeros((order, order), np.int64)
    for level in range(order.bit_length()):
        parity += ((i[:, None] & i[None, :]) >> level) & 1
    return (1 - 2 * (parity % 2)).astype(np.float32)


def moved(block, axis, step):
    count = SIZES[axis]
    return lax.ppermute(block, axis, [(i, (i + step) % count) for i in range(count)])


def inner_kernel(place, gate, up, had, out):
    g = gate[...].astype(jnp.float32)
    hidden = (g / (1.0 + jnp.exp(-g)) * up[...].astype(jnp.float32)).astype(jnp.bfloat16)
    for c in range(GROUPS):
        cols = slice(c * INNER, (c + 1) * INNER)
        out[:, cols] = jnp.dot(hidden[:, cols], had[...], preferred_element_type=jnp.float32)


def inner_transform(gate_pre, up_pre, place):
    had = jnp.asarray(signs(INNER) / 64.0, jnp.bfloat16)
    return pl.pallas_call(
        inner_kernel,
        grid_spec=pltpu.PrefetchScalarGridSpec(
            num_scalar_prefetch=1,
            grid=(1,),
            in_specs=[
                pl.BlockSpec((SLAB, WIDTH), lambda i, place: (place[0], 0)),
                pl.BlockSpec((SLAB, WIDTH), lambda i, place: (place[0], 0)),
                pl.BlockSpec((INNER, INNER), lambda i, place: (0, 0)),
            ],
            out_specs=pl.BlockSpec((SLAB, WIDTH), lambda i, place: (0, 0)),
        ),
        out_shape=jax.ShapeDtypeStruct((SLAB, WIDTH), jnp.float32),
        compiler_params=PARAMS,
        name="inner_transform",
    )(place, gate_pre, up_pre, had)


def outer_kernel(block, had, out):
    out[...] = jnp.dot(
        had[...], block[...], preferred_element_type=jnp.float32, precision=lax.Precision.HIGHEST
    )


def outer_transform(block):
    had = jnp.asarray(signs(N_PIPE), jnp.float32)
    return pl.pallas_call(
        outer_kernel,
        in_specs=[VMEM, VMEM],
        out_specs=VMEM,
        out_shape=jax.ShapeDtypeStruct((N_PIPE, WIDTH), jnp.float32),
        compiler_params=PARAMS,
        name="outer_transform",
    )(block, had)


BN = 256


def product_kernel(place, *refs):
    slabs, (codes, scales), outs, (rows32, rows16, peak) = refs[:8], refs[8:10], refs[10:15], refs[15:]
    step = pl.program_id(0)

    @pl.when(step == 0)
    def _():
        my_z, my_y, my_x, my_c = place[0], place[1], place[2], place[3]
        top = jnp.zeros((8, WIDTH), jnp.float32)
        for j, slab in enumerate(slabs):
            dx, dc = j // NC, j % NC
            z = lax.rem(my_x + NX - dx, NX) * NC + lax.rem(my_c + dc, NC)
            z_step = lax.rem(z - my_z + NZ, NZ)
            for y in range(NY):
                y_step = lax.rem(y - my_y + NY, NY)
                piece = slab[y * OWN : (y + 1) * OWN, :]
                top = jnp.maximum(top, jnp.abs(piece))
                at = pl.multiple_of(y_step * (NZ * OWN) + z_step * OWN, OWN)
                rows32[pl.ds(at, OWN), :] = piece
        rows16[...] = rows32[...].astype(jnp.bfloat16)
        peak[...] = jnp.full((8, 128), jnp.max(top), jnp.float32)
        for out in outs:
            for k in range(out.shape[0] // 8):
                out[k * 8 : (k + 1) * 8, COLS:] = peak[...]

    s = scales[...]
    w = codes[...] * jnp.broadcast_to(s[:, None, :], (WIDTH // 16, 16, BN)).reshape(WIDTH, BN)
    total = jnp.dot(rows16[...], w, preferred_element_type=jnp.float32)
    cols = pl.ds(pl.multiple_of(step * BN, BN), BN)
    at = 0
    for out in outs:
        out[:, cols] = total[at : at + out.shape[0], :]
        at += out.shape[0]


def product(slabs, codes, scales, place):
    sizes = [64, 64, 32, 32, 64]
    full = lambda shape: pl.BlockSpec(shape, lambda i, place: (0, 0))
    return pl.pallas_call(
        product_kernel,
        grid_spec=pltpu.PrefetchScalarGridSpec(
            num_scalar_prefetch=1,
            grid=(COLS // BN,),
            in_specs=[full((SLAB, WIDTH))] * 8
            + [
                pl.BlockSpec((WIDTH, BN), lambda i, place: (0, i)),
                pl.BlockSpec((WIDTH // 16, BN), lambda i, place: (0, i)),
            ],
            out_specs=[full((n, WIDE)) for n in sizes],
            scratch_shapes=[
                pltpu.VMEM((ROWS, WIDTH), jnp.float32),
                pltpu.VMEM((ROWS, WIDTH), jnp.bfloat16),
                pltpu.VMEM((8, 128), jnp.float32),
            ],
        ),
        out_shape=[jax.ShapeDtypeStruct((n, WIDE), jnp.float32) for n in sizes],
        compiler_params=PARAMS,
        name="product",
    )(place, *slabs, codes, scales)


def relay_kernel(a, first, b, second, out_a, out_b):
    out_a[...] = a[...]
    out_b[...] = b[...]
    out_a[:32, :COLS] += first[:, :COLS]
    out_b[32:, :COLS] += second[:, :COLS]
    other = jnp.maximum(first[:, COLS:], second[:, COLS:])
    out_a[:32, COLS:] = jnp.maximum(a[:32, COLS:], other)
    out_b[:32, COLS:] = jnp.maximum(b[:32, COLS:], other)


def relay(a, first, b, second):
    shape = jax.ShapeDtypeStruct((64, WIDE), jnp.float32)
    return pl.pallas_call(
        relay_kernel,
        in_specs=[VMEM] * 4,
        out_specs=[VMEM] * 2,
        out_shape=[shape] * 2,
        compiler_params=PARAMS,
        name="relay",
    )(a, first, b, second)


def y_sum_kernel(a, b, c, *outs):
    top = jnp.maximum(jnp.maximum(a[:8, COLS:], b[:8, COLS:]), c[:8, COLS:])
    for k, out in enumerate(outs):
        r = slice(k * OWN, (k + 1) * OWN)
        out[:, :COLS] = a[r, :COLS] + b[r, :COLS] + c[r, :COLS]
        out[:, COLS:] = top


def y_sum(a, b, c):
    return pl.pallas_call(
        y_sum_kernel,
        in_specs=[VMEM] * 3,
        out_specs=[VMEM] * NZ,
        out_shape=[jax.ShapeDtypeStruct((OWN, WIDE), jnp.float32)] * NZ,
        compiler_params=PARAMS,
        name="y_sum",
    )(a, b, c)


def z_sum_kernel(*refs):
    parts, residual, scale, summed, rounded, squares, top = refs[:NZ], *refs[NZ:]
    total = parts[0][:, :COLS]
    peak = parts[0][:, COLS:]
    for part in parts[1:]:
        total += part[:, :COLS]
        peak = jnp.maximum(peak, part[:, COLS:])
    total = residual[...].astype(jnp.float32) + total * scale[0]
    summed[...] = total
    rounded[...] = total.astype(jnp.bfloat16)
    squares[...] = jnp.broadcast_to(jnp.sum(total * total, axis=1, keepdims=True), (OWN, 128))
    top[...] = peak


def z_sum(parts, residual, weight_scale):
    return pl.pallas_call(
        z_sum_kernel,
        in_specs=[VMEM] * (NZ + 1) + [pl.BlockSpec(memory_space=pltpu.SMEM)],
        out_specs=[VMEM] * 4,
        out_shape=[
            jax.ShapeDtypeStruct((OWN, COLS), jnp.float32),
            jax.ShapeDtypeStruct((OWN, COLS), jnp.bfloat16),
            jax.ShapeDtypeStruct((OWN, 128), jnp.float32),
            jax.ShapeDtypeStruct((OWN, 128), jnp.float32),
        ],
        compiler_params=PARAMS,
        name="z_sum",
    )(*parts, residual, weight_scale)


def norm_kernel(summed, a, b, c, d, gain, out):
    mean = (a[...] + b[...] + c[...] + d[...]) * (1.0 / (COLS * N_TENSOR))
    factor = lax.rsqrt(mean + 1e-05)[:, :1]
    out[...] = (summed[...] * factor * gain[...].astype(jnp.float32)).astype(jnp.bfloat16)


def norm(summed, squares, gain):
    return pl.pallas_call(
        norm_kernel,
        in_specs=[VMEM] * 6,
        out_specs=VMEM,
        out_shape=jax.ShapeDtypeStruct((OWN, COLS), jnp.bfloat16),
        compiler_params=PARAMS,
        name="norm",
    )(summed, *squares, gain)


def blocks_kernel(place, *refs):
    slabs, pick, rows, wide, narrow = refs[:8], *refs[8:]
    my_x, my_c = place[2], place[3]
    lane = lax.broadcasted_iota(jnp.int32, (SLAB, WIDTH), 1)
    for j, slab in enumerate(slabs):
        dx, dc = j // NC, j % NC
        t = lax.rem(my_x + NX - dx, NX) * NC + lax.rem(my_c + dc, NC)
        at = pl.ds(pl.multiple_of(t * SLAB, SLAB), SLAB)
        value = slab[...]
        rows[at, :] = value
        big = jnp.abs(value)
        for shift in (1, 2, 4, 8):
            up = pltpu.roll(big, WIDTH - shift, 1)
            down = pltpu.roll(big, shift, 1)
            big = jnp.maximum(big, jnp.where((lane & shift) == 0, up, down))
        wide[at, :] = big
    narrow[...] = jnp.dot(
        wide[...], pick[...], preferred_element_type=jnp.float32, precision=lax.Precision.HIGHEST
    )


def blocks(slabs, place):
    pick = np.zeros((WIDTH, WIDTH // 16), np.float32)
    pick[np.arange(WIDTH // 16) * 16, np.arange(WIDTH // 16)] = 1.0
    return pl.pallas_call(
        blocks_kernel,
        in_specs=[pl.BlockSpec(memory_space=pltpu.SMEM)] + [VMEM] * 9,
        out_specs=[VMEM] * 3,
        out_shape=[
            jax.ShapeDtypeStruct((ROWS, WIDTH), jnp.float32),
            jax.ShapeDtypeStruct((ROWS, WIDTH), jnp.float32),
            jax.ShapeDtypeStruct((ROWS, WIDTH // 16), jnp.float32),
        ],
        compiler_params=PARAMS,
        name="blocks",
    )(place, *slabs, jnp.asarray(pick))


def payload_kernel(rows, wide, narrow, peak, payload, block_scales):
    top = peak[0, 0]
    low = top / 64.0
    payload[...] = (6.0 * rows[...] / jnp.maximum(wide[...], low)).astype(jnp.bfloat16)
    block_scales[...] = 448.0 * jnp.maximum(narrow[...], low) / top


def encode(rows, wide, narrow, peak):
    return pl.pallas_call(
        payload_kernel,
        in_specs=[VMEM] * 4,
        out_specs=[VMEM] * 2,
        out_shape=[
            jax.ShapeDtypeStruct((ROWS, WIDTH), jnp.bfloat16),
            jax.ShapeDtypeStruct((ROWS, WIDTH // 16), jnp.float32),
        ],
        compiler_params=PARAMS,
        name="encode",
    )(rows, wide, narrow, peak)


def on_device(gate_pre, up_pre, down_codes, down_scales, weight_scale, residual, norm_gain):
    place = jnp.stack([lax.axis_index(a) for a in ("z", "y", "x", "c")]).astype(jnp.int32)
    tensor = (place[2] * NC + place[3]).reshape(1)
    inner = inner_transform(gate_pre, up_pre, tensor)
    one_row = lax.all_to_all(inner, ("z", "y"), 0, 0, tiled=True)
    turned = outer_transform(one_row)
    own = lax.all_to_all(turned, ("z", "y"), 0, 0, tiled=True)

    mine = [own, moved(own, "x", 1), moved(own, "x", 2), moved(own, "x", 3)]
    slabs = []
    for block in mine:
        slabs += [block, moved(block, "c", 1)]

    here, ahead, far_a, far_b, behind = product(slabs, down_codes, down_scales, place)
    first, second = moved(far_a, "y", 1), moved(far_b, "y", -1)
    ahead, behind = relay(ahead, first, behind, second)
    parts = y_sum(here, moved(ahead, "y", 1), moved(behind, "y", -1))
    parts = [parts[0]] + [moved(parts[d], "z", d) for d in (4, 3, 5, 2, 6, 1, 7)]
    summed, rounded, squares, peak = z_sum(parts, residual, weight_scale)
    squares = squares + moved(squares, "c", 1)
    normed = norm(
        summed,
        [squares, moved(squares, "x", 1), moved(squares, "x", 2), moved(squares, "x", 3)],
        norm_gain.reshape(1, COLS),
    )
    payload, block_scales = encode(*blocks(slabs, place), peak)
    return payload, block_scales, rounded, normed


def solution(mesh):
    mesh = Mesh(mesh.devices.reshape(NZ, NY, NX, NC), ("z", "y", "x", "c"))
    pipe, tensor = ("z", "y"), ("x", "c")
    in_specs = (
        P(None, pipe),
        P(None, pipe),
        P(pipe, tensor),
        P(pipe, tensor),
        P(),
        P(pipe, tensor),
        P(tensor),
    )
    out_specs = (P(None, pipe), P(None, pipe), P(pipe, tensor), P(pipe, tensor))
    return jax.shard_map(
        on_device, mesh=mesh, in_specs=in_specs, out_specs=out_specs, check_vma=False
    )
```

time: 549 us -> 123 us (0.22)
  waiting for transfers between devices: 403 us -> 26.7 us
  blocking collectives: 78.8 us -> 36.6 us
  other arithmetic: 22.4 us -> 0.08 us
  Pallas kernels: 0 us -> 18.2 us
  starting transfers between devices: 17.7 us -> 34.6 us
  between operations: 15.4 us -> 1.44 us
  matrix products: 6.84 us -> 0 us
    ppermute x5 -> x22, waiting for transfers between devices: 243 us -> 26.7 us  [moved(): lax.ppermute(block, axis, [(i, (i + step) % count) for i in range(count)])]
    psum x1 -> x0, waiting for transfers between devices: 160 us -> none  [on_device(): lax.psum(jnp.dot(dequant, weight, preferred_element_type=jnp.float32), 'p...]
    pmax x1 -> x0, blocking collectives: 61.9 us -> none  [on_device(): peak_value = lax.pmax(jnp.max(jnp.abs(rotated)), 'pipe')]
    all_to_all x0 -> x2, blocking collectives: none -> 36.6 us  [the longest x1 21.9 us: on_device(): one_row = lax.all_to_all(inner, ('z', 'y'), 0, 0, tiled=True)]
    pallas_call x0 -> x9, Pallas kernels: none -> 18.2 us  [the longest x1 8.06 us: product(): pl.pallas_call(product_kernel, grid_spec=pltpu.PrefetchScalarGridSpec(num...]
    psum x1 -> x0, blocking collectives: 16.9 us -> none  [on_device(): lax.psum(jnp.sum(summed * summed, axis=1), 'tensor')]
    ppermute x5 -> x22, starting transfers between devices: 17.7 us -> 34.6 us  [moved(): lax.ppermute(block, axis, [(i, (i + step) % count) for i in range(count)])]
    convert_element_type x6 -> x0, other arithmetic: 11.9 us -> none  [the longest x1 8.34 us: on_device(): weight = (down_codes.reshape(code_rows // 16, 16, model_cols).astype(jnp....]
  transfers between devices with their start and end apart: 6 -> 22, of which waited for: 6 -> 10; matrix products, arithmetic and copies ran while one was open for 2% -> 1% of each run, Pallas kernels for 0% -> 7%
where the time goes in v1:
time: 123 us; the launch traced here: 122 us
  blocking collectives  36.6 us (30%)
  starting transfers between devices  34.6 us (28%)
  waiting for transfers between devices  26.7 us (22%)
  Pallas kernels  18.2 us (15%)
  local copies, waits for them, and re-layouts  4.31 us (4%)
  between operations  1.44 us (1%)
    ppermute x22, starting transfers between devices, moved(): lax.ppermute(block, axis, [(i, (i + step) % count) for i in range(count)])  34.6 us
    ppermute x22, waiting for transfers between devices, moved(): lax.ppermute(block, axis, [(i, (i + step) % count) for i in range(count)])  26.7 us
    all_to_all x1, blocking collectives, on_device(): one_row = lax.all_to_all(inner, ('z', 'y'), 0, 0, tiled=True)  21.9 us
    all_to_all x1, blocking collectives, on_device(): own = lax.all_to_all(turned, ('z', 'y'), 0, 0, tiled=True)  14.6 us
    pallas_call x1, Pallas kernels, product(): pl.pallas_call(product_kernel, grid_spec=pltpu.PrefetchScalarGridSpec(num...  8.06 us
    pallas_call x1, Pallas kernels, blocks(): pl.pallas_call(blocks_kernel, in_specs=[pl.BlockSpec(memory_space=pltpu.S...  6.63 us
    unnamed x19, local copies, waits for them, and re-layouts  3.85 us
  transfers between devices with their start and end apart: 22, of which 10 were waited for; matrix products, arithmetic and copies ran while one was open for 1% of the time, Pallas kernels for 7%

profile of v1, /device:TPU:1, one launch (start us, length us, event | category | flops | bytes accessed | tf_op | source)
XLA Modules:
  0.0 121.9 jit_solution(10180551479732396526)
XLA Ops:
  0.6 0.0 copy-start.6
  0.7 1.1 copy-done
  1.8 1.2 copy-done.1
  3.0 0.8 copy-done.4
  3.7 0.2 inner_transform.1
  4.0 0.2 copy.15
  4.2 21.9 %all_to_all.22 = f32[32,1,1664]{2,1,0:T(1,128)S(1)} all-to-all(f32[32,1,1664]{2,1,0:T(1,128)S(1)} %copy.15), channel_id=1, replica_groups=mesh['z'=8,'y'=4,'x'=4,'c'=2] {'z','y'}, dimensions={0} | all-to-all | bytes 425984 | tf_op jit(solution)/shard_map/all_to_all | solution.py:298
  26.2 0.3 outer_transform.1
  26.5 0.2 copy.16
  26.7 14.6 %all_to_all.23 = f32[32,1,1664]{2,1,0:T(1,128)S(1)} all-to-all(f32[32,1,1664]{2,1,0:T(1,128)S(1)} %copy.16), channel_id=1, replica_groups=mesh['z'=8,'y'=4,'x'=4,'c'=2] {'z','y'}, dimensions={0} | all-to-all | bytes 425984 | tf_op jit(solution)/shard_map/all_to_all | solution.py:300
  41.4 2.6 %collective-permute-start.5 = (f32[32,1664]{1,0:T(8,128)S(1)}, f32[32,1664]{1,0:T(8,128)S(1)}, u32[]{:S(2)}, u32[]{:S(2)}) collective-permute-start(f32[32,1664]{1,0:T(8,128)S(1)} %bitcast.13), channel_id=1, source_target_pairs={{0,6},{2,0},{4,2},{6,4},{1,7},{3,1},{5,3},{7,5},{8,14},{10,8},{12,... | collective-permute-start | bytes 638984 | tf_op jit(solution)/shard_map/ppermute | solution.py:35
  43.9 0.5 collective-permute-start.3
  44.5 0.6 collective-permute-start.1
  45.1 4.0 %collective-permute-start = (f32[32,1664]{1,0:T(8,128)S(1)}, f32[32,1664]{1,0:T(8,128)S(1)}, u32[]{:S(2)}, u32[]{:S(2)}) collective-permute-start(f32[32,1664]{1,0:T(8,128)S(1)} %bitcast.16), channel_id=1, source_target_pairs={{0,1},{1,0},{2,3},{3,2},{4,5},{5,4},{6,7},{7,6},{8,9},{9,8},{10,11... | collective-permute-start | bytes 638984 | tf_op jit(solution)/shard_map/ppermute | solution.py:35
  49.0 0.4 collective-permute-done.5.refs_6_
  49.4 4.6 %collective-permute-start.6 = (f32[32,1664]{1,0:T(8,128)S(1)}, f32[32,1664]{1,0:T(8,128)S(1)}, u32[]{:S(2)}, u32[]{:S(2)}) collective-permute-start(f32[32,1664]{1,0:T(8,128)S(1)} %collective-permute-done.5.refs_6_), channel_id=1, source_target_pairs={{0,1},{1,0},{2,3},{3,2},{4,5},{5,4},{6,7},{7,6},{8,9},{9,8},{10,11... | collective-permute-start | bytes 638984 | tf_op jit(solution)/shard_map/ppermute | solution.py:35
  54.0 0.0 collective-permute-done.3.refs_4_
  54.0 1.5 %collective-permute-start.4 = (f32[32,1664]{1,0:T(8,128)S(1)}, f32[32,1664]{1,0:T(8,128)S(1)}, u32[]{:S(2)}, u32[]{:S(2)}) collective-permute-start(f32[32,1664]{1,0:T(8,128)S(1)} %collective-permute-done.3.refs_4_), channel_id=1, source_target_pairs={{0,1},{1,0},{2,3},{3,2},{4,5},{5,4},{6,7},{7,6},{8,9},{9,8},{10,11... | collective-permute-start | bytes 638984 | tf_op jit(solution)/shard_map/ppermute | solution.py:35
  55.5 0.0 collective-permute-done.1.refs_2_
  55.5 2.1 %collective-permute-start.2 = (f32[32,1664]{1,0:T(8,128)S(1)}, f32[32,1664]{1,0:T(8,128)S(1)}, u32[]{:S(2)}, u32[]{:S(2)}) collective-permute-start(f32[32,1664]{1,0:T(8,128)S(1)} %collective-permute-done.1.refs_2_), channel_id=1, source_target_pairs={{0,1},{1,0},{2,3},{3,2},{4,5},{5,4},{6,7},{7,6},{8,9},{9,8},{10,11... | collective-permute-start | bytes 638984 | tf_op jit(solution)/shard_map/ppermute | solution.py:35
  57.7 0.1 pad_add_fusion.place
  57.8 0.0 collective-permute-done.refs_1_
  57.8 0.0 collective-permute-done.6.refs_7_
  57.8 0.0 collective-permute-done.4.refs_5_
  57.8 1.0 collective-permute-done.2.refs_3_
  58.8 8.1 %product.1 = (f32[64,2176]{1,0:T(8,128)S(1)}, f32[64,2176]{1,0:T(8,128)S(1)}, f32[32,2176]{1,0:T(8,128)S(1)}, f32[32,2176]{1,0:T(8,128)S(1)}, f32[64,2176]{1,0:T(8,128)S(1)}) custom-call(s32[4]{0:T(128)S(1)} %pad_add_fusion.place, f32[32,1664]{1,0:T(8,128)S(1)} %bitcast.17, f32[32,1664]{1,0:T(8,128)S(1)} %collective-permute-done.refs_1_, ...), custom_call_target="tpu_custom_call" | custom-call | tf_op jit(solution)/shard_map/product/pallas_call | solution.py:124
  66.8 0.0 copy-start.5
  66.8 0.1 collective-permute-start.7
  66.9 2.7 %collective-permute-start.8 = (f32[32,2176]{1,0:T(8,128)S(1)}, f32[32,2176]{1,0:T(8,128)S(1)}, u32[]{:S(2)}, u32[]{:S(2)}) collective-permute-start(f32[32,2176]{1,0:T(8,128)S(1)} %get-tuple-element.35), channel_id=1, source_target_pairs={{0,24},{8,0},{16,8},{24,16},{1,25},{9,1},{17,9},{25,17},{2,26},{10... | collective-permute-start | bytes 835592 | tf_op jit(solution)/shard_map/ppermute | solution.py:35
  69.6 6.4 %collective-permute-done.7.first = f32[32,2176]{1,0:T(8,128)S(1)} collective-permute-done((f32[32,2176]{1,0:T(8,128)S(1)}, f32[32,2176]{1,0:T(8,128)S(1)}, u32[]{:S(2)}, u32[]{:S(2)}) %collective-permute-start.7) | collective-permute-done | bytes 278560 | tf_op jit(solution)/shard_map/ppermute | solution.py:35
  76.0 0.0 collective-permute-done.8.second
  76.0 0.1 relay.1
  76.1 0.1 collective-permute-start.9
  76.2 2.7 %collective-permute-start.10 = (f32[64,2176]{1,0:T(8,128)S(1)}, f32[64,2176]{1,0:T(8,128)S(1)}, u32[]{:S(2)}, u32[]{:S(2)}) collective-permute-start(f32[64,2176]{1,0:T(8,128)S(1)} %get-tuple-element.37), channel_id=1, source_target_pairs={{0,24},{8,0},{16,8},{24,16},{1,25},{9,1},{17,9},{25,17},{2,26},{10... | collective-permute-start | bytes 1671176 | tf_op jit(solution)/shard_map/ppermute | solution.py:35
  78.9 11.5 %collective-permute-done.9.b = f32[64,2176]{1,0:T(8,128)S(1)} collective-permute-done((f32[64,2176]{1,0:T(8,128)S(1)}, f32[64,2176]{1,0:T(8,128)S(1)}, u32[]{:S(2)}, u32[]{:S(2)}) %collective-permute-start.9) | collective-permute-done | bytes 557088 | tf_op jit(solution)/shard_map/ppermute | solution.py:35
  90.3 0.0 collective-permute-done.10.c
  90.3 0.1 y_sum.1
  90.4 1.2 collective-permute-start.11
  91.6 2.4 %collective-permute-start.12 = (f32[8,2176]{1,0:T(8,128)S(1)}, f32[8,2176]{1,0:T(8,128)S(1)}, u32[]{:S(2)}, u32[]{:S(2)}) collective-permute-start(f32[8,2176]{1,0:T(8,128)S(1)} %get-tuple-element.40), channel_id=1, source_target_pairs={{0,96},{32,128},{64,160},{96,192},{128,224},{160,0},{192,32},{224,... | collective-permute-start | bytes 208904 | tf_op jit(solution)/shard_map/ppermute | solution.py:35
  94.0 2.1 %collective-permute-start.13 = (f32[8,2176]{1,0:T(8,128)S(1)}, f32[8,2176]{1,0:T(8,128)S(1)}, u32[]{:S(2)}, u32[]{:S(2)}) collective-permute-start(f32[8,2176]{1,0:T(8,128)S(1)} %get-tuple-element.41), channel_id=1, source_target_pairs={{0,160},{32,192},{64,224},{96,0},{128,32},{160,64},{192,96},{224,1... | collective-permute-start | bytes 208904 | tf_op jit(solution)/shard_map/ppermute | solution.py:35
  96.1 1.6 %collective-permute-start.14 = (f32[8,2176]{1,0:T(8,128)S(1)}, f32[8,2176]{1,0:T(8,128)S(1)}, u32[]{:S(2)}, u32[]{:S(2)}) collective-permute-start(f32[8,2176]{1,0:T(8,128)S(1)} %get-tuple-element.42), channel_id=1, source_target_pairs={{0,64},{32,96},{64,128},{96,160},{128,192},{160,224},{192,0},{224,... | collective-permute-start | bytes 208904 | tf_op jit(solution)/shard_map/ppermute | solution.py:35
  97.7 2.0 %collective-permute-start.15 = (f32[8,2176]{1,0:T(8,128)S(1)}, f32[8,2176]{1,0:T(8,128)S(1)}, u32[]{:S(2)}, u32[]{:S(2)}) collective-permute-start(f32[8,2176]{1,0:T(8,128)S(1)} %get-tuple-element.43), channel_id=1, source_target_pairs={{0,192},{32,224},{64,0},{96,32},{128,64},{160,96},{192,128},{224,1... | collective-permute-start | bytes 208904 | tf_op jit(solution)/shard_map/ppermute | solution.py:35
  99.7 0.0 collective-permute-done.11.refs_1_
  99.7 0.8 collective-permute-start.16
  100.5 3.3 %collective-permute-done.12.refs_2_ = f32[8,2176]{1,0:T(8,128)S(1)} collective-permute-done((f32[8,2176]{1,0:T(8,128)S(1)}, f32[8,2176]{1,0:T(8,128)S(1)}, u32[]{:S(2)}, u32[]{:S(2)}) %collective-permute-start.12) | collective-permute-done | bytes 69664 | tf_op jit(solution)/shard_map/ppermute | solution.py:35
  103.8 0.0 collective-permute-start.17
  104.4 0.0 collective-permute-done.13.refs_3_
  104.5 0.6 collective-permute-done.14.refs_4_
  105.1 0.7 collective-permute-done.15.refs_5_
  105.8 1.5 %collective-permute-done.16.refs_6_ = f32[8,2176]{1,0:T(8,128)S(1)} collective-permute-done((f32[8,2176]{1,0:T(8,128)S(1)}, f32[8,2176]{1,0:T(8,128)S(1)}, u32[]{:S(2)}, u32[]{:S(2)}) %collective-permute-start.16) | collective-permute-done | bytes 69664 | tf_op jit(solution)/shard_map/ppermute | solution.py:35
  107.3 0.4 collective-permute-done.17.refs_7_
  107.8 0.7 z_sum.1
  108.4 1.7 %collective-permute-start.18 = (f32[8,128]{1,0:T(8,128)S(1)}, f32[8,128]{1,0:T(8,128)S(1)}, u32[]{:S(2)}, u32[]{:S(2)}) collective-permute-start(f32[8,128]{1,0:T(8,128)S(1)} %get-tuple-element.51), channel_id=1, source_target_pairs={{0,1},{1,0},{2,3},{3,2},{4,5},{5,4},{6,7},{7,6},{8,9},{9,8},{10,11... | collective-permute-start | bytes 12296 | tf_op jit(solution)/shard_map/ppermute | solution.py:35
  110.1 0.8 collective-permute-done.18
  110.9 0.4 collective-permute-start.21
  111.3 0.4 collective-permute-start.20
  111.7 0.6 collective-permute-start.19
  112.4 6.6 %blocks.1 = (f32[256,1664]{1,0:T(8,128)S(1)}, f32[256,1664]{1,0:T(8,128)S(1)}, f32[256,104]{1,0:T(8,128)S(1)}) custom-call(s32[4]{0:T(128)S(1)} %pad_add_fusion.place, f32[32,1664]{1,0:T(8,128)S(1)} %bitcast.18, f32[32,1664]{1,0:T(8,128)S(1)} %collective-permute-done.refs_1_, f32[32,1664]{1,0:T(8,128)S(1)} %collective-permute-done.1.refs_2_, ...), custom_call_target="tpu_custom_call" | custom-call | tf_op jit(solution)/shard_map/blocks/pallas_call | solution.py:259
  119.0 1.4 %encode.1 = (bf16[256,1664]{1,0:T(8,128)(2,1)}, f32[256,104]{1,0:T(8,128)S(1)}) custom-call(f32[256,1664]{1,0:T(8,128)S(1)} %get-tuple-element.28.rows, f32[256,1664]{1,0:T(8,128)S(1)} %get-tuple-element.29.wide, f32[256,104]{1,0:T(8,128)S(1)} %get-tuple-element.30.narrow, f32[8,128]{1,0:T(8,128)S(1)} %get-tuple-element.46.peak), custom_call_target="tpu_custom_call" | custom-call | tf_op jit(solution)/shard_map/encode/pallas_call | solution.py:281
  120.4 0.7 copy.17
  121.2 0.0 collective-permute-done.21.d
  121.2 0.0 collective-permute-done.20.c
  121.2 0.0 collective-permute-done.19.b
  121.2 0.7 norm.1
  (15 shorter events, 0.1 us)
Async XLA Ops:
  0.6 25.5 %copy-start.6 = (f32[32,32]{1,0:T(8,128)S(1)}, f32[32,32]{1,0:T(8,128)}, u32[]{:S(2)}) copy-start(f32[32,32]{1,0:T(8,128)} %constant.25.clone.had) | copy-start | bytes 12292
  0.7 1.2 copy-start
  1.8 1.2 copy-start.1
  3.0 0.8 copy-start.4
  4.0 54.8 %copy-start.3 = (bf16[104,2048]{1,0:T(8,128)(2,1)S(1)}, bf16[104,2048]{1,0:T(8,128)(2,1)}, u32[]{:S(2)}) copy-start(bf16[104,2048]{1,0:T(8,128)(2,1)} %refs_9_.2) | copy-start | bytes 1277956
  41.4 8.1 %collective-permute-start.5 = (f32[32,1664]{1,0:T(8,128)S(1)}, f32[32,1664]{1,0:T(8,128)S(1)}, u32[]{:S(2)}, u32[]{:S(2)}) collective-permute-start(f32[32,1664]{1,0:T(8,128)S(1)} %bitcast.13), channel_id=1, source_target_pairs={{0,6},{2,0},{4,2},{6,4},{1,7},{3,1},{5,3},{7,5},{8,14},{10,8},{12,... | collective-permute-start | bytes 638984 | tf_op jit(solution)/shard_map/ppermute | solution.py:35
  43.9 10.1 %collective-permute-start.3 = (f32[32,1664]{1,0:T(8,128)S(1)}, f32[32,1664]{1,0:T(8,128)S(1)}, u32[]{:S(2)}, u32[]{:S(2)}) collective-permute-start(f32[32,1664]{1,0:T(8,128)S(1)} %bitcast.14), channel_id=1, source_target_pairs={{0,4},{2,6},{4,0},{6,2},{1,5},{3,7},{5,1},{7,3},{8,12},{10,14},{12... | collective-permute-start | bytes 638984 | tf_op jit(solution)/shard_map/ppermute | solution.py:35
  44.5 11.1 %collective-permute-start.1 = (f32[32,1664]{1,0:T(8,128)S(1)}, f32[32,1664]{1,0:T(8,128)S(1)}, u32[]{:S(2)}, u32[]{:S(2)}) collective-permute-start(f32[32,1664]{1,0:T(8,128)S(1)} %bitcast.15), channel_id=1, source_target_pairs={{0,2},{2,4},{4,6},{6,0},{1,3},{3,5},{5,7},{7,1},{8,10},{10,12},{12... | collective-permute-start | bytes 638984 | tf_op jit(solution)/shard_map/ppermute | solution.py:35
  45.1 12.7 %collective-permute-start = (f32[32,1664]{1,0:T(8,128)S(1)}, f32[32,1664]{1,0:T(8,128)S(1)}, u32[]{:S(2)}, u32[]{:S(2)}) collective-permute-start(f32[32,1664]{1,0:T(8,128)S(1)} %bitcast.16), channel_id=1, source_target_pairs={{0,1},{1,0},{2,3},{3,2},{4,5},{5,4},{6,7},{7,6},{8,9},{9,8},{10,11... | collective-permute-start | bytes 638984 | tf_op jit(solution)/shard_map/ppermute | solution.py:35
  49.4 8.3 %collective-permute-start.6 = (f32[32,1664]{1,0:T(8,128)S(1)}, f32[32,1664]{1,0:T(8,128)S(1)}, u32[]{:S(2)}, u32[]{:S(2)}) collective-permute-start(f32[32,1664]{1,0:T(8,128)S(1)} %collective-permute-done.5.refs_6_), channel_id=1, source_target_pairs={{0,1},{1,0},{2,3},{3,2},{4,5},{5,4},{6,7},{7,6},{8,9},{9,8},{10,11... | collective-permute-start | bytes 638984 | tf_op jit(solution)/shard_map/ppermute | solution.py:35
  54.0 3.8 %collective-permute-start.4 = (f32[32,1664]{1,0:T(8,128)S(1)}, f32[32,1664]{1,0:T(8,128)S(1)}, u32[]{:S(2)}, u32[]{:S(2)}) collective-permute-start(f32[32,1664]{1,0:T(8,128)S(1)} %collective-permute-done.3.refs_4_), channel_id=1, source_target_pairs={{0,1},{1,0},{2,3},{3,2},{4,5},{5,4},{6,7},{7,6},{8,9},{9,8},{10,11... | collective-permute-start | bytes 638984 | tf_op jit(solution)/shard_map/ppermute | solution.py:35
  55.5 3.2 %collective-permute-start.2 = (f32[32,1664]{1,0:T(8,128)S(1)}, f32[32,1664]{1,0:T(8,128)S(1)}, u32[]{:S(2)}, u32[]{:S(2)}) collective-permute-start(f32[32,1664]{1,0:T(8,128)S(1)} %collective-permute-done.1.refs_2_), channel_id=1, source_target_pairs={{0,1},{1,0},{2,3},{3,2},{4,5},{5,4},{6,7},{7,6},{8,9},{9,8},{10,11... | collective-permute-start | bytes 638984 | tf_op jit(solution)/shard_map/ppermute | solution.py:35
  66.8 40.9 %copy-start.5 = (bf16[8,2048]{1,0:T(8,128)(2,1)S(1)}, bf16[8,2048]{1,0:T(8,128)(2,1)}, u32[]{:S(2)}) copy-start(bf16[8,2048]{1,0:T(8,128)(2,1)} %refs_8_.4) | copy-start | bytes 98308
  66.8 9.2 %collective-permute-start.7 = (f32[32,2176]{1,0:T(8,128)S(1)}, f32[32,2176]{1,0:T(8,128)S(1)}, u32[]{:S(2)}, u32[]{:S(2)}) collective-permute-start(f32[32,2176]{1,0:T(8,128)S(1)} %get-tuple-element.33), channel_id=1, source_target_pairs={{0,8},{8,16},{16,24},{24,0},{1,9},{9,17},{17,25},{25,1},{2,10},{10... | collective-permute-start | bytes 835592 | tf_op jit(solution)/shard_map/ppermute | solution.py:35
  66.9 9.1 %collective-permute-start.8 = (f32[32,2176]{1,0:T(8,128)S(1)}, f32[32,2176]{1,0:T(8,128)S(1)}, u32[]{:S(2)}, u32[]{:S(2)}) collective-permute-start(f32[32,2176]{1,0:T(8,128)S(1)} %get-tuple-element.35), channel_id=1, source_target_pairs={{0,24},{8,0},{16,8},{24,16},{1,25},{9,1},{17,9},{25,17},{2,26},{10... | collective-permute-start | bytes 835592 | tf_op jit(solution)/shard_map/ppermute | solution.py:35
  76.0 36.4 %copy-start.7 = (bf16[2048]{0:T(1024)(128)(2,1)S(1)}, bf16[2048]{0:T(1024)(128)(2,1)}, u32[]{:S(2)}) copy-start(bf16[2048]{0:T(1024)(128)(2,1)} %param.16) | copy-start | bytes 12292
  76.0 36.4 %copy-start.2 = (f32[1664,104]{1,0:T(8,128)S(1)}, f32[1664,104]{1,0:T(8,128)}, u32[]{:S(2)}) copy-start(f32[1664,104]{1,0:T(8,128)} %constant.26.clone.refs_8_) | copy-start | bytes 2076676
  76.1 14.2 %collective-permute-start.9 = (f32[64,2176]{1,0:T(8,128)S(1)}, f32[64,2176]{1,0:T(8,128)S(1)}, u32[]{:S(2)}, u32[]{:S(2)}) collective-permute-start(f32[64,2176]{1,0:T(8,128)S(1)} %get-tuple-element.36), channel_id=1, source_target_pairs={{0,8},{8,16},{16,24},{24,0},{1,9},{9,17},{17,25},{25,1},{2,10},{10... | collective-permute-start | bytes 1671176 | tf_op jit(solution)/shard_map/ppermute | solution.py:35
  76.2 14.1 %collective-permute-start.10 = (f32[64,2176]{1,0:T(8,128)S(1)}, f32[64,2176]{1,0:T(8,128)S(1)}, u32[]{:S(2)}, u32[]{:S(2)}) collective-permute-start(f32[64,2176]{1,0:T(8,128)S(1)} %get-tuple-element.37), channel_id=1, source_target_pairs={{0,24},{8,0},{16,8},{24,16},{1,25},{9,1},{17,9},{25,17},{2,26},{10... | collective-permute-start | bytes 1671176 | tf_op jit(solution)/shard_map/ppermute | solution.py:35
  90.4 9.3 %collective-permute-start.11 = (f32[8,2176]{1,0:T(8,128)S(1)}, f32[8,2176]{1,0:T(8,128)S(1)}, u32[]{:S(2)}, u32[]{:S(2)}) collective-permute-start(f32[8,2176]{1,0:T(8,128)S(1)} %get-tuple-element.39), channel_id=1, source_target_pairs={{0,128},{32,160},{64,192},{96,224},{128,0},{160,32},{192,64},{224,... | collective-permute-start | bytes 208904 | tf_op jit(solution)/shard_map/ppermute | solution.py:35
  91.6 12.2 %collective-permute-start.12 = (f32[8,2176]{1,0:T(8,128)S(1)}, f32[8,2176]{1,0:T(8,128)S(1)}, u32[]{:S(2)}, u32[]{:S(2)}) collective-permute-start(f32[8,2176]{1,0:T(8,128)S(1)} %get-tuple-element.40), channel_id=1, source_target_pairs={{0,96},{32,128},{64,160},{96,192},{128,224},{160,0},{192,32},{224,... | collective-permute-start | bytes 208904 | tf_op jit(solution)/shard_map/ppermute | solution.py:35
  94.0 10.5 %collective-permute-start.13 = (f32[8,2176]{1,0:T(8,128)S(1)}, f32[8,2176]{1,0:T(8,128)S(1)}, u32[]{:S(2)}, u32[]{:S(2)}) collective-permute-start(f32[8,2176]{1,0:T(8,128)S(1)} %get-tuple-element.41), channel_id=1, source_target_pairs={{0,160},{32,192},{64,224},{96,0},{128,32},{160,64},{192,96},{224,1... | collective-permute-start | bytes 208904 | tf_op jit(solution)/shard_map/ppermute | solution.py:35
  96.1 9.0 %collective-permute-start.14 = (f32[8,2176]{1,0:T(8,128)S(1)}, f32[8,2176]{1,0:T(8,128)S(1)}, u32[]{:S(2)}, u32[]{:S(2)}) collective-permute-start(f32[8,2176]{1,0:T(8,128)S(1)} %get-tuple-element.42), channel_id=1, source_target_pairs={{0,64},{32,96},{64,128},{96,160},{128,192},{160,224},{192,0},{224,... | collective-permute-start | bytes 208904 | tf_op jit(solution)/shard_map/ppermute | solution.py:35
  97.7 8.1 %collective-permute-start.15 = (f32[8,2176]{1,0:T(8,128)S(1)}, f32[8,2176]{1,0:T(8,128)S(1)}, u32[]{:S(2)}, u32[]{:S(2)}) collective-permute-start(f32[8,2176]{1,0:T(8,128)S(1)} %get-tuple-element.43), channel_id=1, source_target_pairs={{0,192},{32,224},{64,0},{96,32},{128,64},{160,96},{192,128},{224,1... | collective-permute-start | bytes 208904 | tf_op jit(solution)/shard_map/ppermute | solution.py:35
  99.7 7.6 %collective-permute-start.16 = (f32[8,2176]{1,0:T(8,128)S(1)}, f32[8,2176]{1,0:T(8,128)S(1)}, u32[]{:S(2)}, u32[]{:S(2)}) collective-permute-start(f32[8,2176]{1,0:T(8,128)S(1)} %get-tuple-element.44), channel_id=1, source_target_pairs={{0,32},{32,64},{64,96},{96,128},{128,160},{160,192},{192,224},{224... | collective-permute-start | bytes 208904 | tf_op jit(solution)/shard_map/ppermute | solution.py:35
  103.8 4.0 %collective-permute-start.17 = (f32[8,2176]{1,0:T(8,128)S(1)}, f32[8,2176]{1,0:T(8,128)S(1)}, u32[]{:S(2)}, u32[]{:S(2)}) collective-permute-start(f32[8,2176]{1,0:T(8,128)S(1)} %get-tuple-element.45), channel_id=1, source_target_pairs={{0,224},{32,0},{64,32},{96,64},{128,96},{160,128},{192,160},{224,1... | collective-permute-start | bytes 208904 | tf_op jit(solution)/shard_map/ppermute | solution.py:35
  108.4 2.5 %collective-permute-start.18 = (f32[8,128]{1,0:T(8,128)S(1)}, f32[8,128]{1,0:T(8,128)S(1)}, u32[]{:S(2)}, u32[]{:S(2)}) collective-permute-start(f32[8,128]{1,0:T(8,128)S(1)} %get-tuple-element.51), channel_id=1, source_target_pairs={{0,1},{1,0},{2,3},{3,2},{4,5},{5,4},{6,7},{7,6},{8,9},{9,8},{10,11... | collective-permute-start | bytes 12296 | tf_op jit(solution)/shard_map/ppermute | solution.py:35
  110.9 10.3 %collective-permute-start.21 = (f32[8,128]{1,0:T(8,128)S(1)}, f32[8,128]{1,0:T(8,128)S(1)}, u32[]{:S(2)}, u32[]{:S(2)}) collective-permute-start(f32[8,128]{1,0:T(8,128)S(1)} %add.7.a), channel_id=1, source_target_pairs={{0,6},{2,0},{4,2},{6,4},{1,7},{3,1},{5,3},{7,5},{8,14},{10,8},{12,... | collective-permute-start | bytes 12296 | tf_op jit(solution)/shard_map/ppermute | solution.py:35
  111.3 9.8 %collective-permute-start.20 = (f32[8,128]{1,0:T(8,128)S(1)}, f32[8,128]{1,0:T(8,128)S(1)}, u32[]{:S(2)}, u32[]{:S(2)}) collective-permute-start(f32[8,128]{1,0:T(8,128)S(1)} %add.7.a), channel_id=1, source_target_pairs={{0,4},{2,6},{4,0},{6,2},{1,5},{3,7},{5,1},{7,3},{8,12},{10,14},{12... | collective-permute-start | bytes 12296 | tf_op jit(solution)/shard_map/ppermute | solution.py:35
  111.7 9.4 %collective-permute-start.19 = (f32[8,128]{1,0:T(8,128)S(1)}, f32[8,128]{1,0:T(8,128)S(1)}, u32[]{:S(2)}, u32[]{:S(2)}) collective-permute-start(f32[8,128]{1,0:T(8,128)S(1)} %add.7.a), channel_id=1, source_target_pairs={{0,2},{2,4},{4,6},{6,0},{1,3},{3,5},{5,7},{7,1},{8,10},{10,12},{12... | collective-permute-start | bytes 12296 | tf_op jit(solution)/shard_map/ppermute | solution.py:35

commit v2 on v1

v2 whole, which is shorter than its diff:
```python
import jax
import jax.numpy as jnp
from jax import lax
from jax.experimental import pallas as pl
from jax.experimental.pallas import tpu as pltpu
from jax.sharding import Mesh
from jax.sharding import PartitionSpec as P

NZ, NY, NX, NC = 8, 4, 4, 2
N_PIPE, N_TENSOR = NZ * NY, NX * NC
ROWS, GROUPS, INNER = 256, 13, 128
WIDTH = GROUPS * INNER
COLS = 2048
WIDE = COLS + 128
SLAB = ROWS // N_TENSOR
OWN = ROWS // N_PIPE
SIZES = {"z": NZ, "y": NY, "x": NX, "c": NC}
VMEM = pl.BlockSpec(memory_space=pltpu.VMEM)
SMEM = pl.BlockSpec(memory_space=pltpu.SMEM)
ANY = pl.BlockSpec(memory_space=pl.ANY)
HBM = pl.BlockSpec(memory_space=pltpu.HBM)
PARAMS = pltpu.CompilerParams(vmem_limit_bytes=16 * 1024 * 1024)
WEIGHT_PARAMS = pltpu.CompilerParams(vmem_limit_bytes=46 * 1024 * 1024)
def moved(block, axis, step):
    count = SIZES[axis]
    return lax.ppermute(block, axis, [(i, (i + step) % count) for i in range(count)])


def sign_matrix(order, scale):
    i = lax.broadcasted_iota(jnp.int32, (order, order), 0)
    j = lax.broadcasted_iota(jnp.int32, (order, order), 1)
    odd = i & j
    for shift in (4, 2, 1):
        odd = odd ^ (odd >> shift)
    return jnp.where((odd & 1) == 1, -scale, scale).astype(jnp.float32)


def inner_kernel(hidden, out):
    had = sign_matrix(INNER, 1.0 / 64.0).astype(jnp.bfloat16)
    for c in range(GROUPS):
        cols = slice(c * INNER, (c + 1) * INNER)
        out[:, cols] = jnp.dot(hidden[:, cols], had, preferred_element_type=jnp.float32)


def inner_transform(hidden):
    return pl.pallas_call(
        inner_kernel,
        in_specs=[VMEM],
        out_specs=VMEM,
        out_shape=jax.ShapeDtypeStruct((SLAB, WIDTH), jnp.float32),
        compiler_params=PARAMS,
        name="inner_transform",
    )(hidden)


def outer_kernel(block, out):
    out[...] = jnp.dot(
        sign_matrix(N_PIPE, 1.0),
        block[...],
        preferred_element_type=jnp.float32,
        precision=lax.Precision.HIGHEST,
    )


def outer_transform(block):
    return pl.pallas_call(
        outer_kernel,
        in_specs=[VMEM],
        out_specs=VMEM,
        out_shape=jax.ShapeDtypeStruct((N_PIPE, WIDTH), jnp.float32),
        compiler_params=PARAMS,
        name="outer_transform",
    )(block)


def stack_kernel(*refs):
    blocks, out = refs[:NX], refs[-1]
    for k, block in enumerate(blocks):
        out[k * SLAB : (k + 1) * SLAB, :] = block[...]


def stack(blocks, after):
    return pl.pallas_call(
        stack_kernel,
        in_specs=[VMEM] * NX + [ANY],
        out_specs=VMEM,
        out_shape=jax.ShapeDtypeStruct((NX * SLAB, WIDTH), jnp.float32),
        compiler_params=PARAMS,
        name="stack",
    )(*blocks, after)


def slab_list(halves, my_x, my_c):
    slabs = []
    for dc, half in enumerate(halves):
        for dx in range(NX):
            t = lax.rem(my_x + NX - dx, NX) * NC + lax.rem(my_c + dc, NC)
            slabs.append((half.at[pl.ds(dx * SLAB, SLAB)], t))
    return slabs


PART = 128
PARTS = WIDTH // PART


def decode_kernel(codes, scales, after, out, done, raw, raw_scales, wide, loaded, stored):
    def load(k):
        r = pl.ds(pl.multiple_of(k * PART, PART), PART)
        return pltpu.make_async_copy(codes.at[r], raw.at[r], loaded.at[k])

    def store(k):
        r = pl.ds(pl.multiple_of(k * PART, PART), PART)
        return pltpu.make_async_copy(raw.at[r], out.at[r], stored.at[k])

    load_scales = pltpu.make_async_copy(scales, raw_scales, loaded.at[PARTS])
    load_scales.start()
    for k in range(PARTS):
        load(k).start()
    done[...] = jnp.zeros((8, 128), jnp.float32)
    load_scales.wait()
    wide[...] = raw_scales[...].astype(jnp.float32)

    @pl.loop(0, PARTS)
    def _(k):
        load(k).wait()
        rows = wide[pl.ds(pl.multiple_of(k * 8, 8), 8), :]
        for i in range(PART // 16):
            at = pl.ds(pl.multiple_of(k * PART + i * 16, 16), 16)
            s = jnp.broadcast_to(rows[i : i + 1, :], (16, COLS)).astype(jnp.bfloat16)
            raw[at, :] = raw[at, :] * s
        store(k).start()

    for k in range(PARTS):
        store(k).wait()


def decode(codes, scales, after):
    return pl.pallas_call(
        decode_kernel,
        in_specs=[HBM, HBM, ANY],
        out_specs=[HBM, VMEM],
        out_shape=[
            jax.ShapeDtypeStruct((WIDTH, COLS), jnp.bfloat16),
            jax.ShapeDtypeStruct((8, 128), jnp.float32),
        ],
        scratch_shapes=[
            pltpu.VMEM((WIDTH, COLS), jnp.bfloat16),
            pltpu.VMEM((WIDTH // 16, COLS), jnp.bfloat16),
            pltpu.VMEM((WIDTH // 16, COLS), jnp.float32),
            pltpu.SemaphoreType.DMA((PARTS + 1,)),
            pltpu.SemaphoreType.DMA((PARTS,)),
        ],
        compiler_params=WEIGHT_PARAMS,
        cost_estimate=pl.CostEstimate(flops=WIDTH * COLS, bytes_accessed=14 << 20, transcendentals=0),
        name="decode",
    )(codes, scales, after)


BN = 512
TILES = COLS // BN


def product_kernel(place, *refs):
    halves, weight, outs, (rows32, rows16, tiles, sems) = refs[:2], refs[2], refs[3:8], refs[8:]
    copies = [
        pltpu.make_async_copy(weight.at[:, pl.ds(k * BN, BN)], tiles.at[k], sems.at[k])
        for k in range(TILES)
    ]
    for copy in copies:
        copy.start()
    my_z, my_y, my_x, my_c = place[0], place[1], place[2], place[3]
    top = jnp.zeros((8, WIDTH), jnp.float32)
    for slab, z in slab_list(halves, my_x, my_c):
        z_step = lax.rem(z - my_z + NZ, NZ)
        for y in range(NY):
            y_step = lax.rem(y - my_y + NY, NY)
            piece = slab[y * OWN : (y + 1) * OWN, :]
            top = jnp.maximum(top, jnp.abs(piece))
            at = pl.multiple_of(y_step * (NZ * OWN) + z_step * OWN, OWN)
            rows32[pl.ds(at, OWN), :] = piece
    rows16[...] = rows32[...].astype(jnp.bfloat16)
    peak = jnp.full((8, 128), jnp.max(top), jnp.float32)
    for out in outs:
        for k in range(out.shape[0] // 8):
            out[k * 8 : (k + 1) * 8, COLS:] = peak

    for k, copy in enumerate(copies):
        copy.wait()
        total = jnp.dot(rows16[...], tiles[k], preferred_element_type=jnp.float32)
        at = 0
        for out in outs:
            out[:, k * BN : (k + 1) * BN] = total[at : at + out.shape[0], :]
            at += out.shape[0]


def product(slabs, weight, place):
    sizes = [64, 64, 32, 32, 64]
    return pl.pallas_call(
        product_kernel,
        in_specs=[SMEM] + [VMEM] * 2 + [HBM],
        out_specs=[VMEM] * 5,
        out_shape=[jax.ShapeDtypeStruct((n, WIDE), jnp.float32) for n in sizes],
        scratch_shapes=[
            pltpu.VMEM((ROWS, WIDTH), jnp.float32),
            pltpu.VMEM((ROWS, WIDTH), jnp.bfloat16),
            pltpu.VMEM((TILES, WIDTH, BN), jnp.bfloat16),
            pltpu.SemaphoreType.DMA((TILES,)),
        ],
        compiler_params=WEIGHT_PARAMS,
        name="product",
    )(place, *slabs, weight)


def relay_kernel(a, first, b, second, out_a, out_b):
    out_a[...] = a[...]
    out_b[...] = b[...]
    out_a[:32, :COLS] += first[:, :COLS]
    out_b[32:, :COLS] += second[:, :COLS]
    other = jnp.maximum(first[:, COLS:], second[:, COLS:])
    out_a[:32, COLS:] = jnp.maximum(a[:32, COLS:], other)
    out_b[:32, COLS:] = jnp.maximum(b[:32, COLS:], other)


def relay(a, first, b, second):
    shape = jax.ShapeDtypeStruct((64, WIDE), jnp.float32)
    return pl.pallas_call(
        relay_kernel,
        in_specs=[VMEM] * 4,
        out_specs=[VMEM] * 2,
        out_shape=[shape] * 2,
        compiler_params=PARAMS,
        name="relay",
    )(a, first, b, second)


def y_sum_kernel(a, b, c, after, *outs):
    top = jnp.maximum(jnp.maximum(a[:8, COLS:], b[:8, COLS:]), c[:8, COLS:])
    for k, out in enumerate(outs):
        r = slice(k * OWN, (k + 1) * OWN)
        out[:, :COLS] = a[r, :COLS] + b[r, :COLS] + c[r, :COLS]
        out[:, COLS:] = top


def y_sum(a, b, c, after):
    return pl.pallas_call(
        y_sum_kernel,
        in_specs=[VMEM] * 3 + [ANY],
        out_specs=[VMEM] * NZ,
        out_shape=[jax.ShapeDtypeStruct((OWN, WIDE), jnp.float32)] * NZ,
        compiler_params=PARAMS,
        name="y_sum",
    )(a, b, c, after)


def z_sum_kernel(*refs):
    parts, residual, scale, summed, rounded, squares, top = refs[:NZ], *refs[NZ:]
    total = parts[0][:, :COLS]
    peak = parts[0][:, COLS:]
    for part in parts[1:]:
        total += part[:, :COLS]
        peak = jnp.maximum(peak, part[:, COLS:])
    total = residual[...].astype(jnp.float32) + total * scale[0]
    summed[...] = total
    rounded[...] = total.astype(jnp.bfloat16)
    squares[...] = jnp.broadcast_to(jnp.sum(total * total, axis=1, keepdims=True), (OWN, 128))
    top[...] = peak


def z_sum(parts, residual, weight_scale):
    return pl.pallas_call(
        z_sum_kernel,
        in_specs=[VMEM] * (NZ + 1) + [SMEM],
        out_specs=[VMEM] * 4,
        out_shape=[
            jax.ShapeDtypeStruct((OWN, COLS), jnp.float32),
            jax.ShapeDtypeStruct((OWN, COLS), jnp.bfloat16),
            jax.ShapeDtypeStruct((OWN, 128), jnp.float32),
            jax.ShapeDtypeStruct((OWN, 128), jnp.float32),
        ],
        compiler_params=PARAMS,
        name="z_sum",
    )(*parts, residual, weight_scale)


def norm_kernel(summed, a, b, c, d, gain, after, out):
    mean = (a[...] + b[...] + c[...] + d[...]) * (1.0 / (COLS * N_TENSOR))
    factor = lax.rsqrt(mean + 1e-05)[:, :1]
    out[...] = (summed[...] * factor * gain[...].astype(jnp.float32)).astype(jnp.bfloat16)


def norm(summed, squares, gain, after):
    return pl.pallas_call(
        norm_kernel,
        in_specs=[VMEM] * 6 + [ANY],
        out_specs=VMEM,
        out_shape=jax.ShapeDtypeStruct((OWN, COLS), jnp.bfloat16),
        compiler_params=PARAMS,
        name="norm",
    )(summed, *squares, gain, after)


def split3(value):
    parts = []
    for _ in range(3):
        part = value.astype(jnp.bfloat16)
        parts.append(part)
        value = value - part.astype(jnp.float32)
    return parts


def blocks_kernel(place, *refs):
    halves, after, narrow, factor, wide = refs[:2], *refs[2:]
    my_x, my_c = place[2], place[3]
    lane = lax.broadcasted_iota(jnp.int32, (SLAB, WIDTH), 1)
    for slab, t in slab_list(halves, my_x, my_c):
        at = pl.ds(pl.multiple_of(t * SLAB, SLAB), SLAB)
        big = jnp.abs(slab[...])
        for shift in (1, 2, 4, 8):
            up = pltpu.roll(big, WIDTH - shift, 1)
            down = pltpu.roll(big, shift, 1)
            big = jnp.maximum(big, jnp.where((lane & shift) == 0, up, down))
        wide[at, :] = big
        factor[at, :] = 6.0 / big
    block = lax.broadcasted_iota(jnp.int32, (WIDTH // 16, WIDTH), 0)
    unit = lax.broadcasted_iota(jnp.int32, (WIDTH // 16, WIDTH), 1)
    first = jnp.where(unit == 16 * block, 1.0, 0.0).astype(jnp.bfloat16)
    narrow[...] = sum(
        lax.dot_general(first, part, (((1,), (1,)), ((), ())), preferred_element_type=jnp.float32)
        for part in split3(wide[...])
    )


def blocks(slabs, place, after):
    return pl.pallas_call(
        blocks_kernel,
        in_specs=[SMEM] + [VMEM] * 2 + [ANY],
        out_specs=[VMEM] * 2,
        out_shape=[
            jax.ShapeDtypeStruct((WIDTH // 16, ROWS), jnp.float32),
            jax.ShapeDtypeStruct((ROWS, WIDTH), jnp.float32),
        ],
        scratch_shapes=[pltpu.VMEM((ROWS, WIDTH), jnp.float32)],
        compiler_params=PARAMS,
        name="blocks",
    )(place, *slabs, after)


def encode_kernel(place, *refs):
    halves, narrow, factor, peak, payload, block_scales, done = refs[:2], *refs[2:]
    done[...] = peak[...]
    my_x, my_c = place[2], place[3]
    top = peak[...]
    low = top / 64.0
    most = (6.0 / low)[:1, :1]
    block_scales[...] = jnp.maximum(narrow[...], low[:1, :1]) * (448.0 / top)[:1, :1]
    for slab, t in slab_list(halves, my_x, my_c):
        at = pl.ds(pl.multiple_of(t * SLAB, SLAB), SLAB)
        payload[at, :] = (slab[...] * jnp.minimum(factor[at, :], most)).astype(jnp.bfloat16)


def encode(slabs, place, narrow, factor, peak):
    return pl.pallas_call(
        encode_kernel,
        in_specs=[SMEM] + [VMEM] * 5,
        out_specs=[VMEM] * 3,
        out_shape=[
            jax.ShapeDtypeStruct((ROWS, WIDTH), jnp.bfloat16),
            jax.ShapeDtypeStruct((WIDTH // 16, ROWS), jnp.float32),
            jax.ShapeDtypeStruct((OWN, 128), jnp.float32),
        ],
        compiler_params=PARAMS,
        name="encode",
    )(place, *slabs, narrow, factor, peak)


def on_device(gate_pre, up_pre, down_codes, down_scales, weight_scale, residual, norm_gain):
    place = jnp.stack([lax.axis_index(a) for a in ("z", "y", "x", "c")]).astype(jnp.int32)
    first_row = (place[2] * NC + place[3]) * SLAB
    gate = lax.dynamic_slice_in_dim(gate_pre, first_row, SLAB, 0).astype(jnp.float32)
    up = lax.dynamic_slice_in_dim(up_pre, first_row, SLAB, 0).astype(jnp.float32)
    inner = inner_transform((gate / (1.0 + jnp.exp(-gate)) * up).astype(jnp.bfloat16))
    one_row = lax.all_to_all(inner, ("z", "y"), 0, 0, tiled=True)
    turned = outer_transform(one_row)
    own = lax.all_to_all(turned, ("z", "y"), 0, 0, tiled=True)

    mine = [moved(own, "x", k) for k in (1, 2, 3)]
    weight, done = decode(down_codes, down_scales, own)
    mine = stack([own] + mine, done)
    slabs = [mine, moved(mine, "c", 1)]
    here, ahead, far_a, far_b, behind = product(slabs, weight, place)
    first, second = moved(far_a, "y", 1), moved(far_b, "y", -1)
    ahead, behind = relay(ahead, first, behind, second)
    narrow, factor = blocks(slabs, place, ahead)
    parts = y_sum(here, moved(ahead, "y", 1), moved(behind, "y", -1), narrow)
    parts = [parts[0]] + [moved(parts[d], "z", d) for d in (4, 3, 5, 2, 6, 1, 7)]
    summed, rounded, squares, peak = z_sum(parts, residual, weight_scale)
    squares = squares + moved(squares, "c", 1)
    others = [moved(squares, "x", 1), moved(squares, "x", 2), moved(squares, "x", 3)]
    payload, block_scales, done = encode(slabs, place, narrow, factor, peak)
    normed = norm(summed, [squares] + others, norm_gain.reshape(1, COLS), done)
    return payload, block_scales.T, rounded, normed


def solution(mesh):
    mesh = Mesh(mesh.devices.reshape(NZ, NY, NX, NC), ("z", "y", "x", "c"))
    pipe, tensor = ("z", "y"), ("x", "c")
    in_specs = (
        P(None, pipe),
        P(None, pipe),
        P(pipe, tensor),
        P(pipe, tensor),
        P(),
        P(pipe, tensor),
        P(tensor),
    )
    out_specs = (P(None, pipe), P(None, pipe), P(pipe, tensor), P(pipe, tensor))
    return jax.shard_map(
        on_device, mesh=mesh, in_specs=in_specs, out_specs=out_specs, check_vma=False
    )
```

time: 123 us -> 117 us (0.951)
  waiting for transfers between devices: 26.7 us -> 20.3 us
    ppermute x22 -> x19, waiting for transfers between devices: 26.7 us -> 20.3 us  [moved(): lax.ppermute(block, axis, [(i, (i + step) % count) for i in range(count)])]
    ppermute x22 -> x19, starting transfers between devices: 34.6 us -> 34 us  [moved(): lax.ppermute(block, axis, [(i, (i + step) % count) for i in range(count)])]
    pallas_call x8 -> x10, Pallas kernels: 18.1 us -> 18.4 us  [the longest x1 6.31 us: blocks(): pl.pallas_call(blocks_kernel, in_specs=[SMEM] + [VMEM] * 2 + [ANY], out_s...]
    unnamed x19 -> x10, local copies, waits for them, and re-layouts: 3.85 us -> 3.86 us
  transfers between devices with their start and end apart: 22 -> 19, of which waited for: 10 -> 7; matrix products, arithmetic and copies ran while one was open for 1% -> 0% of each run, Pallas kernels for 7% -> 10%
where the time goes in v2:
time: 117 us; the launch traced here: 116 us
  blocking collectives  36.6 us (31%)
  starting transfers between devices  34 us (29%)
  waiting for transfers between devices  20.3 us (17%)
  Pallas kernels  18.5 us (16%)
  local copies, waits for them, and re-layouts  4.32 us (4%)
  between operations  1.44 us (1%)
    ppermute x19, starting transfers between devices, moved(): lax.ppermute(block, axis, [(i, (i + step) % count) for i in range(count)])  34 us
    all_to_all x1, blocking collectives, on_device(): one_row = lax.all_to_all(inner, ('z', 'y'), 0, 0, tiled=True)  21.9 us
    ppermute x19, waiting for transfers between devices, moved(): lax.ppermute(block, axis, [(i, (i + step) % count) for i in range(count)])  20.3 us
    all_to_all x1, blocking collectives, on_device(): own = lax.all_to_all(turned, ('z', 'y'), 0, 0, tiled=True)  14.6 us
    pallas_call x1, Pallas kernels, blocks(): pl.pallas_call(blocks_kernel, in_specs=[SMEM] + [VMEM] * 2 + [ANY], out_s...  6.31 us
    pallas_call x1, Pallas kernels, product(): pl.pallas_call(product_kernel, in_specs=[SMEM] + [VMEM] * 2 + [HBM], out_...  4.76 us
    unnamed x10, local copies, waits for them, and re-layouts  3.86 us
    pallas_call x1, Pallas kernels, decode(): pl.pallas_call(decode_kernel, in_specs=[HBM, HBM, ANY], out_specs=[HBM, V...  3.51 us
  transfers between devices with their start and end apart: 19, of which 7 were waited for; matrix products, arithmetic and copies ran while one was open for 0% of the time, Pallas kernels for 10%

profile of v2, /device:TPU:1, one launch (start us, length us, event | category | flops | bytes accessed | tf_op | source)
XLA Modules:
  0.0 116.3 jit_solution(17414940654132669939)
XLA Ops:
  0.6 1.0 fusion.3.hidden
  1.7 0.2 inner_transform.1
  1.9 0.2 copy.11
  2.1 21.9 %all_to_all.22 = f32[32,1,1664]{2,1,0:T(1,128)S(1)} all-to-all(f32[32,1,1664]{2,1,0:T(1,128)S(1)} %copy.11), channel_id=1, replica_groups=mesh['z'=8,'y'=4,'x'=4,'c'=2] {'z','y'}, dimensions={0} | all-to-all | bytes 425984 | tf_op jit(solution)/shard_map/all_to_all | solution.py:382
  24.1 0.3 outer_transform.1
  24.4 0.2 copy.12
  24.7 14.6 %all_to_all.23 = f32[32,1,1664]{2,1,0:T(1,128)S(1)} all-to-all(f32[32,1,1664]{2,1,0:T(1,128)S(1)} %copy.12), channel_id=1, replica_groups=mesh['z'=8,'y'=4,'x'=4,'c'=2] {'z','y'}, dimensions={0} | all-to-all | bytes 425984 | tf_op jit(solution)/shard_map/all_to_all | solution.py:384
  39.3 1.3 %collective-permute-start = (f32[32,1664]{1,0:T(8,128)S(1)}, f32[32,1664]{1,0:T(8,128)S(1)}, u32[]{:S(2)}, u32[]{:S(2)}) collective-permute-start(f32[32,1664]{1,0:T(8,128)S(1)} %bitcast.13), channel_id=1, source_target_pairs={{0,2},{2,4},{4,6},{6,0},{1,3},{3,5},{5,7},{7,1},{8,10},{10,12},{12... | collective-permute-start | bytes 638984 | tf_op jit(solution)/shard_map/ppermute | solution.py:26
  40.6 2.5 %collective-permute-start.1 = (f32[32,1664]{1,0:T(8,128)S(1)}, f32[32,1664]{1,0:T(8,128)S(1)}, u32[]{:S(2)}, u32[]{:S(2)}) collective-permute-start(f32[32,1664]{1,0:T(8,128)S(1)} %bitcast.14), channel_id=1, source_target_pairs={{0,4},{2,6},{4,0},{6,2},{1,5},{3,7},{5,1},{7,3},{8,12},{10,14},{12... | collective-permute-start | bytes 638984 | tf_op jit(solution)/shard_map/ppermute | solution.py:26
  43.1 1.1 collective-permute-start.2
  44.2 0.0 copy-start.1
  44.2 1.0 copy-done.1
  45.2 3.5 %decode.1 = (bf16[1664,2048]{1,0:T(8,128)(2,1)S(1)}, f32[8,128]{1,0:T(8,128)S(1)}) custom-call(bf16[1664,2048]{1,0:T(8,128)(2,1)} %codes.1, bf16[104,2048]{1,0:T(8,128)(2,1)S(1)} %copy-done.1, f32[32,1664]{1,0:T(8,128)S(1)} %bitcast.16), custom_call_target="tpu_custom_call" | custom-call | flops 3407872 | bytes 14680064 | tf_op jit(solution)/shard_map/decode/pallas_call | solution.py:138
  48.8 0.0 copy-start
  48.8 2.8 %copy-done = bf16[1664,2048]{1,0:T(8,128)(2,1)} copy-done((bf16[1664,2048]{1,0:T(8,128)(2,1)}, bf16[1664,2048]{1,0:T(8,128)(2,1)S(1)}, u32[]{:S(2)}) %copy-start) | copy-done | bytes 6815768
  51.6 0.0 collective-permute-done.refs_1_
  51.6 0.0 collective-permute-done.1.refs_2_
  51.6 0.0 collective-permute-done.2.refs_3_
  51.6 0.1 stack.21.refs_0_
  51.7 4.1 %collective-permute-start.3 = (f32[128,1664]{1,0:T(8,128)S(1)}, f32[128,1664]{1,0:T(8,128)S(1)}, u32[]{:S(2)}, u32[]{:S(2)}) collective-permute-start(f32[128,1664]{1,0:T(8,128)S(1)} %stack.21.refs_0_), channel_id=1, source_target_pairs={{0,1},{1,0},{2,3},{3,2},{4,5},{5,4},{6,7},{7,6},{8,9},{9,8},{10,11... | collective-permute-start | bytes 2555912 | tf_op jit(solution)/shard_map/ppermute | solution.py:26
  55.7 0.1 pad_add_fusion.place
  55.8 1.9 %collective-permute-done.3.refs_1_ = f32[128,1664]{1,0:T(8,128)S(1)} collective-permute-done((f32[128,1664]{1,0:T(8,128)S(1)}, f32[128,1664]{1,0:T(8,128)S(1)}, u32[]{:S(2)}, u32[]{:S(2)}) %collective-permute-start.3) | collective-permute-done | bytes 852000 | tf_op jit(solution)/shard_map/ppermute | solution.py:26
  57.7 0.0 copy-start.2
  57.7 0.0 copy-start.3
  57.7 4.8 %product.1 = (f32[64,2176]{1,0:T(8,128)S(1)}, f32[64,2176]{1,0:T(8,128)S(1)}, f32[32,2176]{1,0:T(8,128)S(1)}, f32[32,2176]{1,0:T(8,128)S(1)}, f32[64,2176]{1,0:T(8,128)S(1)}) custom-call(s32[4]{0:T(128)S(1)} %pad_add_fusion.place, f32[128,1664]{1,0:T(8,128)S(1)} %stack.21.refs_0_, f32[128,1664]{1,0:T(8,128)S(1)} %collective-permute-done.3.refs_1_, ...), custom_call_target="tpu_custom_call" | custom-call | tf_op jit(solution)/shard_map/product/pallas_call | solution.py:198
  62.5 0.1 collective-permute-start.4
  62.6 2.7 %collective-permute-start.5 = (f32[32,2176]{1,0:T(8,128)S(1)}, f32[32,2176]{1,0:T(8,128)S(1)}, u32[]{:S(2)}, u32[]{:S(2)}) collective-permute-start(f32[32,2176]{1,0:T(8,128)S(1)} %get-tuple-element.35), channel_id=1, source_target_pairs={{0,24},{8,0},{16,8},{24,16},{1,25},{9,1},{17,9},{25,17},{2,26},{10... | collective-permute-start | bytes 835592 | tf_op jit(solution)/shard_map/ppermute | solution.py:26
  65.3 6.4 %collective-permute-done.4.first = f32[32,2176]{1,0:T(8,128)S(1)} collective-permute-done((f32[32,2176]{1,0:T(8,128)S(1)}, f32[32,2176]{1,0:T(8,128)S(1)}, u32[]{:S(2)}, u32[]{:S(2)}) %collective-permute-start.4) | collective-permute-done | bytes 278560 | tf_op jit(solution)/shard_map/ppermute | solution.py:26
  71.7 0.0 collective-permute-done.5.second
  71.7 0.1 relay.1
  71.8 0.1 collective-permute-start.6
  71.9 2.7 %collective-permute-start.7 = (f32[64,2176]{1,0:T(8,128)S(1)}, f32[64,2176]{1,0:T(8,128)S(1)}, u32[]{:S(2)}, u32[]{:S(2)}) collective-permute-start(f32[64,2176]{1,0:T(8,128)S(1)} %get-tuple-element.40), channel_id=1, source_target_pairs={{0,24},{8,0},{16,8},{24,16},{1,25},{9,1},{17,9},{25,17},{2,26},{10... | collective-permute-start | bytes 1671176 | tf_op jit(solution)/shard_map/ppermute | solution.py:26
  74.5 6.3 %blocks.1 = (f32[104,256]{1,0:T(8,128)S(1)}, f32[256,1664]{1,0:T(8,128)S(1)}) custom-call(s32[4]{0:T(128)S(1)} %pad_add_fusion.place, f32[128,1664]{1,0:T(8,128)S(1)} %stack.21.refs_0_, f32[128,1664]{1,0:T(8,128)S(1)} %collective-permute-done.3.refs_1_, f32[64,2176]{1,0:T(8,128)S(1)} %get-tuple-element.36.refs_2_), custom_call_target="tpu_custom_call" | custom-call | tf_op jit(solution)/shard_map/blocks/pallas_call | solution.py:334
  80.9 5.1 %collective-permute-done.6.b = f32[64,2176]{1,0:T(8,128)S(1)} collective-permute-done((f32[64,2176]{1,0:T(8,128)S(1)}, f32[64,2176]{1,0:T(8,128)S(1)}, u32[]{:S(2)}, u32[]{:S(2)}) %collective-permute-start.6) | collective-permute-done | bytes 557088 | tf_op jit(solution)/shard_map/ppermute | solution.py:26
  86.0 0.0 collective-permute-done.7.c
  86.0 0.1 y_sum.1
  86.1 0.3 collective-permute-start.10
  86.4 2.1 %collective-permute-start.11 = (f32[8,2176]{1,0:T(8,128)S(1)}, f32[8,2176]{1,0:T(8,128)S(1)}, u32[]{:S(2)}, u32[]{:S(2)}) collective-permute-start(f32[8,2176]{1,0:T(8,128)S(1)} %get-tuple-element.45), channel_id=1, source_target_pairs={{0,64},{32,96},{64,128},{96,160},{128,192},{160,224},{192,0},{224,... | collective-permute-start | bytes 208904 | tf_op jit(solution)/shard_map/ppermute | solution.py:26
  88.5 1.5 %collective-permute-start.12 = (f32[8,2176]{1,0:T(8,128)S(1)}, f32[8,2176]{1,0:T(8,128)S(1)}, u32[]{:S(2)}, u32[]{:S(2)}) collective-permute-start(f32[8,2176]{1,0:T(8,128)S(1)} %get-tuple-element.46), channel_id=1, source_target_pairs={{0,192},{32,224},{64,0},{96,32},{128,64},{160,96},{192,128},{224,1... | collective-permute-start | bytes 208904 | tf_op jit(solution)/shard_map/ppermute | solution.py:26
  90.0 1.3 %collective-permute-start.13 = (f32[8,2176]{1,0:T(8,128)S(1)}, f32[8,2176]{1,0:T(8,128)S(1)}, u32[]{:S(2)}, u32[]{:S(2)}) collective-permute-start(f32[8,2176]{1,0:T(8,128)S(1)} %get-tuple-element.47), channel_id=1, source_target_pairs={{0,32},{32,64},{64,96},{96,128},{128,160},{160,192},{192,224},{224... | collective-permute-start | bytes 208904 | tf_op jit(solution)/shard_map/ppermute | solution.py:26
  91.3 1.4 %collective-permute-start.14 = (f32[8,2176]{1,0:T(8,128)S(1)}, f32[8,2176]{1,0:T(8,128)S(1)}, u32[]{:S(2)}, u32[]{:S(2)}) collective-permute-start(f32[8,2176]{1,0:T(8,128)S(1)} %get-tuple-element.48), channel_id=1, source_target_pairs={{0,224},{32,0},{64,32},{96,64},{128,96},{160,128},{192,160},{224,1... | collective-permute-start | bytes 208904 | tf_op jit(solution)/shard_map/ppermute | solution.py:26
  92.6 0.0 collective-permute-done.10.refs_3_
  92.7 4.4 %collective-permute-start.8 = (f32[8,2176]{1,0:T(8,128)S(1)}, f32[8,2176]{1,0:T(8,128)S(1)}, u32[]{:S(2)}, u32[]{:S(2)}) collective-permute-start(f32[8,2176]{1,0:T(8,128)S(1)} %get-tuple-element.42), channel_id=1, source_target_pairs={{0,128},{32,160},{64,192},{96,224},{128,0},{160,32},{192,64},{224,... | collective-permute-start | bytes 208904 | tf_op jit(solution)/shard_map/ppermute | solution.py:26
  97.1 0.0 collective-permute-done.11.refs_4_
  97.1 0.0 collective-permute-start.9
  97.7 0.0 collective-permute-done.12.refs_5_
  97.7 0.0 collective-permute-done.13.refs_6_
  97.8 0.0 collective-permute-done.14.refs_7_
  97.8 3.3 %collective-permute-done.8.refs_1_ = f32[8,2176]{1,0:T(8,128)S(1)} collective-permute-done((f32[8,2176]{1,0:T(8,128)S(1)}, f32[8,2176]{1,0:T(8,128)S(1)}, u32[]{:S(2)}, u32[]{:S(2)}) %collective-permute-start.8) | collective-permute-done | bytes 69664 | tf_op jit(solution)/shard_map/ppermute | solution.py:26
  101.0 2.6 %collective-permute-done.9.refs_2_ = f32[8,2176]{1,0:T(8,128)S(1)} collective-permute-done((f32[8,2176]{1,0:T(8,128)S(1)}, f32[8,2176]{1,0:T(8,128)S(1)}, u32[]{:S(2)}, u32[]{:S(2)}) %collective-permute-start.9) | collective-permute-done | bytes 69664 | tf_op jit(solution)/shard_map/ppermute | solution.py:26
  103.6 0.0 copy-done.2
  103.6 0.7 z_sum.1
  104.3 5.9 %collective-permute-start.15 = (f32[8,128]{1,0:T(8,128)S(1)}, f32[8,128]{1,0:T(8,128)S(1)}, u32[]{:S(2)}, u32[]{:S(2)}) collective-permute-start(f32[8,128]{1,0:T(8,128)S(1)} %get-tuple-element.54), channel_id=1, source_target_pairs={{0,1},{1,0},{2,3},{3,2},{4,5},{5,4},{6,7},{7,6},{8,9},{9,8},{10,11... | collective-permute-start | bytes 12296 | tf_op jit(solution)/shard_map/ppermute | solution.py:26
  110.1 0.8 collective-permute-done.15
  111.0 0.3 collective-permute-start.16
  111.2 0.7 collective-permute-start.17
  112.0 1.7 %collective-permute-start.18 = (f32[8,128]{1,0:T(8,128)S(1)}, f32[8,128]{1,0:T(8,128)S(1)}, u32[]{:S(2)}, u32[]{:S(2)}) collective-permute-start(f32[8,128]{1,0:T(8,128)S(1)} %add.20.a), channel_id=1, source_target_pairs={{0,6},{2,0},{4,2},{6,4},{1,7},{3,1},{5,3},{7,5},{8,14},{10,8},{12,... | collective-permute-start | bytes 12296 | tf_op jit(solution)/shard_map/ppermute | solution.py:26
  113.7 0.0 copy-done.3
  113.7 1.7 %encode.1 = (bf16[256,1664]{1,0:T(8,128)(2,1)}, f32[104,256]{1,0:T(8,128)}, f32[8,128]{1,0:T(8,128)S(1)}) custom-call(s32[4]{0:T(128)S(1)} %pad_add_fusion.place, f32[128,1664]{1,0:T(8,128)S(1)} %stack.21.refs_0_, f32[128,1664]{1,0:T(8,128)S(1)} %collective-permute-done.3.refs_1_, f32[104,256]{1,0:T(8,128)S(1)} %get-tuple-element.37.after.refs_2_, ...), custom_call_target="tpu_custom_call" | custom-call | tf_op jit(solution)/shard_map/encode/pallas_call | solution.py:362
  115.4 0.0 collective-permute-done.16.b
  115.4 0.0 collective-permute-done.17.c
  115.4 0.1 collective-permute-done.18.d
  115.6 0.7 norm.1
  (4 shorter events, 0.0 us)
Async XLA Ops:
  39.3 12.2 %collective-permute-start = (f32[32,1664]{1,0:T(8,128)S(1)}, f32[32,1664]{1,0:T(8,128)S(1)}, u32[]{:S(2)}, u32[]{:S(2)}) collective-permute-start(f32[32,1664]{1,0:T(8,128)S(1)} %bitcast.13), channel_id=1, source_target_pairs={{0,2},{2,4},{4,6},{6,0},{1,3},{3,5},{5,7},{7,1},{8,10},{10,12},{12... | collective-permute-start | bytes 638984 | tf_op jit(solution)/shard_map/ppermute | solution.py:26
  40.6 11.0 %collective-permute-start.1 = (f32[32,1664]{1,0:T(8,128)S(1)}, f32[32,1664]{1,0:T(8,128)S(1)}, u32[]{:S(2)}, u32[]{:S(2)}) collective-permute-start(f32[32,1664]{1,0:T(8,128)S(1)} %bitcast.14), channel_id=1, source_target_pairs={{0,4},{2,6},{4,0},{6,2},{1,5},{3,7},{5,1},{7,3},{8,12},{10,14},{12... | collective-permute-start | bytes 638984 | tf_op jit(solution)/shard_map/ppermute | solution.py:26
  43.1 8.5 %collective-permute-start.2 = (f32[32,1664]{1,0:T(8,128)S(1)}, f32[32,1664]{1,0:T(8,128)S(1)}, u32[]{:S(2)}, u32[]{:S(2)}) collective-permute-start(f32[32,1664]{1,0:T(8,128)S(1)} %bitcast.15), channel_id=1, source_target_pairs={{0,6},{2,0},{4,2},{6,4},{1,7},{3,1},{5,3},{7,5},{8,14},{10,8},{12,... | collective-permute-start | bytes 638984 | tf_op jit(solution)/shard_map/ppermute | solution.py:26
  44.2 1.0 copy-start.1
  48.8 2.8 %copy-start = (bf16[1664,2048]{1,0:T(8,128)(2,1)}, bf16[1664,2048]{1,0:T(8,128)(2,1)S(1)}, u32[]{:S(2)}) copy-start(bf16[1664,2048]{1,0:T(8,128)(2,1)S(1)} %get-tuple-element.31.refs_2_) | copy-start | bytes 20447236
  51.7 6.1 %collective-permute-start.3 = (f32[128,1664]{1,0:T(8,128)S(1)}, f32[128,1664]{1,0:T(8,128)S(1)}, u32[]{:S(2)}, u32[]{:S(2)}) collective-permute-start(f32[128,1664]{1,0:T(8,128)S(1)} %stack.21.refs_0_), channel_id=1, source_target_pairs={{0,1},{1,0},{2,3},{3,2},{4,5},{5,4},{6,7},{7,6},{8,9},{9,8},{10,11... | collective-permute-start | bytes 2555912 | tf_op jit(solution)/shard_map/ppermute | solution.py:26
  57.7 45.9 %copy-start.2 = (bf16[8,2048]{1,0:T(8,128)(2,1)S(1)}, bf16[8,2048]{1,0:T(8,128)(2,1)}, u32[]{:S(2)}) copy-start(bf16[8,2048]{1,0:T(8,128)(2,1)} %refs_8_.1) | copy-start | bytes 98308
  57.7 55.9 %copy-start.3 = (bf16[2048]{0:T(1024)(128)(2,1)S(1)}, bf16[2048]{0:T(1024)(128)(2,1)}, u32[]{:S(2)}) copy-start(bf16[2048]{0:T(1024)(128)(2,1)} %param.13) | copy-start | bytes 12292
  62.5 9.2 %collective-permute-start.4 = (f32[32,2176]{1,0:T(8,128)S(1)}, f32[32,2176]{1,0:T(8,128)S(1)}, u32[]{:S(2)}, u32[]{:S(2)}) collective-permute-start(f32[32,2176]{1,0:T(8,128)S(1)} %get-tuple-element.33), channel_id=1, source_target_pairs={{0,8},{8,16},{16,24},{24,0},{1,9},{9,17},{17,25},{25,1},{2,10},{10... | collective-permute-start | bytes 835592 | tf_op jit(solution)/shard_map/ppermute | solution.py:26
  62.6 9.1 %collective-permute-start.5 = (f32[32,2176]{1,0:T(8,128)S(1)}, f32[32,2176]{1,0:T(8,128)S(1)}, u32[]{:S(2)}, u32[]{:S(2)}) collective-permute-start(f32[32,2176]{1,0:T(8,128)S(1)} %get-tuple-element.35), channel_id=1, source_target_pairs={{0,24},{8,0},{16,8},{24,16},{1,25},{9,1},{17,9},{25,17},{2,26},{10... | collective-permute-start | bytes 835592 | tf_op jit(solution)/shard_map/ppermute | solution.py:26
  71.8 14.2 %collective-permute-start.6 = (f32[64,2176]{1,0:T(8,128)S(1)}, f32[64,2176]{1,0:T(8,128)S(1)}, u32[]{:S(2)}, u32[]{:S(2)}) collective-permute-start(f32[64,2176]{1,0:T(8,128)S(1)} %get-tuple-element.36.refs_2_), channel_id=1, source_target_pairs={{0,8},{8,16},{16,24},{24,0},{1,9},{9,17},{17,25},{25,1},{2,10},{10... | collective-permute-start | bytes 1671176 | tf_op jit(solution)/shard_map/ppermute | solution.py:26
  71.9 14.1 %collective-permute-start.7 = (f32[64,2176]{1,0:T(8,128)S(1)}, f32[64,2176]{1,0:T(8,128)S(1)}, u32[]{:S(2)}, u32[]{:S(2)}) collective-permute-start(f32[64,2176]{1,0:T(8,128)S(1)} %get-tuple-element.40), channel_id=1, source_target_pairs={{0,24},{8,0},{16,8},{24,16},{1,25},{9,1},{17,9},{25,17},{2,26},{10... | collective-permute-start | bytes 1671176 | tf_op jit(solution)/shard_map/ppermute | solution.py:26
  86.1 6.6 %collective-permute-start.10 = (f32[8,2176]{1,0:T(8,128)S(1)}, f32[8,2176]{1,0:T(8,128)S(1)}, u32[]{:S(2)}, u32[]{:S(2)}) collective-permute-start(f32[8,2176]{1,0:T(8,128)S(1)} %get-tuple-element.44), channel_id=1, source_target_pairs={{0,160},{32,192},{64,224},{96,0},{128,32},{160,64},{192,96},{224,1... | collective-permute-start | bytes 208904 | tf_op jit(solution)/shard_map/ppermute | solution.py:26
  86.4 10.7 %collective-permute-start.11 = (f32[8,2176]{1,0:T(8,128)S(1)}, f32[8,2176]{1,0:T(8,128)S(1)}, u32[]{:S(2)}, u32[]{:S(2)}) collective-permute-start(f32[8,2176]{1,0:T(8,128)S(1)} %get-tuple-element.45), channel_id=1, source_target_pairs={{0,64},{32,96},{64,128},{96,160},{128,192},{160,224},{192,0},{224,... | collective-permute-start | bytes 208904 | tf_op jit(solution)/shard_map/ppermute | solution.py:26
  88.5 9.2 %collective-permute-start.12 = (f32[8,2176]{1,0:T(8,128)S(1)}, f32[8,2176]{1,0:T(8,128)S(1)}, u32[]{:S(2)}, u32[]{:S(2)}) collective-permute-start(f32[8,2176]{1,0:T(8,128)S(1)} %get-tuple-element.46), channel_id=1, source_target_pairs={{0,192},{32,224},{64,0},{96,32},{128,64},{160,96},{192,128},{224,1... | collective-permute-start | bytes 208904 | tf_op jit(solution)/shard_map/ppermute | solution.py:26
  90.0 7.8 %collective-permute-start.13 = (f32[8,2176]{1,0:T(8,128)S(1)}, f32[8,2176]{1,0:T(8,128)S(1)}, u32[]{:S(2)}, u32[]{:S(2)}) collective-permute-start(f32[8,2176]{1,0:T(8,128)S(1)} %get-tuple-element.47), channel_id=1, source_target_pairs={{0,32},{32,64},{64,96},{96,128},{128,160},{160,192},{192,224},{224... | collective-permute-start | bytes 208904 | tf_op jit(solution)/shard_map/ppermute | solution.py:26
  91.3 6.5 %collective-permute-start.14 = (f32[8,2176]{1,0:T(8,128)S(1)}, f32[8,2176]{1,0:T(8,128)S(1)}, u32[]{:S(2)}, u32[]{:S(2)}) collective-permute-start(f32[8,2176]{1,0:T(8,128)S(1)} %get-tuple-element.48), channel_id=1, source_target_pairs={{0,224},{32,0},{64,32},{96,64},{128,96},{160,128},{192,160},{224,1... | collective-permute-start | bytes 208904 | tf_op jit(solution)/shard_map/ppermute | solution.py:26
  92.7 8.4 %collective-permute-start.8 = (f32[8,2176]{1,0:T(8,128)S(1)}, f32[8,2176]{1,0:T(8,128)S(1)}, u32[]{:S(2)}, u32[]{:S(2)}) collective-permute-start(f32[8,2176]{1,0:T(8,128)S(1)} %get-tuple-element.42), channel_id=1, source_target_pairs={{0,128},{32,160},{64,192},{96,224},{128,0},{160,32},{192,64},{224,... | collective-permute-start | bytes 208904 | tf_op jit(solution)/shard_map/ppermute | solution.py:26
  97.1 6.5 %collective-permute-start.9 = (f32[8,2176]{1,0:T(8,128)S(1)}, f32[8,2176]{1,0:T(8,128)S(1)}, u32[]{:S(2)}, u32[]{:S(2)}) collective-permute-start(f32[8,2176]{1,0:T(8,128)S(1)} %get-tuple-element.43), channel_id=1, source_target_pairs={{0,96},{32,128},{64,160},{96,192},{128,224},{160,0},{192,32},{224,... | collective-permute-start | bytes 208904 | tf_op jit(solution)/shard_map/ppermute | solution.py:26
  104.3 6.7 %collective-permute-start.15 = (f32[8,128]{1,0:T(8,128)S(1)}, f32[8,128]{1,0:T(8,128)S(1)}, u32[]{:S(2)}, u32[]{:S(2)}) collective-permute-start(f32[8,128]{1,0:T(8,128)S(1)} %get-tuple-element.54), channel_id=1, source_target_pairs={{0,1},{1,0},{2,3},{3,2},{4,5},{5,4},{6,7},{7,6},{8,9},{9,8},{10,11... | collective-permute-start | bytes 12296 | tf_op jit(solution)/shard_map/ppermute | solution.py:26
  111.0 4.4 %collective-permute-start.16 = (f32[8,128]{1,0:T(8,128)S(1)}, f32[8,128]{1,0:T(8,128)S(1)}, u32[]{:S(2)}, u32[]{:S(2)}) collective-permute-start(f32[8,128]{1,0:T(8,128)S(1)} %add.20.a), channel_id=1, source_target_pairs={{0,2},{2,4},{4,6},{6,0},{1,3},{3,5},{5,7},{7,1},{8,10},{10,12},{12... | collective-permute-start | bytes 12296 | tf_op jit(solution)/shard_map/ppermute | solution.py:26
  111.2 4.2 %collective-permute-start.17 = (f32[8,128]{1,0:T(8,128)S(1)}, f32[8,128]{1,0:T(8,128)S(1)}, u32[]{:S(2)}, u32[]{:S(2)}) collective-permute-start(f32[8,128]{1,0:T(8,128)S(1)} %add.20.a), channel_id=1, source_target_pairs={{0,4},{2,6},{4,0},{6,2},{1,5},{3,7},{5,1},{7,3},{8,12},{10,14},{12... | collective-permute-start | bytes 12296 | tf_op jit(solution)/shard_map/ppermute | solution.py:26
  112.0 3.6 %collective-permute-start.18 = (f32[8,128]{1,0:T(8,128)S(1)}, f32[8,128]{1,0:T(8,128)S(1)}, u32[]{:S(2)}, u32[]{:S(2)}) collective-permute-start(f32[8,128]{1,0:T(8,128)S(1)} %add.20.a), channel_id=1, source_target_pairs={{0,6},{2,0},{4,2},{6,4},{1,7},{3,1},{5,3},{7,5},{8,14},{10,8},{12,... | collective-permute-start | bytes 12296 | tf_op jit(solution)/shard_map/ppermute | solution.py:26

commit v3 on v2

--- a/solution.py
+++ b/solution.py
@@ -20,6 +20,7 @@
 ANY = pl.BlockSpec(memory_space=pl.ANY)
 HBM = pl.BlockSpec(memory_space=pltpu.HBM)
 PARAMS = pltpu.CompilerParams(vmem_limit_bytes=16 * 1024 * 1024)
+DECODE_PARAMS = pltpu.CompilerParams(vmem_limit_bytes=50 * 1024 * 1024)
 WEIGHT_PARAMS = pltpu.CompilerParams(vmem_limit_bytes=46 * 1024 * 1024)
 def moved(block, axis, step):
     count = SIZES[axis]
@@ -73,30 +74,23 @@
     )(block)
 
 
-def stack_kernel(*refs):
-    blocks, out = refs[:NX], refs[-1]
-    for k, block in enumerate(blocks):
-        out[k * SLAB : (k + 1) * SLAB, :] = block[...]
-
-
-def stack(blocks, after):
-    return pl.pallas_call(
-        stack_kernel,
-        in_specs=[VMEM] * NX + [ANY],
+def hand_on_kernel(block, after, out):
+    out[...] = block[...]
+
+
+def hand_on(block, after):
+    return pl.pallas_call(
+        hand_on_kernel,
+        in_specs=[VMEM, ANY],
         out_specs=VMEM,
-        out_shape=jax.ShapeDtypeStruct((NX * SLAB, WIDTH), jnp.float32),
-        compiler_params=PARAMS,
-        name="stack",
-    )(*blocks, after)
-
-
-def slab_list(halves, my_x, my_c):
-    slabs = []
-    for dc, half in enumerate(halves):
-        for dx in range(NX):
-            t = lax.rem(my_x + NX - dx, NX) * NC + lax.rem(my_c + dc, NC)
-            slabs.append((half.at[pl.ds(dx * SLAB, SLAB)], t))
-    return slabs
+        out_shape=jax.ShapeDtypeStruct((SLAB, WIDTH), jnp.float32),
+        compiler_params=PARAMS,
+        name="hand_on",
+    )(block, after)
+
+
+def slab_place(j, my_x, my_c):
+    return lax.rem(my_x + NX - j % NX, NX) * NC + lax.rem(my_c + j // NX, NC)
 
 
 PART = 128
@@ -150,7 +144,7 @@
             pltpu.SemaphoreType.DMA((PARTS + 1,)),
             pltpu.SemaphoreType.DMA((PARTS,)),
         ],
-        compiler_params=WEIGHT_PARAMS,
+        compiler_params=DECODE_PARAMS,
         cost_estimate=pl.CostEstimate(flops=WIDTH * COLS, bytes_accessed=14 << 20, transcendentals=0),
         name="decode",
     )(codes, scales, after)
@@ -158,10 +152,12 @@
 
 BN = 512
 TILES = COLS // BN
+HALF = 32
+Z_ORDER = (4, 3, 5, 2, 6, 1, 7, 0)
 
 
 def product_kernel(place, *refs):
-    halves, weight, outs, (rows32, rows16, tiles, sems) = refs[:2], refs[2], refs[3:8], refs[8:]
+    slabs, weight, outs, (rows32, rows16, tiles, sems) = refs[:8], refs[8], refs[9:17], refs[17:]
     copies = [
         pltpu.make_async_copy(weight.at[:, pl.ds(k * BN, BN)], tiles.at[k], sems.at[k])
         for k in range(TILES)
@@ -169,37 +165,37 @@
     for copy in copies:
         copy.start()
     my_z, my_y, my_x, my_c = place[0], place[1], place[2], place[3]
-    top = jnp.zeros((8, WIDTH), jnp.float32)
-    for slab, z in slab_list(halves, my_x, my_c):
+    biggest = jnp.zeros((8, WIDTH), jnp.float32)
+    for j, slab in enumerate(slabs):
+        z = slab_place(j, my_x, my_c)
         z_step = lax.rem(z - my_z + NZ, NZ)
+        z_at = jnp.int32(0)
+        for k, step in enumerate(Z_ORDER):
+            z_at = jnp.where(z_step == step, k, z_at)
         for y in range(NY):
             y_step = lax.rem(y - my_y + NY, NY)
             piece = slab[y * OWN : (y + 1) * OWN, :]
-            top = jnp.maximum(top, jnp.abs(piece))
-            at = pl.multiple_of(y_step * (NZ * OWN) + z_step * OWN, OWN)
+            biggest = jnp.maximum(biggest, jnp.abs(piece))
+            at = pl.multiple_of(y_step * (NZ * OWN) + z_at * OWN, OWN)
             rows32[pl.ds(at, OWN), :] = piece
     rows16[...] = rows32[...].astype(jnp.bfloat16)
-    peak = jnp.full((8, 128), jnp.max(top), jnp.float32)
+    top = jnp.full((8, 128), jnp.max(biggest), jnp.float32)
     for out in outs:
-        for k in range(out.shape[0] // 8):
-            out[k * 8 : (k + 1) * 8, COLS:] = peak
-
+        for k in range(HALF // 8):
+            out[k * 8 : (k + 1) * 8, COLS:] = top
     for k, copy in enumerate(copies):
         copy.wait()
         total = jnp.dot(rows16[...], tiles[k], preferred_element_type=jnp.float32)
-        at = 0
-        for out in outs:
-            out[:, k * BN : (k + 1) * BN] = total[at : at + out.shape[0], :]
-            at += out.shape[0]
+        for i, out in enumerate(outs):
+            out[:, k * BN : (k + 1) * BN] = total[i * HALF : (i + 1) * HALF, :]
 
 
 def product(slabs, weight, place):
-    sizes = [64, 64, 32, 32, 64]
     return pl.pallas_call(
         product_kernel,
-        in_specs=[SMEM] + [VMEM] * 2 + [HBM],
-        out_specs=[VMEM] * 5,
-        out_shape=[jax.ShapeDtypeStruct((n, WIDE), jnp.float32) for n in sizes],
+        in_specs=[SMEM] + [VMEM] * 8 + [HBM],
+        out_specs=[VMEM] * 8,
+        out_shape=[jax.ShapeDtypeStruct((HALF, WIDE), jnp.float32)] * 8,
         scratch_shapes=[
             pltpu.VMEM((ROWS, WIDTH), jnp.float32),
             pltpu.VMEM((ROWS, WIDTH), jnp.bfloat16),
@@ -211,26 +207,20 @@
     )(place, *slabs, weight)
 
 
-def relay_kernel(a, first, b, second, out_a, out_b):
-    out_a[...] = a[...]
-    out_b[...] = b[...]
-    out_a[:32, :COLS] += first[:, :COLS]
-    out_b[32:, :COLS] += second[:, :COLS]
-    other = jnp.maximum(first[:, COLS:], second[:, COLS:])
-    out_a[:32, COLS:] = jnp.maximum(a[:32, COLS:], other)
-    out_b[:32, COLS:] = jnp.maximum(b[:32, COLS:], other)
-
-
-def relay(a, first, b, second):
-    shape = jax.ShapeDtypeStruct((64, WIDE), jnp.float32)
+def relay_kernel(own, arrived, out):
+    out[:, :COLS] = own[:, :COLS] + arrived[:, :COLS]
+    out[:, COLS:] = jnp.maximum(own[:, COLS:], arrived[:, COLS:])
+
+
+def relay(own, arrived):
     return pl.pallas_call(
         relay_kernel,
-        in_specs=[VMEM] * 4,
-        out_specs=[VMEM] * 2,
-        out_shape=[shape] * 2,
+        in_specs=[VMEM] * 2,
+        out_specs=VMEM,
+        out_shape=jax.ShapeDtypeStruct((HALF, WIDE), jnp.float32),
         compiler_params=PARAMS,
         name="relay",
-    )(a, first, b, second)
+    )(own, arrived)
 
 
 def y_sum_kernel(a, b, c, after, *outs):
@@ -245,15 +235,15 @@
     return pl.pallas_call(
         y_sum_kernel,
         in_specs=[VMEM] * 3 + [ANY],
-        out_specs=[VMEM] * NZ,
-        out_shape=[jax.ShapeDtypeStruct((OWN, WIDE), jnp.float32)] * NZ,
+        out_specs=[VMEM] * (HALF // OWN),
+        out_shape=[jax.ShapeDtypeStruct((OWN, WIDE), jnp.float32)] * (HALF // OWN),
         compiler_params=PARAMS,
         name="y_sum",
     )(a, b, c, after)
 
 
 def z_sum_kernel(*refs):
-    parts, residual, scale, summed, rounded, squares, top = refs[:NZ], *refs[NZ:]
+    parts, residual, scale, after, summed, rounded, squares, top = refs[:NZ], *refs[NZ:]
     total = parts[0][:, :COLS]
     peak = parts[0][:, COLS:]
     for part in parts[1:]:
@@ -266,10 +256,10 @@
     top[...] = peak
 
 
-def z_sum(parts, residual, weight_scale):
+def z_sum(parts, residual, weight_scale, after):
     return pl.pallas_call(
         z_sum_kernel,
-        in_specs=[VMEM] * (NZ + 1) + [SMEM],
+        in_specs=[VMEM] * (NZ + 1) + [SMEM, ANY],
         out_specs=[VMEM] * 4,
         out_shape=[
             jax.ShapeDtypeStruct((OWN, COLS), jnp.float32),
@@ -279,7 +269,7 @@
         ],
         compiler_params=PARAMS,
         name="z_sum",
-    )(*parts, residual, weight_scale)
+    )(*parts, residual, weight_scale, after)
 
 
 def norm_kernel(summed, a, b, c, d, gain, after, out):
@@ -308,12 +298,10 @@
     return parts
 
 
-def blocks_kernel(place, *refs):
-    halves, after, narrow, factor, wide = refs[:2], *refs[2:]
-    my_x, my_c = place[2], place[3]
+def block_maxima(rows, factor, wide):
     lane = lax.broadcasted_iota(jnp.int32, (SLAB, WIDTH), 1)
-    for slab, t in slab_list(halves, my_x, my_c):
-        at = pl.ds(pl.multiple_of(t * SLAB, SLAB), SLAB)
+    for k, slab in enumerate(rows):
+        at = slice(k * SLAB, (k + 1) * SLAB)
         big = jnp.abs(slab[...])
         for shift in (1, 2, 4, 8):
             up = pltpu.roll(big, WIDTH - shift, 1)
@@ -321,47 +309,82 @@
             big = jnp.maximum(big, jnp.where((lane & shift) == 0, up, down))
         wide[at, :] = big
         factor[at, :] = 6.0 / big
-    block = lax.broadcasted_iota(jnp.int32, (WIDTH // 16, WIDTH), 0)
-    unit = lax.broadcasted_iota(jnp.int32, (WIDTH // 16, WIDTH), 1)
+    block = lax.broadcasted_iota(jnp.int32, (WIDTH, WIDTH // 16), 1)
+    unit = lax.broadcasted_iota(jnp.int32, (WIDTH, WIDTH // 16), 0)
     first = jnp.where(unit == 16 * block, 1.0, 0.0).astype(jnp.bfloat16)
-    narrow[...] = sum(
-        lax.dot_general(first, part, (((1,), (1,)), ((), ())), preferred_element_type=jnp.float32)
-        for part in split3(wide[...])
+    return sum(
+        jnp.dot(part, first, preferred_element_type=jnp.float32) for part in split3(wide[...])
     )
 
 
-def blocks(slabs, place, after):
-    return pl.pallas_call(
-        blocks_kernel,
-        in_specs=[SMEM] + [VMEM] * 2 + [ANY],
+def mine_kernel(*refs):
+    rows, (after, narrow, factor, wide) = refs[:4], refs[4:]
+    narrow[...] = block_maxima(rows, factor, wide)
+
+
+def theirs_kernel(place, *refs):
+    rows, (mine, after, narrow, factor, wide, all_rows) = refs[:4], refs[4:]
+    maxima = block_maxima(rows, factor, wide)
+    for dc, half in enumerate((mine[...], maxima)):
+        for dx in range(NX):
+            t = slab_place(dc * NX + dx, place[2], place[3])
+            at = pl.ds(pl.multiple_of(t * SLAB, SLAB), SLAB)
+            all_rows[at, :] = half[dx * SLAB : (dx + 1) * SLAB, :]
+    narrow[...] = all_rows[...].T
+
+
+def mine_blocks(rows, after):
+    return pl.pallas_call(
+        mine_kernel,
+        in_specs=[VMEM] * 4 + [ANY],
+        out_specs=[VMEM] * 2,
+        out_shape=[
+            jax.ShapeDtypeStruct((ROWS // 2, WIDTH // 16), jnp.float32),
+            jax.ShapeDtypeStruct((ROWS // 2, WIDTH), jnp.float32),
+        ],
+        scratch_shapes=[pltpu.VMEM((ROWS // 2, WIDTH), jnp.float32)],
+        compiler_params=PARAMS,
+        name="mine_blocks",
+    )(*rows, after)
+
+
+def theirs_blocks(place, rows, mine, after):
+    return pl.pallas_call(
+        theirs_kernel,
+        in_specs=[SMEM] + [VMEM] * 5 + [ANY],
         out_specs=[VMEM] * 2,
         out_shape=[
             jax.ShapeDtypeStruct((WIDTH // 16, ROWS), jnp.float32),
-            jax.ShapeDtypeStruct((ROWS, WIDTH), jnp.float32),
-        ],
-        scratch_shapes=[pltpu.VMEM((ROWS, WIDTH), jnp.float32)],
-        compiler_params=PARAMS,
-        name="blocks",
-    )(place, *slabs, after)
+            jax.ShapeDtypeStruct((ROWS // 2, WIDTH), jnp.float32),
+        ],
+        scratch_shapes=[
+            pltpu.VMEM((ROWS // 2, WIDTH), jnp.float32),
+            pltpu.VMEM((ROWS, WIDTH // 16), jnp.float32),
+        ],
+        compiler_params=PARAMS,
+        name="theirs_blocks",
+    )(place, *rows, mine, after)
 
 
 def encode_kernel(place, *refs):
-    halves, narrow, factor, peak, payload, block_scales, done = refs[:2], *refs[2:]
+    slabs, factors, (narrow, peak, payload, block_scales, done) = refs[:8], refs[8:10], refs[10:]
     done[...] = peak[...]
     my_x, my_c = place[2], place[3]
     top = peak[...]
     low = top / 64.0
     most = (6.0 / low)[:1, :1]
     block_scales[...] = jnp.maximum(narrow[...], low[:1, :1]) * (448.0 / top)[:1, :1]
-    for slab, t in slab_list(halves, my_x, my_c):
-        at = pl.ds(pl.multiple_of(t * SLAB, SLAB), SLAB)
-        payload[at, :] = (slab[...] * jnp.minimum(factor[at, :], most)).astype(jnp.bfloat16)
-
-
-def encode(slabs, place, narrow, factor, peak):
+    for j, slab in enumerate(slabs):
+        at = pl.ds(pl.multiple_of(slab_place(j, my_x, my_c) * SLAB, SLAB), SLAB)
+        k = j % NX * SLAB
+        value = slab[...] * jnp.minimum(factors[j // NX][k : k + SLAB, :], most)
+        payload[at, :] = value.astype(jnp.bfloat16)
+
+
+def encode(slabs, factors, place, narrow, peak):
     return pl.pallas_call(
         encode_kernel,
-        in_specs=[SMEM] + [VMEM] * 5,
+        in_specs=[SMEM] + [VMEM] * 12,
         out_specs=[VMEM] * 3,
         out_shape=[
             jax.ShapeDtypeStruct((ROWS, WIDTH), jnp.bfloat16),
@@ -370,7 +393,7 @@
         ],
         compiler_params=PARAMS,
         name="encode",
-    )(place, *slabs, narrow, factor, peak)
+    )(place, *slabs, *factors, narrow, peak)
 
 
 def on_device(gate_pre, up_pre, down_codes, down_scales, weight_scale, residual, norm_gain):
@@ -385,18 +408,25 @@
 
     mine = [moved(own, "x", k) for k in (1, 2, 3)]
     weight, done = decode(down_codes, down_scales, own)
-    mine = stack([own] + mine, done)
-    slabs = [mine, moved(mine, "c", 1)]
-    here, ahead, far_a, far_b, behind = product(slabs, weight, place)
+    mine = [own] + [hand_on(block, done) for block in mine]
+    theirs = [moved(block, "c", 1) for block in mine]
+    slabs = mine + theirs
+    here_a, here_b, ahead_a, ahead_b, far_a, far_b, behind_a, behind_b = product(slabs, weight, place)
     first, second = moved(far_a, "y", 1), moved(far_b, "y", -1)
-    ahead, behind = relay(ahead, first, behind, second)
-    narrow, factor = blocks(slabs, place, ahead)
-    parts = y_sum(here, moved(ahead, "y", 1), moved(behind, "y", -1), narrow)
-    parts = [parts[0]] + [moved(parts[d], "z", d) for d in (4, 3, 5, 2, 6, 1, 7)]
-    summed, rounded, squares, peak = z_sum(parts, residual, weight_scale)
+    ahead_b, behind_a = moved(ahead_b, "y", 1), moved(behind_a, "y", -1)
+    ahead_a, behind_b = relay(ahead_a, first), relay(behind_b, second)
+    mine_most, mine_factor = mine_blocks(mine, behind_b)
+    sums_a = y_sum(here_a, moved(ahead_a, "y", 1), behind_a, mine_most)
+    sums_b = y_sum(here_b, ahead_b, moved(behind_b, "y", -1), mine_most)
+    sums = [*sums_a, *sums_b]
+    parts = [moved(part, "z", step) if step else part for part, step in zip(sums, Z_ORDER)]
+    narrow, theirs_factor = theirs_blocks(place, theirs, mine_most, sums_b[0])
+    summed, rounded, squares, peak = z_sum(parts, residual, weight_scale, narrow)
     squares = squares + moved(squares, "c", 1)
     others = [moved(squares, "x", 1), moved(squares, "x", 2), moved(squares, "x", 3)]
-    payload, block_scales, done = encode(slabs, place, narrow, factor, peak)
+    payload, block_scales, done = encode(
+        slabs, (mine_factor, theirs_factor), place, narrow, peak
+    )
     normed = norm(summed, [squares] + others, norm_gain.reshape(1, COLS), done)
     return payload, block_scales.T, rounded, normed
 

time: 117 us -> 109 us (0.932)
  waiting for transfers between devices: 20.3 us -> 11.6 us
  local copies, waits for them, and re-layouts: 4.32 us -> 1.5 us
  Pallas kernels: 18.5 us -> 21.1 us
  starting transfers between devices: 34 us -> 35.2 us
    ppermute x19 -> x24, waiting for transfers between devices: 20.3 us -> 11.6 us  [moved(): lax.ppermute(block, axis, [(i, (i + step) % count) for i in range(count)])]
    unnamed x10 -> x8, local copies, waits for them, and re-layouts: 3.86 us -> 1.04 us
    pallas_call x1, Pallas kernels: 3.51 us -> 6.08 us  [decode(): pl.pallas_call(decode_kernel, in_specs=[HBM, HBM, ANY], out_specs=[HBM, V...]
    ppermute x19 -> x24, starting transfers between devices: 34 us -> 35.2 us  [moved(): lax.ppermute(block, axis, [(i, (i + step) % count) for i in range(count)])]
    pallas_call x6 -> x10, Pallas kernels: 13.6 us -> 13.7 us  [the longest x1 4.93 us: product(): pl.pallas_call(product_kernel, in_specs=[SMEM] + [VMEM] * 8 + [HBM], out_...]
  transfers between devices with their start and end apart: 19 -> 24, of which waited for: 7 -> 8; matrix products, arithmetic and copies ran while one was open for 0% -> 0% of each run, Pallas kernels for 10% -> 13%
where the time goes in v3:
time: 109 us
  blocking collectives  36.6 us (34%)
  starting transfers between devices  35.2 us (32%)
  Pallas kernels  21.1 us (19%)
  waiting for transfers between devices  11.6 us (11%)
  local copies, waits for them, and re-layouts  1.5 us (1%)
  between operations  1.5 us (1%)
  other arithmetic  1.1 us (1%)
    ppermute x24, starting transfers between devices, moved(): lax.ppermute(block, axis, [(i, (i + step) % count) for i in range(count)])  35.2 us
    all_to_all x1, blocking collectives, on_device(): one_row = lax.all_to_all(inner, ('z', 'y'), 0, 0, tiled=True)  21.9 us
    all_to_all x1, blocking collectives, on_device(): own = lax.all_to_all(turned, ('z', 'y'), 0, 0, tiled=True)  14.6 us
    ppermute x24, waiting for transfers between devices, moved(): lax.ppermute(block, axis, [(i, (i + step) % count) for i in range(count)])  11.6 us
    pallas_call x1, Pallas kernels, decode(): pl.pallas_call(decode_kernel, in_specs=[HBM, HBM, ANY], out_specs=[HBM, V...  6.08 us
    pallas_call x1, Pallas kernels, product(): pl.pallas_call(product_kernel, in_specs=[SMEM] + [VMEM] * 8 + [HBM], out_...  4.93 us
    pallas_call x1, Pallas kernels, theirs_blocks(): pl.pallas_call(theirs_kernel, in_specs=[SMEM] + [VMEM] * 5 + [ANY], out_s...  3.43 us
    pallas_call x1, Pallas kernels, mine_blocks(): pl.pallas_call(mine_kernel, in_specs=[VMEM] * 4 + [ANY], out_specs=[VMEM]...  2.8 us
  transfers between devices with their start and end apart: 24, of which 8 were waited for; matrix products, arithmetic and copies ran while one was open for 0% of the time, Pallas kernels for 13%

profile of v3, /device:TPU:1, one launch (start us, length us, event | category | flops | bytes accessed | tf_op | source)
XLA Modules:
  0.0 108.7 jit_solution(8592441566068381398)
XLA Ops:
  0.6 1.0 fusion.3.hidden
  1.7 0.2 inner_transform.1
  1.9 0.2 copy.11
  2.1 21.9 %all_to_all.22 = f32[32,1,1664]{2,1,0:T(1,128)S(1)} all-to-all(f32[32,1,1664]{2,1,0:T(1,128)S(1)} %copy.11), channel_id=1, replica_groups=mesh['z'=8,'y'=4,'x'=4,'c'=2] {'z','y'}, dimensions={0} | all-to-all | bytes 425984 | tf_op jit(solution)/shard_map/all_to_all | solution.py:405
  24.1 0.3 outer_transform.1
  24.4 0.2 copy.12
  24.7 14.6 %all_to_all.23 = f32[32,1,1664]{2,1,0:T(1,128)S(1)} all-to-all(f32[32,1,1664]{2,1,0:T(1,128)S(1)} %copy.12), channel_id=1, replica_groups=mesh['z'=8,'y'=4,'x'=4,'c'=2] {'z','y'}, dimensions={0} | all-to-all | bytes 425984 | tf_op jit(solution)/shard_map/all_to_all | solution.py:407
  39.3 2.6 %collective-permute-start.2 = (f32[32,1664]{1,0:T(8,128)S(1)}, f32[32,1664]{1,0:T(8,128)S(1)}, u32[]{:S(2)}, u32[]{:S(2)}) collective-permute-start(f32[32,1664]{1,0:T(8,128)S(1)} %bitcast.13), channel_id=1, source_target_pairs={{0,6},{2,0},{4,2},{6,4},{1,7},{3,1},{5,3},{7,5},{8,14},{10,8},{12,... | collective-permute-start | bytes 638984 | tf_op jit(solution)/shard_map/ppermute | solution.py:27
  41.9 0.5 collective-permute-start.1
  42.4 0.6 collective-permute-start
  43.0 4.0 %collective-permute-start.3 = (f32[32,1664]{1,0:T(8,128)S(1)}, f32[32,1664]{1,0:T(8,128)S(1)}, u32[]{:S(2)}, u32[]{:S(2)}) collective-permute-start(f32[32,1664]{1,0:T(8,128)S(1)} %bitcast.16), channel_id=1, source_target_pairs={{0,1},{1,0},{2,3},{3,2},{4,5},{5,4},{6,7},{7,6},{8,9},{9,8},{10,11... | collective-permute-start | bytes 638984 | tf_op jit(solution)/shard_map/ppermute | solution.py:27
  47.0 1.0 copy-done
  48.0 6.1 %decode.1 = (bf16[1664,2048]{1,0:T(8,128)(2,1)}, f32[8,128]{1,0:T(8,128)S(1)}) custom-call(bf16[1664,2048]{1,0:T(8,128)(2,1)} %codes.1, bf16[104,2048]{1,0:T(8,128)(2,1)S(1)} %copy-done, f32[32,1664]{1,0:T(8,128)S(1)} %bitcast.17), custom_call_target="tpu_custom_call" | custom-call | flops 3407872 | bytes 14680064 | tf_op jit(solution)/shard_map/decode/pallas_call | solution.py:132
  54.1 0.0 collective-permute-done.2.block
  54.1 0.1 collective-permute-start.6
  54.2 0.0 collective-permute-done.1.block
  54.3 0.6 collective-permute-start.5
  54.8 0.0 collective-permute-done.block
  54.9 0.9 collective-permute-start.4
  55.7 0.1 pad_add_fusion.place
  55.8 0.0 collective-permute-done.3.refs_4_.refs_0_
  55.8 0.0 collective-permute-done.6.refs_7_.refs_3_
  55.8 0.2 collective-permute-done.5.refs_6_.refs_2_
  56.0 0.8 collective-permute-done.4.refs_5_.refs_1_
  56.8 4.9 %product.1 = (f32[32,2176]{1,0:T(8,128)S(1)}, f32[32,2176]{1,0:T(8,128)S(1)}, f32[32,2176]{1,0:T(8,128)S(1)}, f32[32,2176]{1,0:T(8,128)S(1)}, f32[32,2176]{1,0:T...) custom-call(s32[4]{0:T(128)S(1)} %pad_add_fusion.place, ...), custom_call_target="tpu_custom_call" | custom-call | tf_op jit(solution)/shard_map/product/pallas_call | solution.py:194
  61.8 0.1 collective-permute-start.10
  61.9 2.7 %collective-permute-start.7 = (f32[32,2176]{1,0:T(8,128)S(1)}, f32[32,2176]{1,0:T(8,128)S(1)}, u32[]{:S(2)}, u32[]{:S(2)}) collective-permute-start(f32[32,2176]{1,0:T(8,128)S(1)} %get-tuple-element.36), channel_id=1, source_target_pairs={{0,24},{8,0},{16,8},{24,16},{1,25},{9,1},{17,9},{25,17},{2,26},{10... | collective-permute-start | bytes 835592 | tf_op jit(solution)/shard_map/ppermute | solution.py:27
  64.5 0.0 collective-permute-start.12
  64.6 6.4 %collective-permute-done.10.arrived = f32[32,2176]{1,0:T(8,128)S(1)} collective-permute-done((f32[32,2176]{1,0:T(8,128)S(1)}, f32[32,2176]{1,0:T(8,128)S(1)}, u32[]{:S(2)}, u32[]{:S(2)}) %collective-permute-start.10) | collective-permute-done | bytes 278560 | tf_op jit(solution)/shard_map/ppermute | solution.py:27
  71.0 0.1 collective-permute-start.11
  71.1 0.3 collective-permute-start.8
  71.3 0.0 collective-permute-done.7.arrived
  71.4 2.7 %collective-permute-start.9 = (f32[32,2176]{1,0:T(8,128)S(1)}, f32[32,2176]{1,0:T(8,128)S(1)}, u32[]{:S(2)}, u32[]{:S(2)}) collective-permute-start(f32[32,2176]{1,0:T(8,128)S(1)} %relay.2.refs_4_), channel_id=1, source_target_pairs={{0,24},{8,0},{16,8},{24,16},{1,25},{9,1},{17,9},{25,17},{2,26},{10... | collective-permute-start | bytes 835592 | tf_op jit(solution)/shard_map/ppermute | solution.py:27
  74.1 2.8 %mine_blocks.1 = (f32[128,104]{1,0:T(8,128)S(1)}, f32[128,1664]{1,0:T(8,128)S(1)}) custom-call(f32[32,1664]{1,0:T(8,128)S(1)} %bitcast.19, f32[32,1664]{1,0:T(8,128)S(1)} %hand_on.3.refs_1_, f32[32,1664]{1,0:T(8,128)S(1)} %hand_on.4.refs_2_, f32[32,1664]{1,0:T(8,128)S(1)} %hand_on.5.refs_3_, f32[32,2176]{1,0:T(8,128)S(1)} %relay.2.refs_4_), custom_call_target="tpu_custom_call" | custom-call | tf_op jit(solution)/shard_map/mine_blocks/pallas_call | solution.py:337
  76.9 0.0 collective-permute-done.12.c
  76.9 2.3 %collective-permute-done.11.b = f32[32,2176]{1,0:T(8,128)S(1)} collective-permute-done((f32[32,2176]{1,0:T(8,128)S(1)}, f32[32,2176]{1,0:T(8,128)S(1)}, u32[]{:S(2)}, u32[]{:S(2)}) %collective-permute-start.11) | collective-permute-done | bytes 278560 | tf_op jit(solution)/shard_map/ppermute | solution.py:27
  79.2 1.3 %collective-permute-start.13 = (f32[8,2176]{1,0:T(8,128)S(1)}, f32[8,2176]{1,0:T(8,128)S(1)}, u32[]{:S(2)}, u32[]{:S(2)}) collective-permute-start(f32[8,2176]{1,0:T(8,128)S(1)} %get-tuple-element.48), channel_id=1, source_target_pairs={{0,128},{32,160},{64,192},{96,224},{128,0},{160,32},{192,64},{224,... | collective-permute-start | bytes 208904 | tf_op jit(solution)/shard_map/ppermute | solution.py:27
  80.5 2.3 %collective-permute-start.14 = (f32[8,2176]{1,0:T(8,128)S(1)}, f32[8,2176]{1,0:T(8,128)S(1)}, u32[]{:S(2)}, u32[]{:S(2)}) collective-permute-start(f32[8,2176]{1,0:T(8,128)S(1)} %get-tuple-element.49), channel_id=1, source_target_pairs={{0,96},{32,128},{64,160},{96,192},{128,224},{160,0},{192,32},{224,... | collective-permute-start | bytes 208904 | tf_op jit(solution)/shard_map/ppermute | solution.py:27
  82.8 2.2 %collective-permute-start.15 = (f32[8,2176]{1,0:T(8,128)S(1)}, f32[8,2176]{1,0:T(8,128)S(1)}, u32[]{:S(2)}, u32[]{:S(2)}) collective-permute-start(f32[8,2176]{1,0:T(8,128)S(1)} %get-tuple-element.50), channel_id=1, source_target_pairs={{0,160},{32,192},{64,224},{96,0},{128,32},{160,64},{192,96},{224,1... | collective-permute-start | bytes 208904 | tf_op jit(solution)/shard_map/ppermute | solution.py:27
  85.0 0.2 collective-permute-done.8.b
  85.2 1.3 %collective-permute-start.16 = (f32[8,2176]{1,0:T(8,128)S(1)}, f32[8,2176]{1,0:T(8,128)S(1)}, u32[]{:S(2)}, u32[]{:S(2)}) collective-permute-start(f32[8,2176]{1,0:T(8,128)S(1)} %get-tuple-element.51), channel_id=1, source_target_pairs={{0,64},{32,96},{64,128},{96,160},{128,192},{160,224},{192,0},{224,... | collective-permute-start | bytes 208904 | tf_op jit(solution)/shard_map/ppermute | solution.py:27
  86.5 0.0 collective-permute-done.9.c
  86.6 2.3 %collective-permute-start.17 = (f32[8,2176]{1,0:T(8,128)S(1)}, f32[8,2176]{1,0:T(8,128)S(1)}, u32[]{:S(2)}, u32[]{:S(2)}) collective-permute-start(f32[8,2176]{1,0:T(8,128)S(1)} %get-tuple-element.41.refs_5_), channel_id=1, source_target_pairs={{0,192},{32,224},{64,0},{96,32},{128,64},{160,96},{192,128},{224,1... | collective-permute-start | bytes 208904 | tf_op jit(solution)/shard_map/ppermute | solution.py:27
  88.9 0.0 collective-permute-done.13.refs_0_
  88.9 0.7 collective-permute-start.18
  89.6 0.0 collective-permute-done.14.refs_1_
  89.6 2.0 %collective-permute-start.19 = (f32[8,2176]{1,0:T(8,128)S(1)}, f32[8,2176]{1,0:T(8,128)S(1)}, u32[]{:S(2)}, u32[]{:S(2)}) collective-permute-start(f32[8,2176]{1,0:T(8,128)S(1)} %get-tuple-element.53), channel_id=1, source_target_pairs={{0,224},{32,0},{64,32},{96,64},{128,96},{160,128},{192,160},{224,1... | collective-permute-start | bytes 208904 | tf_op jit(solution)/shard_map/ppermute | solution.py:27
  92.2 3.4 %theirs_blocks.1 = (f32[104,256]{1,0:T(8,128)S(1)}, f32[128,1664]{1,0:T(8,128)S(1)}) custom-call(s32[4]{0:T(128)S(1)} %pad_add_fusion.place, f32[32,1664]{1,0:T(8,128)S(1)} %collective-permute-done.3.refs_4_.refs_0_, f32[32,1664]{1,0:T(8,128)S(1)} %collective-permute-done.4.refs_5_.refs_1_, f32[32,1664]{1,0:T(8,128)S(1)} %collective-permute-done.5.refs_6_.refs_2_, ...), custom_call_target="tpu_custom_call" | custom-call | tf_op jit(solution)/shard_map/theirs_blocks/pallas_call | solution.py:352
  95.6 0.0 collective-permute-done.15.refs_2_
  95.7 0.0 collective-permute-done.16.refs_3_
  95.7 0.0 collective-permute-done.17.refs_4_
  95.7 0.6 collective-permute-done.18.refs_5_
  96.3 0.0 collective-permute-done.19.refs_6_
  96.3 0.7 z_sum.1
  97.0 5.1 %collective-permute-start.20 = (f32[8,128]{1,0:T(8,128)S(1)}, f32[8,128]{1,0:T(8,128)S(1)}, u32[]{:S(2)}, u32[]{:S(2)}) collective-permute-start(f32[8,128]{1,0:T(8,128)S(1)} %get-tuple-element.60), channel_id=1, source_target_pairs={{0,1},{1,0},{2,3},{3,2},{4,5},{5,4},{6,7},{7,6},{8,9},{9,8},{10,11... | collective-permute-start | bytes 12296 | tf_op jit(solution)/shard_map/ppermute | solution.py:27
  102.0 0.8 collective-permute-done.20
  102.8 0.7 collective-permute-start.21
  103.5 1.7 %collective-permute-start.22 = (f32[8,128]{1,0:T(8,128)S(1)}, f32[8,128]{1,0:T(8,128)S(1)}, u32[]{:S(2)}, u32[]{:S(2)}) collective-permute-start(f32[8,128]{1,0:T(8,128)S(1)} %add.20.a), channel_id=1, source_target_pairs={{0,4},{2,6},{4,0},{6,2},{1,5},{3,7},{5,1},{7,3},{8,12},{10,14},{12... | collective-permute-start | bytes 12296 | tf_op jit(solution)/shard_map/ppermute | solution.py:27
  105.2 0.7 collective-permute-start.23
  105.9 1.7 %encode.1 = (bf16[256,1664]{1,0:T(8,128)(2,1)}, f32[104,256]{1,0:T(8,128)}, f32[8,128]{1,0:T(8,128)S(1)}) custom-call(s32[4]{0:T(128)S(1)} %pad_add_fusion.place, f32[32,1664]{1,0:T(8,128)S(1)} %bitcast.20, f32[32,1664]{1,0:T(8,128)S(1)} %hand_on.3.refs_1_, f32[32,1664]{1,0:T(8,128)S(1)} %hand_on.4.refs_2_, f32[32,1664]{1,0:T(8,128)S(1)} %hand_on.5.refs_3_, ...), custom_call_target="tpu_custom_call" | custom-call | tf_op jit(solution)/shard_map/encode/pallas_call | solution.py:385
  107.7 0.0 collective-permute-done.21.b
  107.7 0.0 collective-permute-done.22.c
  107.7 0.3 collective-permute-done.23.d
  108.0 0.7 norm.1
  (16 shorter events, 0.2 us)
Async XLA Ops:
  39.3 14.8 %collective-permute-start.2 = (f32[32,1664]{1,0:T(8,128)S(1)}, f32[32,1664]{1,0:T(8,128)S(1)}, u32[]{:S(2)}, u32[]{:S(2)}) collective-permute-start(f32[32,1664]{1,0:T(8,128)S(1)} %bitcast.13), channel_id=1, source_target_pairs={{0,6},{2,0},{4,2},{6,4},{1,7},{3,1},{5,3},{7,5},{8,14},{10,8},{12,... | collective-permute-start | bytes 638984 | tf_op jit(solution)/shard_map/ppermute | solution.py:27
  41.9 12.3 %collective-permute-start.1 = (f32[32,1664]{1,0:T(8,128)S(1)}, f32[32,1664]{1,0:T(8,128)S(1)}, u32[]{:S(2)}, u32[]{:S(2)}) collective-permute-start(f32[32,1664]{1,0:T(8,128)S(1)} %bitcast.14), channel_id=1, source_target_pairs={{0,4},{2,6},{4,0},{6,2},{1,5},{3,7},{5,1},{7,3},{8,12},{10,14},{12... | collective-permute-start | bytes 638984 | tf_op jit(solution)/shard_map/ppermute | solution.py:27
  42.4 12.4 %collective-permute-start = (f32[32,1664]{1,0:T(8,128)S(1)}, f32[32,1664]{1,0:T(8,128)S(1)}, u32[]{:S(2)}, u32[]{:S(2)}) collective-permute-start(f32[32,1664]{1,0:T(8,128)S(1)} %bitcast.15), channel_id=1, source_target_pairs={{0,2},{2,4},{4,6},{6,0},{1,3},{3,5},{5,7},{7,1},{8,10},{10,12},{12... | collective-permute-start | bytes 638984 | tf_op jit(solution)/shard_map/ppermute | solution.py:27
  43.0 12.8 %collective-permute-start.3 = (f32[32,1664]{1,0:T(8,128)S(1)}, f32[32,1664]{1,0:T(8,128)S(1)}, u32[]{:S(2)}, u32[]{:S(2)}) collective-permute-start(f32[32,1664]{1,0:T(8,128)S(1)} %bitcast.16), channel_id=1, source_target_pairs={{0,1},{1,0},{2,3},{3,2},{4,5},{5,4},{6,7},{7,6},{8,9},{9,8},{10,11... | collective-permute-start | bytes 638984 | tf_op jit(solution)/shard_map/ppermute | solution.py:27
  47.0 1.0 copy-start
  54.1 1.7 %collective-permute-start.6 = (f32[32,1664]{1,0:T(8,128)S(1)}, f32[32,1664]{1,0:T(8,128)S(1)}, u32[]{:S(2)}, u32[]{:S(2)}) collective-permute-start(f32[32,1664]{1,0:T(8,128)S(1)} %hand_on.5.refs_3_), channel_id=1, source_target_pairs={{0,1},{1,0},{2,3},{3,2},{4,5},{5,4},{6,7},{7,6},{8,9},{9,8},{10,11... | collective-permute-start | bytes 638984 | tf_op jit(solution)/shard_map/ppermute | solution.py:27
  54.3 1.7 %collective-permute-start.5 = (f32[32,1664]{1,0:T(8,128)S(1)}, f32[32,1664]{1,0:T(8,128)S(1)}, u32[]{:S(2)}, u32[]{:S(2)}) collective-permute-start(f32[32,1664]{1,0:T(8,128)S(1)} %hand_on.4.refs_2_), channel_id=1, source_target_pairs={{0,1},{1,0},{2,3},{3,2},{4,5},{5,4},{6,7},{7,6},{8,9},{9,8},{10,11... | collective-permute-start | bytes 638984 | tf_op jit(solution)/shard_map/ppermute | solution.py:27
  54.9 2.0 %collective-permute-start.4 = (f32[32,1664]{1,0:T(8,128)S(1)}, f32[32,1664]{1,0:T(8,128)S(1)}, u32[]{:S(2)}, u32[]{:S(2)}) collective-permute-start(f32[32,1664]{1,0:T(8,128)S(1)} %hand_on.3.refs_1_), channel_id=1, source_target_pairs={{0,1},{1,0},{2,3},{3,2},{4,5},{5,4},{6,7},{7,6},{8,9},{9,8},{10,11... | collective-permute-start | bytes 638984 | tf_op jit(solution)/shard_map/ppermute | solution.py:27
  56.8 39.5 %copy-start.1 = (bf16[8,2048]{1,0:T(8,128)(2,1)S(1)}, bf16[8,2048]{1,0:T(8,128)(2,1)}, u32[]{:S(2)}) copy-start(bf16[8,2048]{1,0:T(8,128)(2,1)} %refs_8_.1) | copy-start | bytes 98308
  56.8 49.1 %copy-start.2 = (bf16[2048]{0:T(1024)(128)(2,1)S(1)}, bf16[2048]{0:T(1024)(128)(2,1)}, u32[]{:S(2)}) copy-start(bf16[2048]{0:T(1024)(128)(2,1)} %param.13) | copy-start | bytes 12292
  61.8 9.2 %collective-permute-start.10 = (f32[32,2176]{1,0:T(8,128)S(1)}, f32[32,2176]{1,0:T(8,128)S(1)}, u32[]{:S(2)}, u32[]{:S(2)}) collective-permute-start(f32[32,2176]{1,0:T(8,128)S(1)} %get-tuple-element.46), channel_id=1, source_target_pairs={{0,8},{8,16},{16,24},{24,0},{1,9},{9,17},{17,25},{25,1},{2,10},{10... | collective-permute-start | bytes 835592 | tf_op jit(solution)/shard_map/ppermute | solution.py:27
  61.9 9.5 %collective-permute-start.7 = (f32[32,2176]{1,0:T(8,128)S(1)}, f32[32,2176]{1,0:T(8,128)S(1)}, u32[]{:S(2)}, u32[]{:S(2)}) collective-permute-start(f32[32,2176]{1,0:T(8,128)S(1)} %get-tuple-element.36), channel_id=1, source_target_pairs={{0,24},{8,0},{16,8},{24,16},{1,25},{9,1},{17,9},{25,17},{2,26},{10... | collective-permute-start | bytes 835592 | tf_op jit(solution)/shard_map/ppermute | solution.py:27
  64.5 12.4 %collective-permute-start.12 = (f32[32,2176]{1,0:T(8,128)S(1)}, f32[32,2176]{1,0:T(8,128)S(1)}, u32[]{:S(2)}, u32[]{:S(2)}) collective-permute-start(f32[32,2176]{1,0:T(8,128)S(1)} %get-tuple-element.47), channel_id=1, source_target_pairs={{0,24},{8,0},{16,8},{24,16},{1,25},{9,1},{17,9},{25,17},{2,26},{10... | collective-permute-start | bytes 835592 | tf_op jit(solution)/shard_map/ppermute | solution.py:27
  71.0 8.2 %collective-permute-start.11 = (f32[32,2176]{1,0:T(8,128)S(1)}, f32[32,2176]{1,0:T(8,128)S(1)}, u32[]{:S(2)}, u32[]{:S(2)}) collective-permute-start(f32[32,2176]{1,0:T(8,128)S(1)} %relay.3), channel_id=1, source_target_pairs={{0,8},{8,16},{16,24},{24,0},{1,9},{9,17},{17,25},{25,1},{2,10},{10... | collective-permute-start | bytes 835592 | tf_op jit(solution)/shard_map/ppermute | solution.py:27
  71.1 14.1 %collective-permute-start.8 = (f32[32,2176]{1,0:T(8,128)S(1)}, f32[32,2176]{1,0:T(8,128)S(1)}, u32[]{:S(2)}, u32[]{:S(2)}) collective-permute-start(f32[32,2176]{1,0:T(8,128)S(1)} %get-tuple-element.40), channel_id=1, source_target_pairs={{0,8},{8,16},{16,24},{24,0},{1,9},{9,17},{17,25},{25,1},{2,10},{10... | collective-permute-start | bytes 835592 | tf_op jit(solution)/shard_map/ppermute | solution.py:27
  71.4 15.1 %collective-permute-start.9 = (f32[32,2176]{1,0:T(8,128)S(1)}, f32[32,2176]{1,0:T(8,128)S(1)}, u32[]{:S(2)}, u32[]{:S(2)}) collective-permute-start(f32[32,2176]{1,0:T(8,128)S(1)} %relay.2.refs_4_), channel_id=1, source_target_pairs={{0,24},{8,0},{16,8},{24,16},{1,25},{9,1},{17,9},{25,17},{2,26},{10... | collective-permute-start | bytes 835592 | tf_op jit(solution)/shard_map/ppermute | solution.py:27
  79.2 9.6 %collective-permute-start.13 = (f32[8,2176]{1,0:T(8,128)S(1)}, f32[8,2176]{1,0:T(8,128)S(1)}, u32[]{:S(2)}, u32[]{:S(2)}) collective-permute-start(f32[8,2176]{1,0:T(8,128)S(1)} %get-tuple-element.48), channel_id=1, source_target_pairs={{0,128},{32,160},{64,192},{96,224},{128,0},{160,32},{192,64},{224,... | collective-permute-start | bytes 208904 | tf_op jit(solution)/shard_map/ppermute | solution.py:27
  80.5 9.1 %collective-permute-start.14 = (f32[8,2176]{1,0:T(8,128)S(1)}, f32[8,2176]{1,0:T(8,128)S(1)}, u32[]{:S(2)}, u32[]{:S(2)}) collective-permute-start(f32[8,2176]{1,0:T(8,128)S(1)} %get-tuple-element.49), channel_id=1, source_target_pairs={{0,96},{32,128},{64,160},{96,192},{128,224},{160,0},{192,32},{224,... | collective-permute-start | bytes 208904 | tf_op jit(solution)/shard_map/ppermute | solution.py:27
  82.8 12.8 %collective-permute-start.15 = (f32[8,2176]{1,0:T(8,128)S(1)}, f32[8,2176]{1,0:T(8,128)S(1)}, u32[]{:S(2)}, u32[]{:S(2)}) collective-permute-start(f32[8,2176]{1,0:T(8,128)S(1)} %get-tuple-element.50), channel_id=1, source_target_pairs={{0,160},{32,192},{64,224},{96,0},{128,32},{160,64},{192,96},{224,1... | collective-permute-start | bytes 208904 | tf_op jit(solution)/shard_map/ppermute | solution.py:27
  85.2 10.5 %collective-permute-start.16 = (f32[8,2176]{1,0:T(8,128)S(1)}, f32[8,2176]{1,0:T(8,128)S(1)}, u32[]{:S(2)}, u32[]{:S(2)}) collective-permute-start(f32[8,2176]{1,0:T(8,128)S(1)} %get-tuple-element.51), channel_id=1, source_target_pairs={{0,64},{32,96},{64,128},{96,160},{128,192},{160,224},{192,0},{224,... | collective-permute-start | bytes 208904 | tf_op jit(solution)/shard_map/ppermute | solution.py:27
  86.6 9.1 %collective-permute-start.17 = (f32[8,2176]{1,0:T(8,128)S(1)}, f32[8,2176]{1,0:T(8,128)S(1)}, u32[]{:S(2)}, u32[]{:S(2)}) collective-permute-start(f32[8,2176]{1,0:T(8,128)S(1)} %get-tuple-element.41.refs_5_), channel_id=1, source_target_pairs={{0,192},{32,224},{64,0},{96,32},{128,64},{160,96},{192,128},{224,1... | collective-permute-start | bytes 208904 | tf_op jit(solution)/shard_map/ppermute | solution.py:27
  88.9 7.4 %collective-permute-start.18 = (f32[8,2176]{1,0:T(8,128)S(1)}, f32[8,2176]{1,0:T(8,128)S(1)}, u32[]{:S(2)}, u32[]{:S(2)}) collective-permute-start(f32[8,2176]{1,0:T(8,128)S(1)} %get-tuple-element.52), channel_id=1, source_target_pairs={{0,32},{32,64},{64,96},{96,128},{128,160},{160,192},{192,224},{224... | collective-permute-start | bytes 208904 | tf_op jit(solution)/shard_map/ppermute | solution.py:27
  89.6 6.7 %collective-permute-start.19 = (f32[8,2176]{1,0:T(8,128)S(1)}, f32[8,2176]{1,0:T(8,128)S(1)}, u32[]{:S(2)}, u32[]{:S(2)}) collective-permute-start(f32[8,2176]{1,0:T(8,128)S(1)} %get-tuple-element.53), channel_id=1, source_target_pairs={{0,224},{32,0},{64,32},{96,64},{128,96},{160,128},{192,160},{224,1... | collective-permute-start | bytes 208904 | tf_op jit(solution)/shard_map/ppermute | solution.py:27
  97.0 5.9 %collective-permute-start.20 = (f32[8,128]{1,0:T(8,128)S(1)}, f32[8,128]{1,0:T(8,128)S(1)}, u32[]{:S(2)}, u32[]{:S(2)}) collective-permute-start(f32[8,128]{1,0:T(8,128)S(1)} %get-tuple-element.60), channel_id=1, source_target_pairs={{0,1},{1,0},{2,3},{3,2},{4,5},{5,4},{6,7},{7,6},{8,9},{9,8},{10,11... | collective-permute-start | bytes 12296 | tf_op jit(solution)/shard_map/ppermute | solution.py:27
  102.8 4.8 %collective-permute-start.21 = (f32[8,128]{1,0:T(8,128)S(1)}, f32[8,128]{1,0:T(8,128)S(1)}, u32[]{:S(2)}, u32[]{:S(2)}) collective-permute-start(f32[8,128]{1,0:T(8,128)S(1)} %add.20.a), channel_id=1, source_target_pairs={{0,2},{2,4},{4,6},{6,0},{1,3},{3,5},{5,7},{7,1},{8,10},{10,12},{12... | collective-permute-start | bytes 12296 | tf_op jit(solution)/shard_map/ppermute | solution.py:27
  103.5 4.2 %collective-permute-start.22 = (f32[8,128]{1,0:T(8,128)S(1)}, f32[8,128]{1,0:T(8,128)S(1)}, u32[]{:S(2)}, u32[]{:S(2)}) collective-permute-start(f32[8,128]{1,0:T(8,128)S(1)} %add.20.a), channel_id=1, source_target_pairs={{0,4},{2,6},{4,0},{6,2},{1,5},{3,7},{5,1},{7,3},{8,12},{10,14},{12... | collective-permute-start | bytes 12296 | tf_op jit(solution)/shard_map/ppermute | solution.py:27
  105.2 2.8 %collective-permute-start.23 = (f32[8,128]{1,0:T(8,128)S(1)}, f32[8,128]{1,0:T(8,128)S(1)}, u32[]{:S(2)}, u32[]{:S(2)}) collective-permute-start(f32[8,128]{1,0:T(8,128)S(1)} %add.20.a), channel_id=1, source_target_pairs={{0,6},{2,0},{4,2},{6,4},{1,7},{3,1},{5,3},{7,5},{8,14},{10,8},{12,... | collective-permute-start | bytes 12296 | tf_op jit(solution)/shard_map/ppermute | solution.py:27

commit v4 on v3

--- a/solution.py
+++ b/solution.py
@@ -153,7 +153,7 @@
 BN = 512
 TILES = COLS // BN
 HALF = 32
-Z_ORDER = (4, 3, 5, 2, 6, 1, 7, 0)
+Z_ORDER = (6, 1, 7, 0, 4, 3, 5, 2)
 
 
 def product_kernel(place, *refs):
@@ -207,20 +207,20 @@
     )(place, *slabs, weight)
 
 
-def relay_kernel(own, arrived, out):
+def relay_kernel(own, arrived, after, out):
     out[:, :COLS] = own[:, :COLS] + arrived[:, :COLS]
     out[:, COLS:] = jnp.maximum(own[:, COLS:], arrived[:, COLS:])
 
 
-def relay(own, arrived):
+def relay(own, arrived, after):
     return pl.pallas_call(
         relay_kernel,
-        in_specs=[VMEM] * 2,
+        in_specs=[VMEM] * 2 + [ANY],
         out_specs=VMEM,
         out_shape=jax.ShapeDtypeStruct((HALF, WIDE), jnp.float32),
         compiler_params=PARAMS,
         name="relay",
-    )(own, arrived)
+    )(own, arrived, after)
 
 
 def y_sum_kernel(a, b, c, after, *outs):
@@ -243,7 +243,7 @@
 
 
 def z_sum_kernel(*refs):
-    parts, residual, scale, after, summed, rounded, squares, top = refs[:NZ], *refs[NZ:]
+    parts, residual, scale, summed, rounded, squares, top = refs[:NZ], *refs[NZ:]
     total = parts[0][:, :COLS]
     peak = parts[0][:, COLS:]
     for part in parts[1:]:
@@ -256,10 +256,10 @@
     top[...] = peak
 
 
-def z_sum(parts, residual, weight_scale, after):
+def z_sum(parts, residual, weight_scale):
     return pl.pallas_call(
         z_sum_kernel,
-        in_specs=[VMEM] * (NZ + 1) + [SMEM, ANY],
+        in_specs=[VMEM] * (NZ + 1) + [SMEM],
         out_specs=[VMEM] * 4,
         out_shape=[
             jax.ShapeDtypeStruct((OWN, COLS), jnp.float32),
@@ -269,7 +269,7 @@
         ],
         compiler_params=PARAMS,
         name="z_sum",
-    )(*parts, residual, weight_scale, after)
+    )(*parts, residual, weight_scale)
 
 
 def norm_kernel(summed, a, b, c, d, gain, after, out):
@@ -408,20 +408,20 @@
 
     mine = [moved(own, "x", k) for k in (1, 2, 3)]
     weight, done = decode(down_codes, down_scales, own)
-    mine = [own] + [hand_on(block, done) for block in mine]
+    mine = [hand_on(block, done) for block in [own] + mine]
     theirs = [moved(block, "c", 1) for block in mine]
     slabs = mine + theirs
     here_a, here_b, ahead_a, ahead_b, far_a, far_b, behind_a, behind_b = product(slabs, weight, place)
     first, second = moved(far_a, "y", 1), moved(far_b, "y", -1)
     ahead_b, behind_a = moved(ahead_b, "y", 1), moved(behind_a, "y", -1)
-    ahead_a, behind_b = relay(ahead_a, first), relay(behind_b, second)
-    mine_most, mine_factor = mine_blocks(mine, behind_b)
-    sums_a = y_sum(here_a, moved(ahead_a, "y", 1), behind_a, mine_most)
-    sums_b = y_sum(here_b, ahead_b, moved(behind_b, "y", -1), mine_most)
+    mine_most, mine_factor = mine_blocks(mine, here_a)
+    ahead_a, behind_b = relay(ahead_a, first, mine_most), relay(behind_b, second, mine_most)
+    narrow, theirs_factor = theirs_blocks(place, theirs, mine_most, behind_b)
+    sums_a = y_sum(here_a, moved(ahead_a, "y", 1), behind_a, narrow)
+    sums_b = y_sum(here_b, ahead_b, moved(behind_b, "y", -1), narrow)
     sums = [*sums_a, *sums_b]
     parts = [moved(part, "z", step) if step else part for part, step in zip(sums, Z_ORDER)]
-    narrow, theirs_factor = theirs_blocks(place, theirs, mine_most, sums_b[0])
-    summed, rounded, squares, peak = z_sum(parts, residual, weight_scale, narrow)
+    summed, rounded, squares, peak = z_sum(parts, residual, weight_scale)
     squares = squares + moved(squares, "c", 1)
     others = [moved(squares, "x", 1), moved(squares, "x", 2), moved(squares, "x", 3)]
     payload, block_scales, done = encode(

time: 109 us -> 106 us (0.972)
  starting transfers between devices: 35.2 us -> 32.6 us
    ppermute x24, starting transfers between devices: 35.2 us -> 32.6 us  [moved(): lax.ppermute(block, axis, [(i, (i + step) % count) for i in range(count)])]
  transfers between devices with their start and end apart: 24 -> 24, of which waited for: 8 -> 10; matrix products, arithmetic and copies ran while one was open for 0% -> 0% of each run, Pallas kernels for 13% -> 14%
where the time goes in v4:
time: 106 us; the launch traced here: 105 us
  blocking collectives  36.6 us (35%)
  starting transfers between devices  32.6 us (31%)
  Pallas kernels  21.1 us (20%)
  waiting for transfers between devices  10.7 us (10%)
  local copies, waits for them, and re-layouts  1.5 us (1%)
  between operations  1.43 us (1%)
  other arithmetic  1.1 us (1%)
    ppermute x24, starting transfers between devices, moved(): lax.ppermute(block, axis, [(i, (i + step) % count) for i in range(count)])  32.6 us
    all_to_all x1, blocking collectives, on_device(): one_row = lax.all_to_all(inner, ('z', 'y'), 0, 0, tiled=True)  21.9 us
    all_to_all x1, blocking collectives, on_device(): own = lax.all_to_all(turned, ('z', 'y'), 0, 0, tiled=True)  14.6 us
    ppermute x24, waiting for transfers between devices, moved(): lax.ppermute(block, axis, [(i, (i + step) % count) for i in range(count)])  10.7 us
    pallas_call x1, Pallas kernels, decode(): pl.pallas_call(decode_kernel, in_specs=[HBM, HBM, ANY], out_specs=[HBM, V...  6.08 us
    pallas_call x1, Pallas kernels, product(): pl.pallas_call(product_kernel, in_specs=[SMEM] + [VMEM] * 8 + [HBM], out_...  4.93 us
    pallas_call x1, Pallas kernels, theirs_blocks(): pl.pallas_call(theirs_kernel, in_specs=[SMEM] + [VMEM] * 5 + [ANY], out_s...  3.43 us
    pallas_call x1, Pallas kernels, mine_blocks(): pl.pallas_call(mine_kernel, in_specs=[VMEM] * 4 + [ANY], out_specs=[VMEM]...  2.8 us
  transfers between devices with their start and end apart: 24, of which 10 were waited for; matrix products, arithmetic and copies ran while one was open for 0% of the time, Pallas kernels for 14%

profile of v4, /device:TPU:1, one launch (start us, length us, event | category | flops | bytes accessed | tf_op | source)
XLA Modules:
  0.0 105.1 jit_solution(16254133381324019274)
XLA Ops:
  0.6 1.0 fusion.3.hidden
  1.7 0.2 inner_transform.1
  1.9 0.2 copy.11
  2.1 21.9 %all_to_all.22 = f32[32,1,1664]{2,1,0:T(1,128)S(1)} all-to-all(f32[32,1,1664]{2,1,0:T(1,128)S(1)} %copy.11), channel_id=1, replica_groups=mesh['z'=8,'y'=4,'x'=4,'c'=2] {'z','y'}, dimensions={0} | all-to-all | bytes 425984 | tf_op jit(solution)/shard_map/all_to_all | solution.py:405
  24.1 0.3 outer_transform.1
  24.4 0.2 copy.12
  24.7 14.6 %all_to_all.23 = f32[32,1,1664]{2,1,0:T(1,128)S(1)} all-to-all(f32[32,1,1664]{2,1,0:T(1,128)S(1)} %copy.12), channel_id=1, replica_groups=mesh['z'=8,'y'=4,'x'=4,'c'=2] {'z','y'}, dimensions={0} | all-to-all | bytes 425984 | tf_op jit(solution)/shard_map/all_to_all | solution.py:407
  39.3 2.6 %collective-permute-start.2 = (f32[32,1664]{1,0:T(8,128)S(1)}, f32[32,1664]{1,0:T(8,128)S(1)}, u32[]{:S(2)}, u32[]{:S(2)}) collective-permute-start(f32[32,1664]{1,0:T(8,128)S(1)} %bitcast.13), channel_id=1, source_target_pairs={{0,6},{2,0},{4,2},{6,4},{1,7},{3,1},{5,3},{7,5},{8,14},{10,8},{12,... | collective-permute-start | bytes 638984 | tf_op jit(solution)/shard_map/ppermute | solution.py:27
  41.9 0.5 collective-permute-start.1
  42.4 0.6 collective-permute-start
  43.0 1.0 copy-done
  44.0 6.1 %decode.1 = (bf16[1664,2048]{1,0:T(8,128)(2,1)}, f32[8,128]{1,0:T(8,128)S(1)}) custom-call(bf16[1664,2048]{1,0:T(8,128)(2,1)} %codes.1, bf16[104,2048]{1,0:T(8,128)(2,1)S(1)} %copy-done, f32[32,1664]{1,0:T(8,128)S(1)} %bitcast.16), custom_call_target="tpu_custom_call" | custom-call | flops 3407872 | bytes 14680064 | tf_op jit(solution)/shard_map/decode/pallas_call | solution.py:132
  50.1 4.1 %collective-permute-start.3 = (f32[32,1664]{1,0:T(8,128)S(1)}, f32[32,1664]{1,0:T(8,128)S(1)}, u32[]{:S(2)}, u32[]{:S(2)}) collective-permute-start(f32[32,1664]{1,0:T(8,128)S(1)} %hand_on.4.refs_0_), channel_id=1, source_target_pairs={{0,1},{1,0},{2,3},{3,2},{4,5},{5,4},{6,7},{7,6},{8,9},{9,8},{10,11... | collective-permute-start | bytes 638984 | tf_op jit(solution)/shard_map/ppermute | solution.py:27
  54.2 0.0 collective-permute-done.2.block
  54.2 0.1 collective-permute-start.6
  54.3 0.0 collective-permute-done.1.block
  54.4 0.6 collective-permute-start.5
  54.9 0.0 collective-permute-done.block
  55.0 0.8 collective-permute-start.4
  55.7 0.1 pad_add_fusion.place
  55.8 0.0 collective-permute-done.3.refs_4_.refs_0_
  55.8 0.0 collective-permute-done.6.refs_7_.refs_3_
  55.8 0.3 collective-permute-done.5.refs_6_.refs_2_
  56.1 0.7 collective-permute-done.4.refs_5_.refs_1_
  56.8 4.9 %product.1 = (f32[32,2176]{1,0:T(8,128)S(1)}, f32[32,2176]{1,0:T(8,128)S(1)}, f32[32,2176]{1,0:T(8,128)S(1)}, f32[32,2176]{1,0:T(8,128)S(1)}, f32[32,2176]{1,0:T...) custom-call(s32[4]{0:T(128)S(1)} %pad_add_fusion.place, ...), custom_call_target="tpu_custom_call" | custom-call | tf_op jit(solution)/shard_map/product/pallas_call | solution.py:194
  61.8 1.3 %collective-permute-start.7 = (f32[32,2176]{1,0:T(8,128)S(1)}, f32[32,2176]{1,0:T(8,128)S(1)}, u32[]{:S(2)}, u32[]{:S(2)}) collective-permute-start(f32[32,2176]{1,0:T(8,128)S(1)} %get-tuple-element.39), channel_id=1, source_target_pairs={{0,24},{8,0},{16,8},{24,16},{1,25},{9,1},{17,9},{25,17},{2,26},{10... | collective-permute-start | bytes 835592 | tf_op jit(solution)/shard_map/ppermute | solution.py:27
  63.0 0.3 collective-permute-start.8
  63.3 2.8 %mine_blocks.1 = (f32[128,104]{1,0:T(8,128)S(1)}, f32[128,1664]{1,0:T(8,128)S(1)}) custom-call(f32[32,1664]{1,0:T(8,128)S(1)} %hand_on.4.refs_0_, f32[32,1664]{1,0:T(8,128)S(1)} %hand_on.5.refs_1_, f32[32,1664]{1,0:T(8,128)S(1)} %hand_on.6.refs_2_, f32[32,1664]{1,0:T(8,128)S(1)} %hand_on.7.refs_3_, f32[32,2176]{1,0:T(8,128)S(1)} %get-tuple-element.35.refs_4_.a), custom_call_target="tpu_custom_call" | custom-call | tf_op jit(solution)/shard_map/mine_blocks/pallas_call | solution.py:337
  66.1 0.1 collective-permute-start.14
  66.2 3.5 %collective-permute-done.7.arrived = f32[32,2176]{1,0:T(8,128)S(1)} collective-permute-done((f32[32,2176]{1,0:T(8,128)S(1)}, f32[32,2176]{1,0:T(8,128)S(1)}, u32[]{:S(2)}, u32[]{:S(2)}) %collective-permute-start.7) | collective-permute-done | bytes 278560 | tf_op jit(solution)/shard_map/ppermute | solution.py:27
  69.8 2.5 %collective-permute-start.15 = (f32[32,2176]{1,0:T(8,128)S(1)}, f32[32,2176]{1,0:T(8,128)S(1)}, u32[]{:S(2)}, u32[]{:S(2)}) collective-permute-start(f32[32,2176]{1,0:T(8,128)S(1)} %relay.2.refs_5_), channel_id=1, source_target_pairs={{0,24},{8,0},{16,8},{24,16},{1,25},{9,1},{17,9},{25,17},{2,26},{10... | collective-permute-start | bytes 835592 | tf_op jit(solution)/shard_map/ppermute | solution.py:27
  72.2 0.1 collective-permute-start.10
  72.3 0.0 collective-permute-done.8.arrived
  72.4 1.5 %collective-permute-start.9 = (f32[32,2176]{1,0:T(8,128)S(1)}, f32[32,2176]{1,0:T(8,128)S(1)}, u32[]{:S(2)}, u32[]{:S(2)}) collective-permute-start(f32[32,2176]{1,0:T(8,128)S(1)} %relay.3), channel_id=1, source_target_pairs={{0,8},{8,16},{16,24},{24,0},{1,9},{9,17},{17,25},{25,1},{2,10},{10... | collective-permute-start | bytes 835592 | tf_op jit(solution)/shard_map/ppermute | solution.py:27
  73.8 3.4 %theirs_blocks.1 = (f32[104,256]{1,0:T(8,128)S(1)}, f32[128,1664]{1,0:T(8,128)S(1)}) custom-call(s32[4]{0:T(128)S(1)} %pad_add_fusion.place, f32[32,1664]{1,0:T(8,128)S(1)} %collective-permute-done.3.refs_4_.refs_0_, f32[32,1664]{1,0:T(8,128)S(1)} %collective-permute-done.4.refs_5_.refs_1_, f32[32,1664]{1,0:T(8,128)S(1)} %collective-permute-done.5.refs_6_.refs_2_, ...), custom_call_target="tpu_custom_call" | custom-call | tf_op jit(solution)/shard_map/theirs_blocks/pallas_call | solution.py:352
  77.2 0.5 collective-permute-done.14.b
  77.8 0.0 collective-permute-done.15.c
  77.8 0.7 collective-permute-start.16
  78.5 2.3 %collective-permute-start.17 = (f32[8,2176]{1,0:T(8,128)S(1)}, f32[8,2176]{1,0:T(8,128)S(1)}, u32[]{:S(2)}, u32[]{:S(2)}) collective-permute-start(f32[8,2176]{1,0:T(8,128)S(1)} %get-tuple-element.52), channel_id=1, source_target_pairs={{0,96},{32,128},{64,160},{96,192},{128,224},{160,0},{192,32},{224,... | collective-permute-start | bytes 208904 | tf_op jit(solution)/shard_map/ppermute | solution.py:27
  80.8 2.2 %collective-permute-start.18 = (f32[8,2176]{1,0:T(8,128)S(1)}, f32[8,2176]{1,0:T(8,128)S(1)}, u32[]{:S(2)}, u32[]{:S(2)}) collective-permute-start(f32[8,2176]{1,0:T(8,128)S(1)} %get-tuple-element.53), channel_id=1, source_target_pairs={{0,160},{32,192},{64,224},{96,0},{128,32},{160,64},{192,96},{224,1... | collective-permute-start | bytes 208904 | tf_op jit(solution)/shard_map/ppermute | solution.py:27
  83.0 0.0 collective-permute-done.10.c
  83.0 2.1 %collective-permute-start.19 = (f32[8,2176]{1,0:T(8,128)S(1)}, f32[8,2176]{1,0:T(8,128)S(1)}, u32[]{:S(2)}, u32[]{:S(2)}) collective-permute-start(f32[8,2176]{1,0:T(8,128)S(1)} %get-tuple-element.54), channel_id=1, source_target_pairs={{0,64},{32,96},{64,128},{96,160},{128,192},{160,224},{192,0},{224,... | collective-permute-start | bytes 208904 | tf_op jit(solution)/shard_map/ppermute | solution.py:27
  85.1 0.0 collective-permute-done.9.b
  85.1 0.1 y_sum.2
  85.1 1.6 %collective-permute-start.11 = (f32[8,2176]{1,0:T(8,128)S(1)}, f32[8,2176]{1,0:T(8,128)S(1)}, u32[]{:S(2)}, u32[]{:S(2)}) collective-permute-start(f32[8,2176]{1,0:T(8,128)S(1)} %get-tuple-element.45), channel_id=1, source_target_pairs={{0,192},{32,224},{64,0},{96,32},{128,64},{160,96},{192,128},{224,1... | collective-permute-start | bytes 208904 | tf_op jit(solution)/shard_map/ppermute | solution.py:27
  86.7 0.0 collective-permute-done.16.refs_4_
  86.7 0.9 collective-permute-start.12
  87.6 0.2 collective-permute-done.17.refs_5_
  87.8 1.6 %collective-permute-start.13 = (f32[8,2176]{1,0:T(8,128)S(1)}, f32[8,2176]{1,0:T(8,128)S(1)}, u32[]{:S(2)}, u32[]{:S(2)}) collective-permute-start(f32[8,2176]{1,0:T(8,128)S(1)} %get-tuple-element.47), channel_id=1, source_target_pairs={{0,224},{32,0},{64,32},{96,64},{128,96},{160,128},{192,160},{224,1... | collective-permute-start | bytes 208904 | tf_op jit(solution)/shard_map/ppermute | solution.py:27
  90.0 0.0 collective-permute-done.18.refs_6_
  90.0 1.2 %collective-permute-done.19.refs_7_ = f32[8,2176]{1,0:T(8,128)S(1)} collective-permute-done((f32[8,2176]{1,0:T(8,128)S(1)}, f32[8,2176]{1,0:T(8,128)S(1)}, u32[]{:S(2)}, u32[]{:S(2)}) %collective-permute-start.19) | collective-permute-done | bytes 69664 | tf_op jit(solution)/shard_map/ppermute | solution.py:27
  91.2 1.8 %collective-permute-done.11.refs_0_ = f32[8,2176]{1,0:T(8,128)S(1)} collective-permute-done((f32[8,2176]{1,0:T(8,128)S(1)}, f32[8,2176]{1,0:T(8,128)S(1)}, u32[]{:S(2)}, u32[]{:S(2)}) %collective-permute-start.11) | collective-permute-done | bytes 69664 | tf_op jit(solution)/shard_map/ppermute | solution.py:27
  93.0 1.3 %collective-permute-done.12.refs_1_ = f32[8,2176]{1,0:T(8,128)S(1)} collective-permute-done((f32[8,2176]{1,0:T(8,128)S(1)}, f32[8,2176]{1,0:T(8,128)S(1)}, u32[]{:S(2)}, u32[]{:S(2)}) %collective-permute-start.12) | collective-permute-done | bytes 69664 | tf_op jit(solution)/shard_map/ppermute | solution.py:27
  94.4 0.0 collective-permute-done.13.refs_2_
  94.4 0.7 z_sum.1
  95.0 3.6 %collective-permute-start.20 = (f32[8,128]{1,0:T(8,128)S(1)}, f32[8,128]{1,0:T(8,128)S(1)}, u32[]{:S(2)}, u32[]{:S(2)}) collective-permute-start(f32[8,128]{1,0:T(8,128)S(1)} %get-tuple-element.60), channel_id=1, source_target_pairs={{0,1},{1,0},{2,3},{3,2},{4,5},{5,4},{6,7},{7,6},{8,9},{9,8},{10,11... | collective-permute-start | bytes 12296 | tf_op jit(solution)/shard_map/ppermute | solution.py:27
  98.7 0.8 collective-permute-done.20
  99.5 0.4 collective-permute-start.21
  99.9 1.7 %collective-permute-start.22 = (f32[8,128]{1,0:T(8,128)S(1)}, f32[8,128]{1,0:T(8,128)S(1)}, u32[]{:S(2)}, u32[]{:S(2)}) collective-permute-start(f32[8,128]{1,0:T(8,128)S(1)} %add.20.a), channel_id=1, source_target_pairs={{0,4},{2,6},{4,0},{6,2},{1,5},{3,7},{5,1},{7,3},{8,12},{10,14},{12... | collective-permute-start | bytes 12296 | tf_op jit(solution)/shard_map/ppermute | solution.py:27
  101.7 0.7 collective-permute-start.23
  102.3 1.7 %encode.1 = (bf16[256,1664]{1,0:T(8,128)(2,1)}, f32[104,256]{1,0:T(8,128)}, f32[8,128]{1,0:T(8,128)S(1)}) custom-call(s32[4]{0:T(128)S(1)} %pad_add_fusion.place, f32[32,1664]{1,0:T(8,128)S(1)} %hand_on.4.refs_0_, f32[32,1664]{1,0:T(8,128)S(1)} %hand_on.5.refs_1_, f32[32,1664]{1,0:T(8,128)S(1)} %hand_on.6.refs_2_, f32[32,1664]{1,0:T(8,128)S(1)} %hand_on.7.refs_3_, ...), custom_call_target="tpu_custom_call" | custom-call | tf_op jit(solution)/shard_map/encode/pallas_call | solution.py:385
  104.1 0.0 collective-permute-done.21.b
  104.1 0.3 collective-permute-done.23.d
  104.4 0.7 norm.1
  (17 shorter events, 0.2 us)
Async XLA Ops:
  39.3 14.9 %collective-permute-start.2 = (f32[32,1664]{1,0:T(8,128)S(1)}, f32[32,1664]{1,0:T(8,128)S(1)}, u32[]{:S(2)}, u32[]{:S(2)}) collective-permute-start(f32[32,1664]{1,0:T(8,128)S(1)} %bitcast.13), channel_id=1, source_target_pairs={{0,6},{2,0},{4,2},{6,4},{1,7},{3,1},{5,3},{7,5},{8,14},{10,8},{12,... | collective-permute-start | bytes 638984 | tf_op jit(solution)/shard_map/ppermute | solution.py:27
  41.9 12.5 %collective-permute-start.1 = (f32[32,1664]{1,0:T(8,128)S(1)}, f32[32,1664]{1,0:T(8,128)S(1)}, u32[]{:S(2)}, u32[]{:S(2)}) collective-permute-start(f32[32,1664]{1,0:T(8,128)S(1)} %bitcast.14), channel_id=1, source_target_pairs={{0,4},{2,6},{4,0},{6,2},{1,5},{3,7},{5,1},{7,3},{8,12},{10,14},{12... | collective-permute-start | bytes 638984 | tf_op jit(solution)/shard_map/ppermute | solution.py:27
  42.4 12.5 %collective-permute-start = (f32[32,1664]{1,0:T(8,128)S(1)}, f32[32,1664]{1,0:T(8,128)S(1)}, u32[]{:S(2)}, u32[]{:S(2)}) collective-permute-start(f32[32,1664]{1,0:T(8,128)S(1)} %bitcast.15), channel_id=1, source_target_pairs={{0,2},{2,4},{4,6},{6,0},{1,3},{3,5},{5,7},{7,1},{8,10},{10,12},{12... | collective-permute-start | bytes 638984 | tf_op jit(solution)/shard_map/ppermute | solution.py:27
  43.0 1.0 copy-start
  50.1 5.7 %collective-permute-start.3 = (f32[32,1664]{1,0:T(8,128)S(1)}, f32[32,1664]{1,0:T(8,128)S(1)}, u32[]{:S(2)}, u32[]{:S(2)}) collective-permute-start(f32[32,1664]{1,0:T(8,128)S(1)} %hand_on.4.refs_0_), channel_id=1, source_target_pairs={{0,1},{1,0},{2,3},{3,2},{4,5},{5,4},{6,7},{7,6},{8,9},{9,8},{10,11... | collective-permute-start | bytes 638984 | tf_op jit(solution)/shard_map/ppermute | solution.py:27
  54.2 1.6 %collective-permute-start.6 = (f32[32,1664]{1,0:T(8,128)S(1)}, f32[32,1664]{1,0:T(8,128)S(1)}, u32[]{:S(2)}, u32[]{:S(2)}) collective-permute-start(f32[32,1664]{1,0:T(8,128)S(1)} %hand_on.7.refs_3_), channel_id=1, source_target_pairs={{0,1},{1,0},{2,3},{3,2},{4,5},{5,4},{6,7},{7,6},{8,9},{9,8},{10,11... | collective-permute-start | bytes 638984 | tf_op jit(solution)/shard_map/ppermute | solution.py:27
  54.4 1.7 %collective-permute-start.5 = (f32[32,1664]{1,0:T(8,128)S(1)}, f32[32,1664]{1,0:T(8,128)S(1)}, u32[]{:S(2)}, u32[]{:S(2)}) collective-permute-start(f32[32,1664]{1,0:T(8,128)S(1)} %hand_on.6.refs_2_), channel_id=1, source_target_pairs={{0,1},{1,0},{2,3},{3,2},{4,5},{5,4},{6,7},{7,6},{8,9},{9,8},{10,11... | collective-permute-start | bytes 638984 | tf_op jit(solution)/shard_map/ppermute | solution.py:27
  55.0 1.9 %collective-permute-start.4 = (f32[32,1664]{1,0:T(8,128)S(1)}, f32[32,1664]{1,0:T(8,128)S(1)}, u32[]{:S(2)}, u32[]{:S(2)}) collective-permute-start(f32[32,1664]{1,0:T(8,128)S(1)} %hand_on.5.refs_1_), channel_id=1, source_target_pairs={{0,1},{1,0},{2,3},{3,2},{4,5},{5,4},{6,7},{7,6},{8,9},{9,8},{10,11... | collective-permute-start | bytes 638984 | tf_op jit(solution)/shard_map/ppermute | solution.py:27
  56.8 37.5 %copy-start.1 = (bf16[8,2048]{1,0:T(8,128)(2,1)S(1)}, bf16[8,2048]{1,0:T(8,128)(2,1)}, u32[]{:S(2)}) copy-start(bf16[8,2048]{1,0:T(8,128)(2,1)} %refs_8_.1) | copy-start | bytes 98308
  56.8 45.5 %copy-start.2 = (bf16[2048]{0:T(1024)(128)(2,1)S(1)}, bf16[2048]{0:T(1024)(128)(2,1)}, u32[]{:S(2)}) copy-start(bf16[2048]{0:T(1024)(128)(2,1)} %param.13) | copy-start | bytes 12292
  61.8 7.9 %collective-permute-start.7 = (f32[32,2176]{1,0:T(8,128)S(1)}, f32[32,2176]{1,0:T(8,128)S(1)}, u32[]{:S(2)}, u32[]{:S(2)}) collective-permute-start(f32[32,2176]{1,0:T(8,128)S(1)} %get-tuple-element.39), channel_id=1, source_target_pairs={{0,24},{8,0},{16,8},{24,16},{1,25},{9,1},{17,9},{25,17},{2,26},{10... | collective-permute-start | bytes 835592 | tf_op jit(solution)/shard_map/ppermute | solution.py:27
  63.0 9.3 %collective-permute-start.8 = (f32[32,2176]{1,0:T(8,128)S(1)}, f32[32,2176]{1,0:T(8,128)S(1)}, u32[]{:S(2)}, u32[]{:S(2)}) collective-permute-start(f32[32,2176]{1,0:T(8,128)S(1)} %get-tuple-element.43), channel_id=1, source_target_pairs={{0,8},{8,16},{16,24},{24,0},{1,9},{9,17},{17,25},{25,1},{2,10},{10... | collective-permute-start | bytes 835592 | tf_op jit(solution)/shard_map/ppermute | solution.py:27
  66.1 11.6 %collective-permute-start.14 = (f32[32,2176]{1,0:T(8,128)S(1)}, f32[32,2176]{1,0:T(8,128)S(1)}, u32[]{:S(2)}, u32[]{:S(2)}) collective-permute-start(f32[32,2176]{1,0:T(8,128)S(1)} %get-tuple-element.50), channel_id=1, source_target_pairs={{0,8},{8,16},{16,24},{24,0},{1,9},{9,17},{17,25},{25,1},{2,10},{10... | collective-permute-start | bytes 835592 | tf_op jit(solution)/shard_map/ppermute | solution.py:27
  69.8 8.0 %collective-permute-start.15 = (f32[32,2176]{1,0:T(8,128)S(1)}, f32[32,2176]{1,0:T(8,128)S(1)}, u32[]{:S(2)}, u32[]{:S(2)}) collective-permute-start(f32[32,2176]{1,0:T(8,128)S(1)} %relay.2.refs_5_), channel_id=1, source_target_pairs={{0,24},{8,0},{16,8},{24,16},{1,25},{9,1},{17,9},{25,17},{2,26},{10... | collective-permute-start | bytes 835592 | tf_op jit(solution)/shard_map/ppermute | solution.py:27
  72.2 10.7 %collective-permute-start.10 = (f32[32,2176]{1,0:T(8,128)S(1)}, f32[32,2176]{1,0:T(8,128)S(1)}, u32[]{:S(2)}, u32[]{:S(2)}) collective-permute-start(f32[32,2176]{1,0:T(8,128)S(1)} %get-tuple-element.44), channel_id=1, source_target_pairs={{0,24},{8,0},{16,8},{24,16},{1,25},{9,1},{17,9},{25,17},{2,26},{10... | collective-permute-start | bytes 835592 | tf_op jit(solution)/shard_map/ppermute | solution.py:27
  72.4 12.7 %collective-permute-start.9 = (f32[32,2176]{1,0:T(8,128)S(1)}, f32[32,2176]{1,0:T(8,128)S(1)}, u32[]{:S(2)}, u32[]{:S(2)}) collective-permute-start(f32[32,2176]{1,0:T(8,128)S(1)} %relay.3), channel_id=1, source_target_pairs={{0,8},{8,16},{16,24},{24,0},{1,9},{9,17},{17,25},{25,1},{2,10},{10... | collective-permute-start | bytes 835592 | tf_op jit(solution)/shard_map/ppermute | solution.py:27
  77.8 8.9 %collective-permute-start.16 = (f32[8,2176]{1,0:T(8,128)S(1)}, f32[8,2176]{1,0:T(8,128)S(1)}, u32[]{:S(2)}, u32[]{:S(2)}) collective-permute-start(f32[8,2176]{1,0:T(8,128)S(1)} %get-tuple-element.51), channel_id=1, source_target_pairs={{0,128},{32,160},{64,192},{96,224},{128,0},{160,32},{192,64},{224,... | collective-permute-start | bytes 208904 | tf_op jit(solution)/shard_map/ppermute | solution.py:27
  78.5 9.3 %collective-permute-start.17 = (f32[8,2176]{1,0:T(8,128)S(1)}, f32[8,2176]{1,0:T(8,128)S(1)}, u32[]{:S(2)}, u32[]{:S(2)}) collective-permute-start(f32[8,2176]{1,0:T(8,128)S(1)} %get-tuple-element.52), channel_id=1, source_target_pairs={{0,96},{32,128},{64,160},{96,192},{128,224},{160,0},{192,32},{224,... | collective-permute-start | bytes 208904 | tf_op jit(solution)/shard_map/ppermute | solution.py:27
  80.8 9.3 %collective-permute-start.18 = (f32[8,2176]{1,0:T(8,128)S(1)}, f32[8,2176]{1,0:T(8,128)S(1)}, u32[]{:S(2)}, u32[]{:S(2)}) collective-permute-start(f32[8,2176]{1,0:T(8,128)S(1)} %get-tuple-element.53), channel_id=1, source_target_pairs={{0,160},{32,192},{64,224},{96,0},{128,32},{160,64},{192,96},{224,1... | collective-permute-start | bytes 208904 | tf_op jit(solution)/shard_map/ppermute | solution.py:27
  83.0 8.2 %collective-permute-start.19 = (f32[8,2176]{1,0:T(8,128)S(1)}, f32[8,2176]{1,0:T(8,128)S(1)}, u32[]{:S(2)}, u32[]{:S(2)}) collective-permute-start(f32[8,2176]{1,0:T(8,128)S(1)} %get-tuple-element.54), channel_id=1, source_target_pairs={{0,64},{32,96},{64,128},{96,160},{128,192},{160,224},{192,0},{224,... | collective-permute-start | bytes 208904 | tf_op jit(solution)/shard_map/ppermute | solution.py:27
  85.1 7.9 %collective-permute-start.11 = (f32[8,2176]{1,0:T(8,128)S(1)}, f32[8,2176]{1,0:T(8,128)S(1)}, u32[]{:S(2)}, u32[]{:S(2)}) collective-permute-start(f32[8,2176]{1,0:T(8,128)S(1)} %get-tuple-element.45), channel_id=1, source_target_pairs={{0,192},{32,224},{64,0},{96,32},{128,64},{160,96},{192,128},{224,1... | collective-permute-start | bytes 208904 | tf_op jit(solution)/shard_map/ppermute | solution.py:27
  86.7 7.7 %collective-permute-start.12 = (f32[8,2176]{1,0:T(8,128)S(1)}, f32[8,2176]{1,0:T(8,128)S(1)}, u32[]{:S(2)}, u32[]{:S(2)}) collective-permute-start(f32[8,2176]{1,0:T(8,128)S(1)} %get-tuple-element.46), channel_id=1, source_target_pairs={{0,32},{32,64},{64,96},{96,128},{128,160},{160,192},{192,224},{224... | collective-permute-start | bytes 208904 | tf_op jit(solution)/shard_map/ppermute | solution.py:27
  87.8 6.6 %collective-permute-start.13 = (f32[8,2176]{1,0:T(8,128)S(1)}, f32[8,2176]{1,0:T(8,128)S(1)}, u32[]{:S(2)}, u32[]{:S(2)}) collective-permute-start(f32[8,2176]{1,0:T(8,128)S(1)} %get-tuple-element.47), channel_id=1, source_target_pairs={{0,224},{32,0},{64,32},{96,64},{128,96},{160,128},{192,160},{224,1... | collective-permute-start | bytes 208904 | tf_op jit(solution)/shard_map/ppermute | solution.py:27
  95.0 4.5 %collective-permute-start.20 = (f32[8,128]{1,0:T(8,128)S(1)}, f32[8,128]{1,0:T(8,128)S(1)}, u32[]{:S(2)}, u32[]{:S(2)}) collective-permute-start(f32[8,128]{1,0:T(8,128)S(1)} %get-tuple-element.60), channel_id=1, source_target_pairs={{0,1},{1,0},{2,3},{3,2},{4,5},{5,4},{6,7},{7,6},{8,9},{9,8},{10,11... | collective-permute-start | bytes 12296 | tf_op jit(solution)/shard_map/ppermute | solution.py:27
  99.5 4.6 %collective-permute-start.21 = (f32[8,128]{1,0:T(8,128)S(1)}, f32[8,128]{1,0:T(8,128)S(1)}, u32[]{:S(2)}, u32[]{:S(2)}) collective-permute-start(f32[8,128]{1,0:T(8,128)S(1)} %add.20.a), channel_id=1, source_target_pairs={{0,2},{2,4},{4,6},{6,0},{1,3},{3,5},{5,7},{7,1},{8,10},{10,12},{12... | collective-permute-start | bytes 12296 | tf_op jit(solution)/shard_map/ppermute | solution.py:27
  99.9 4.2 %collective-permute-start.22 = (f32[8,128]{1,0:T(8,128)S(1)}, f32[8,128]{1,0:T(8,128)S(1)}, u32[]{:S(2)}, u32[]{:S(2)}) collective-permute-start(f32[8,128]{1,0:T(8,128)S(1)} %add.20.a), channel_id=1, source_target_pairs={{0,4},{2,6},{4,0},{6,2},{1,5},{3,7},{5,1},{7,3},{8,12},{10,14},{12... | collective-permute-start | bytes 12296 | tf_op jit(solution)/shard_map/ppermute | solution.py:27
  101.7 2.8 %collective-permute-start.23 = (f32[8,128]{1,0:T(8,128)S(1)}, f32[8,128]{1,0:T(8,128)S(1)}, u32[]{:S(2)}, u32[]{:S(2)}) collective-permute-start(f32[8,128]{1,0:T(8,128)S(1)} %add.20.a), channel_id=1, source_target_pairs={{0,6},{2,0},{4,2},{6,4},{1,7},{3,1},{5,3},{7,5},{8,14},{10,8},{12,... | collective-permute-start | bytes 12296 | tf_op jit(solution)/shard_map/ppermute | solution.py:27

commit v5 on v4

--- a/solution.py
+++ b/solution.py
@@ -83,7 +83,7 @@
         hand_on_kernel,
         in_specs=[VMEM, ANY],
         out_specs=VMEM,
-        out_shape=jax.ShapeDtypeStruct((SLAB, WIDTH), jnp.float32),
+        out_shape=jax.ShapeDtypeStruct(block.shape, block.dtype),
         compiler_params=PARAMS,
         name="hand_on",
     )(block, after)
@@ -153,7 +153,7 @@
 BN = 512
 TILES = COLS // BN
 HALF = 32
-Z_ORDER = (6, 1, 7, 0, 4, 3, 5, 2)
+Z_ORDER = (6, 1, 7, 0, 3, 5, 4, 2)
 
 
 def product_kernel(place, *refs):
@@ -413,10 +413,11 @@
     slabs = mine + theirs
     here_a, here_b, ahead_a, ahead_b, far_a, far_b, behind_a, behind_b = product(slabs, weight, place)
     first, second = moved(far_a, "y", 1), moved(far_b, "y", -1)
-    ahead_b, behind_a = moved(ahead_b, "y", 1), moved(behind_a, "y", -1)
+    ahead_b = moved(ahead_b, "y", 1)
     mine_most, mine_factor = mine_blocks(mine, here_a)
     ahead_a, behind_b = relay(ahead_a, first, mine_most), relay(behind_b, second, mine_most)
     narrow, theirs_factor = theirs_blocks(place, theirs, mine_most, behind_b)
+    behind_a = moved(hand_on(behind_a, narrow), "y", -1)
     sums_a = y_sum(here_a, moved(ahead_a, "y", 1), behind_a, narrow)
     sums_b = y_sum(here_b, ahead_b, moved(behind_b, "y", -1), narrow)
     sums = [*sums_a, *sums_b]

time: 106 us -> 106 us (level)
  transfers between devices with their start and end apart: 24 -> 24, of which waited for: 10 -> 9; matrix products, arithmetic and copies ran while one was open for 0% -> 0% of each run, Pallas kernels for 14% -> 14%
where the time goes in v5:
time: 106 us; the launch traced here: 104 us
  blocking collectives  36.6 us (35%)
  starting transfers between devices  32.6 us (31%)
  Pallas kernels  21.1 us (20%)
  waiting for transfers between devices  10 us (9%)
  local copies, waits for them, and re-layouts  1.5 us (1%)
  between operations  1.45 us (1%)
  other arithmetic  1.1 us (1%)
    ppermute x24, starting transfers between devices, moved(): lax.ppermute(block, axis, [(i, (i + step) % count) for i in range(count)])  32.6 us
    all_to_all x1, blocking collectives, on_device(): one_row = lax.all_to_all(inner, ('z', 'y'), 0, 0, tiled=True)  21.9 us
    all_to_all x1, blocking collectives, on_device(): own = lax.all_to_all(turned, ('z', 'y'), 0, 0, tiled=True)  14.6 us
    ppermute x24, waiting for transfers between devices, moved(): lax.ppermute(block, axis, [(i, (i + step) % count) for i in range(count)])  10 us
    pallas_call x1, Pallas kernels, decode(): pl.pallas_call(decode_kernel, in_specs=[HBM, HBM, ANY], out_specs=[HBM, V...  6.08 us
    pallas_call x1, Pallas kernels, product(): pl.pallas_call(product_kernel, in_specs=[SMEM] + [VMEM] * 8 + [HBM], out_...  4.93 us
    pallas_call x1, Pallas kernels, theirs_blocks(): pl.pallas_call(theirs_kernel, in_specs=[SMEM] + [VMEM] * 5 + [ANY], out_s...  3.43 us
    pallas_call x1, Pallas kernels, mine_blocks(): pl.pallas_call(mine_kernel, in_specs=[VMEM] * 4 + [ANY], out_specs=[VMEM]...  2.8 us
  transfers between devices with their start and end apart: 24, of which 9 were waited for; matrix products, arithmetic and copies ran while one was open for 0% of the time, Pallas kernels for 14%

profile of v5, /device:TPU:1, one launch (start us, length us, event | category | flops | bytes accessed | tf_op | source)
XLA Modules:
  0.0 104.4 jit_solution(1207153416612010947)
XLA Ops:
  0.6 1.0 fusion.3.hidden
  1.7 0.2 inner_transform.1
  1.9 0.2 copy.11
  2.1 21.9 %all_to_all.22 = f32[32,1,1664]{2,1,0:T(1,128)S(1)} all-to-all(f32[32,1,1664]{2,1,0:T(1,128)S(1)} %copy.11), channel_id=1, replica_groups=mesh['z'=8,'y'=4,'x'=4,'c'=2] {'z','y'}, dimensions={0} | all-to-all | bytes 425984 | tf_op jit(solution)/shard_map/all_to_all | solution.py:405
  24.1 0.3 outer_transform.1
  24.4 0.2 copy.12
  24.7 14.6 %all_to_all.23 = f32[32,1,1664]{2,1,0:T(1,128)S(1)} all-to-all(f32[32,1,1664]{2,1,0:T(1,128)S(1)} %copy.12), channel_id=1, replica_groups=mesh['z'=8,'y'=4,'x'=4,'c'=2] {'z','y'}, dimensions={0} | all-to-all | bytes 425984 | tf_op jit(solution)/shard_map/all_to_all | solution.py:407
  39.3 2.6 %collective-permute-start.2 = (f32[32,1664]{1,0:T(8,128)S(1)}, f32[32,1664]{1,0:T(8,128)S(1)}, u32[]{:S(2)}, u32[]{:S(2)}) collective-permute-start(f32[32,1664]{1,0:T(8,128)S(1)} %bitcast.13), channel_id=1, source_target_pairs={{0,6},{2,0},{4,2},{6,4},{1,7},{3,1},{5,3},{7,5},{8,14},{10,8},{12,... | collective-permute-start | bytes 638984 | tf_op jit(solution)/shard_map/ppermute | solution.py:27
  41.9 0.5 collective-permute-start.1
  42.4 0.6 collective-permute-start
  43.0 1.0 copy-done
  44.0 6.1 %decode.1 = (bf16[1664,2048]{1,0:T(8,128)(2,1)}, f32[8,128]{1,0:T(8,128)S(1)}) custom-call(bf16[1664,2048]{1,0:T(8,128)(2,1)} %codes.1, bf16[104,2048]{1,0:T(8,128)(2,1)S(1)} %copy-done, f32[32,1664]{1,0:T(8,128)S(1)} %bitcast.16), custom_call_target="tpu_custom_call" | custom-call | flops 3407872 | bytes 14680064 | tf_op jit(solution)/shard_map/decode/pallas_call | solution.py:132
  50.1 4.1 %collective-permute-start.3 = (f32[32,1664]{1,0:T(8,128)S(1)}, f32[32,1664]{1,0:T(8,128)S(1)}, u32[]{:S(2)}, u32[]{:S(2)}) collective-permute-start(f32[32,1664]{1,0:T(8,128)S(1)} %hand_on.5.refs_0_), channel_id=1, source_target_pairs={{0,1},{1,0},{2,3},{3,2},{4,5},{5,4},{6,7},{7,6},{8,9},{9,8},{10,11... | collective-permute-start | bytes 638984 | tf_op jit(solution)/shard_map/ppermute | solution.py:27
  54.2 0.0 collective-permute-done.2.block
  54.2 0.1 collective-permute-start.6
  54.3 0.0 collective-permute-done.1.block
  54.4 0.6 collective-permute-start.5
  54.9 0.0 collective-permute-done.block
  55.0 0.8 collective-permute-start.4
  55.7 0.1 pad_add_fusion.place
  55.8 0.0 collective-permute-done.3.refs_4_.refs_0_
  55.8 0.0 collective-permute-done.6.refs_7_.refs_3_
  55.8 0.3 collective-permute-done.5.refs_6_.refs_2_
  56.1 0.7 collective-permute-done.4.refs_5_.refs_1_
  56.8 4.9 %product.1 = (f32[32,2176]{1,0:T(8,128)S(1)}, f32[32,2176]{1,0:T(8,128)S(1)}, f32[32,2176]{1,0:T(8,128)S(1)}, f32[32,2176]{1,0:T(8,128)S(1)}, f32[32,2176]{1,0:T...) custom-call(s32[4]{0:T(128)S(1)} %pad_add_fusion.place, ...), custom_call_target="tpu_custom_call" | custom-call | tf_op jit(solution)/shard_map/product/pallas_call | solution.py:194
  61.8 1.3 %collective-permute-start.7 = (f32[32,2176]{1,0:T(8,128)S(1)}, f32[32,2176]{1,0:T(8,128)S(1)}, u32[]{:S(2)}, u32[]{:S(2)}) collective-permute-start(f32[32,2176]{1,0:T(8,128)S(1)} %get-tuple-element.39), channel_id=1, source_target_pairs={{0,24},{8,0},{16,8},{24,16},{1,25},{9,1},{17,9},{25,17},{2,26},{10... | collective-permute-start | bytes 835592 | tf_op jit(solution)/shard_map/ppermute | solution.py:27
  63.0 0.3 collective-permute-start.8
  63.3 2.8 %mine_blocks.1 = (f32[128,104]{1,0:T(8,128)S(1)}, f32[128,1664]{1,0:T(8,128)S(1)}) custom-call(f32[32,1664]{1,0:T(8,128)S(1)} %hand_on.5.refs_0_, f32[32,1664]{1,0:T(8,128)S(1)} %hand_on.6.refs_1_, f32[32,1664]{1,0:T(8,128)S(1)} %hand_on.7.refs_2_, f32[32,1664]{1,0:T(8,128)S(1)} %hand_on.8.refs_3_, f32[32,2176]{1,0:T(8,128)S(1)} %get-tuple-element.35.refs_4_.a), custom_call_target="tpu_custom_call" | custom-call | tf_op jit(solution)/shard_map/mine_blocks/pallas_call | solution.py:337
  66.1 0.1 collective-permute-start.14
  66.2 3.5 %collective-permute-done.7.arrived = f32[32,2176]{1,0:T(8,128)S(1)} collective-permute-done((f32[32,2176]{1,0:T(8,128)S(1)}, f32[32,2176]{1,0:T(8,128)S(1)}, u32[]{:S(2)}, u32[]{:S(2)}) %collective-permute-start.7) | collective-permute-done | bytes 278560 | tf_op jit(solution)/shard_map/ppermute | solution.py:27
  69.8 2.5 %collective-permute-start.15 = (f32[32,2176]{1,0:T(8,128)S(1)}, f32[32,2176]{1,0:T(8,128)S(1)}, u32[]{:S(2)}, u32[]{:S(2)}) collective-permute-start(f32[32,2176]{1,0:T(8,128)S(1)} %relay.2.refs_5_), channel_id=1, source_target_pairs={{0,24},{8,0},{16,8},{24,16},{1,25},{9,1},{17,9},{25,17},{2,26},{10... | collective-permute-start | bytes 835592 | tf_op jit(solution)/shard_map/ppermute | solution.py:27
  72.2 3.4 %theirs_blocks.1 = (f32[104,256]{1,0:T(8,128)S(1)}, f32[128,1664]{1,0:T(8,128)S(1)}) custom-call(s32[4]{0:T(128)S(1)} %pad_add_fusion.place, f32[32,1664]{1,0:T(8,128)S(1)} %collective-permute-done.3.refs_4_.refs_0_, f32[32,1664]{1,0:T(8,128)S(1)} %collective-permute-done.4.refs_5_.refs_1_, f32[32,1664]{1,0:T(8,128)S(1)} %collective-permute-done.5.refs_6_.refs_2_, ...), custom_call_target="tpu_custom_call" | custom-call | tf_op jit(solution)/shard_map/theirs_blocks/pallas_call | solution.py:352
  75.7 0.1 collective-permute-start.10
  75.8 0.0 collective-permute-done.8.arrived
  75.8 1.5 %collective-permute-start.9 = (f32[32,2176]{1,0:T(8,128)S(1)}, f32[32,2176]{1,0:T(8,128)S(1)}, u32[]{:S(2)}, u32[]{:S(2)}) collective-permute-start(f32[32,2176]{1,0:T(8,128)S(1)} %relay.3), channel_id=1, source_target_pairs={{0,8},{8,16},{16,24},{24,0},{1,9},{9,17},{17,25},{25,1},{2,10},{10... | collective-permute-start | bytes 835592 | tf_op jit(solution)/shard_map/ppermute | solution.py:27
  77.4 0.4 collective-permute-done.14.b
  77.8 0.0 collective-permute-done.15.c
  77.8 0.7 collective-permute-start.16
  78.5 3.9 %collective-permute-start.17 = (f32[8,2176]{1,0:T(8,128)S(1)}, f32[8,2176]{1,0:T(8,128)S(1)}, u32[]{:S(2)}, u32[]{:S(2)}) collective-permute-start(f32[8,2176]{1,0:T(8,128)S(1)} %get-tuple-element.52), channel_id=1, source_target_pairs={{0,160},{32,192},{64,224},{96,0},{128,32},{160,64},{192,96},{224,1... | collective-permute-start | bytes 208904 | tf_op jit(solution)/shard_map/ppermute | solution.py:27
  82.4 0.6 collective-permute-start.18
  83.0 0.0 collective-permute-done.10.c
  83.0 2.1 %collective-permute-start.19 = (f32[8,2176]{1,0:T(8,128)S(1)}, f32[8,2176]{1,0:T(8,128)S(1)}, u32[]{:S(2)}, u32[]{:S(2)}) collective-permute-start(f32[8,2176]{1,0:T(8,128)S(1)} %get-tuple-element.54), channel_id=1, source_target_pairs={{0,64},{32,96},{64,128},{96,160},{128,192},{160,224},{192,0},{224,... | collective-permute-start | bytes 208904 | tf_op jit(solution)/shard_map/ppermute | solution.py:27
  85.0 0.0 collective-permute-done.9.b
  85.1 1.6 %collective-permute-start.11 = (f32[8,2176]{1,0:T(8,128)S(1)}, f32[8,2176]{1,0:T(8,128)S(1)}, u32[]{:S(2)}, u32[]{:S(2)}) collective-permute-start(f32[8,2176]{1,0:T(8,128)S(1)} %get-tuple-element.45), channel_id=1, source_target_pairs={{0,192},{32,224},{64,0},{96,32},{128,64},{160,96},{192,128},{224,1... | collective-permute-start | bytes 208904 | tf_op jit(solution)/shard_map/ppermute | solution.py:27
  86.7 0.0 collective-permute-done.16.refs_4_
  86.7 0.9 collective-permute-start.12
  87.5 0.0 collective-permute-done.17.refs_5_
  87.5 1.8 %collective-permute-start.13 = (f32[8,2176]{1,0:T(8,128)S(1)}, f32[8,2176]{1,0:T(8,128)S(1)}, u32[]{:S(2)}, u32[]{:S(2)}) collective-permute-start(f32[8,2176]{1,0:T(8,128)S(1)} %get-tuple-element.47), channel_id=1, source_target_pairs={{0,224},{32,0},{64,32},{96,64},{128,96},{160,128},{192,160},{224,1... | collective-permute-start | bytes 208904 | tf_op jit(solution)/shard_map/ppermute | solution.py:27
  90.0 0.0 collective-permute-done.18.refs_6_
  90.0 0.5 collective-permute-done.19.refs_7_
  90.5 2.3 %collective-permute-done.11.refs_0_ = f32[8,2176]{1,0:T(8,128)S(1)} collective-permute-done((f32[8,2176]{1,0:T(8,128)S(1)}, f32[8,2176]{1,0:T(8,128)S(1)}, u32[]{:S(2)}, u32[]{:S(2)}) %collective-permute-start.11) | collective-permute-done | bytes 69664 | tf_op jit(solution)/shard_map/ppermute | solution.py:27
  92.8 0.0 collective-permute-done.12.refs_1_
  92.8 1.1 %collective-permute-done.13.refs_2_ = f32[8,2176]{1,0:T(8,128)S(1)} collective-permute-done((f32[8,2176]{1,0:T(8,128)S(1)}, f32[8,2176]{1,0:T(8,128)S(1)}, u32[]{:S(2)}, u32[]{:S(2)}) %collective-permute-start.13) | collective-permute-done | bytes 69664 | tf_op jit(solution)/shard_map/ppermute | solution.py:27
  93.9 0.7 z_sum.1
  94.6 2.7 %collective-permute-start.20 = (f32[8,128]{1,0:T(8,128)S(1)}, f32[8,128]{1,0:T(8,128)S(1)}, u32[]{:S(2)}, u32[]{:S(2)}) collective-permute-start(f32[8,128]{1,0:T(8,128)S(1)} %get-tuple-element.60), channel_id=1, source_target_pairs={{0,1},{1,0},{2,3},{3,2},{4,5},{5,4},{6,7},{7,6},{8,9},{9,8},{10,11... | collective-permute-start | bytes 12296 | tf_op jit(solution)/shard_map/ppermute | solution.py:27
  97.3 0.8 collective-permute-done.20
  98.1 1.1 %collective-permute-start.21 = (f32[8,128]{1,0:T(8,128)S(1)}, f32[8,128]{1,0:T(8,128)S(1)}, u32[]{:S(2)}, u32[]{:S(2)}) collective-permute-start(f32[8,128]{1,0:T(8,128)S(1)} %add.20.a), channel_id=1, source_target_pairs={{0,2},{2,4},{4,6},{6,0},{1,3},{3,5},{5,7},{7,1},{8,10},{10,12},{12... | collective-permute-start | bytes 12296 | tf_op jit(solution)/shard_map/ppermute | solution.py:27
  99.2 1.7 %collective-permute-start.22 = (f32[8,128]{1,0:T(8,128)S(1)}, f32[8,128]{1,0:T(8,128)S(1)}, u32[]{:S(2)}, u32[]{:S(2)}) collective-permute-start(f32[8,128]{1,0:T(8,128)S(1)} %add.20.a), channel_id=1, source_target_pairs={{0,4},{2,6},{4,0},{6,2},{1,5},{3,7},{5,1},{7,3},{8,12},{10,14},{12... | collective-permute-start | bytes 12296 | tf_op jit(solution)/shard_map/ppermute | solution.py:27
  100.9 0.7 collective-permute-start.23
  101.6 1.7 %encode.1 = (bf16[256,1664]{1,0:T(8,128)(2,1)}, f32[104,256]{1,0:T(8,128)}, f32[8,128]{1,0:T(8,128)S(1)}) custom-call(s32[4]{0:T(128)S(1)} %pad_add_fusion.place, f32[32,1664]{1,0:T(8,128)S(1)} %hand_on.5.refs_0_, f32[32,1664]{1,0:T(8,128)S(1)} %hand_on.6.refs_1_, f32[32,1664]{1,0:T(8,128)S(1)} %hand_on.7.refs_2_, f32[32,1664]{1,0:T(8,128)S(1)} %hand_on.8.refs_3_, ...), custom_call_target="tpu_custom_call" | custom-call | tf_op jit(solution)/shard_map/encode/pallas_call | solution.py:385
  103.4 0.0 collective-permute-done.21.b
  103.4 0.0 collective-permute-done.22.c
  103.4 0.3 collective-permute-done.23.d
  103.7 0.7 norm.1
  (18 shorter events, 0.3 us)
Async XLA Ops:
  39.3 14.9 %collective-permute-start.2 = (f32[32,1664]{1,0:T(8,128)S(1)}, f32[32,1664]{1,0:T(8,128)S(1)}, u32[]{:S(2)}, u32[]{:S(2)}) collective-permute-start(f32[32,1664]{1,0:T(8,128)S(1)} %bitcast.13), channel_id=1, source_target_pairs={{0,6},{2,0},{4,2},{6,4},{1,7},{3,1},{5,3},{7,5},{8,14},{10,8},{12,... | collective-permute-start | bytes 638984 | tf_op jit(solution)/shard_map/ppermute | solution.py:27
  41.9 12.5 %collective-permute-start.1 = (f32[32,1664]{1,0:T(8,128)S(1)}, f32[32,1664]{1,0:T(8,128)S(1)}, u32[]{:S(2)}, u32[]{:S(2)}) collective-permute-start(f32[32,1664]{1,0:T(8,128)S(1)} %bitcast.14), channel_id=1, source_target_pairs={{0,4},{2,6},{4,0},{6,2},{1,5},{3,7},{5,1},{7,3},{8,12},{10,14},{12... | collective-permute-start | bytes 638984 | tf_op jit(solution)/shard_map/ppermute | solution.py:27
  42.4 12.5 %collective-permute-start = (f32[32,1664]{1,0:T(8,128)S(1)}, f32[32,1664]{1,0:T(8,128)S(1)}, u32[]{:S(2)}, u32[]{:S(2)}) collective-permute-start(f32[32,1664]{1,0:T(8,128)S(1)} %bitcast.15), channel_id=1, source_target_pairs={{0,2},{2,4},{4,6},{6,0},{1,3},{3,5},{5,7},{7,1},{8,10},{10,12},{12... | collective-permute-start | bytes 638984 | tf_op jit(solution)/shard_map/ppermute | solution.py:27
  43.0 1.0 copy-start
  50.1 5.7 %collective-permute-start.3 = (f32[32,1664]{1,0:T(8,128)S(1)}, f32[32,1664]{1,0:T(8,128)S(1)}, u32[]{:S(2)}, u32[]{:S(2)}) collective-permute-start(f32[32,1664]{1,0:T(8,128)S(1)} %hand_on.5.refs_0_), channel_id=1, source_target_pairs={{0,1},{1,0},{2,3},{3,2},{4,5},{5,4},{6,7},{7,6},{8,9},{9,8},{10,11... | collective-permute-start | bytes 638984 | tf_op jit(solution)/shard_map/ppermute | solution.py:27
  54.2 1.6 %collective-permute-start.6 = (f32[32,1664]{1,0:T(8,128)S(1)}, f32[32,1664]{1,0:T(8,128)S(1)}, u32[]{:S(2)}, u32[]{:S(2)}) collective-permute-start(f32[32,1664]{1,0:T(8,128)S(1)} %hand_on.8.refs_3_), channel_id=1, source_target_pairs={{0,1},{1,0},{2,3},{3,2},{4,5},{5,4},{6,7},{7,6},{8,9},{9,8},{10,11... | collective-permute-start | bytes 638984 | tf_op jit(solution)/shard_map/ppermute | solution.py:27
  54.4 1.7 %collective-permute-start.5 = (f32[32,1664]{1,0:T(8,128)S(1)}, f32[32,1664]{1,0:T(8,128)S(1)}, u32[]{:S(2)}, u32[]{:S(2)}) collective-permute-start(f32[32,1664]{1,0:T(8,128)S(1)} %hand_on.7.refs_2_), channel_id=1, source_target_pairs={{0,1},{1,0},{2,3},{3,2},{4,5},{5,4},{6,7},{7,6},{8,9},{9,8},{10,11... | collective-permute-start | bytes 638984 | tf_op jit(solution)/shard_map/ppermute | solution.py:27
  55.0 1.9 %collective-permute-start.4 = (f32[32,1664]{1,0:T(8,128)S(1)}, f32[32,1664]{1,0:T(8,128)S(1)}, u32[]{:S(2)}, u32[]{:S(2)}) collective-permute-start(f32[32,1664]{1,0:T(8,128)S(1)} %hand_on.6.refs_1_), channel_id=1, source_target_pairs={{0,1},{1,0},{2,3},{3,2},{4,5},{5,4},{6,7},{7,6},{8,9},{9,8},{10,11... | collective-permute-start | bytes 638984 | tf_op jit(solution)/shard_map/ppermute | solution.py:27
  56.8 37.1 %copy-start.1 = (bf16[8,2048]{1,0:T(8,128)(2,1)S(1)}, bf16[8,2048]{1,0:T(8,128)(2,1)}, u32[]{:S(2)}) copy-start(bf16[8,2048]{1,0:T(8,128)(2,1)} %refs_8_.1) | copy-start | bytes 98308
  56.8 44.8 %copy-start.2 = (bf16[2048]{0:T(1024)(128)(2,1)S(1)}, bf16[2048]{0:T(1024)(128)(2,1)}, u32[]{:S(2)}) copy-start(bf16[2048]{0:T(1024)(128)(2,1)} %param.13) | copy-start | bytes 12292
  61.8 7.9 %collective-permute-start.7 = (f32[32,2176]{1,0:T(8,128)S(1)}, f32[32,2176]{1,0:T(8,128)S(1)}, u32[]{:S(2)}, u32[]{:S(2)}) collective-permute-start(f32[32,2176]{1,0:T(8,128)S(1)} %get-tuple-element.39), channel_id=1, source_target_pairs={{0,24},{8,0},{16,8},{24,16},{1,25},{9,1},{17,9},{25,17},{2,26},{10... | collective-permute-start | bytes 835592 | tf_op jit(solution)/shard_map/ppermute | solution.py:27
  63.0 12.8 %collective-permute-start.8 = (f32[32,2176]{1,0:T(8,128)S(1)}, f32[32,2176]{1,0:T(8,128)S(1)}, u32[]{:S(2)}, u32[]{:S(2)}) collective-permute-start(f32[32,2176]{1,0:T(8,128)S(1)} %get-tuple-element.43), channel_id=1, source_target_pairs={{0,8},{8,16},{16,24},{24,0},{1,9},{9,17},{17,25},{25,1},{2,10},{10... | collective-permute-start | bytes 835592 | tf_op jit(solution)/shard_map/ppermute | solution.py:27
  66.1 11.6 %collective-permute-start.14 = (f32[32,2176]{1,0:T(8,128)S(1)}, f32[32,2176]{1,0:T(8,128)S(1)}, u32[]{:S(2)}, u32[]{:S(2)}) collective-permute-start(f32[32,2176]{1,0:T(8,128)S(1)} %get-tuple-element.50), channel_id=1, source_target_pairs={{0,8},{8,16},{16,24},{24,0},{1,9},{9,17},{17,25},{25,1},{2,10},{10... | collective-permute-start | bytes 835592 | tf_op jit(solution)/shard_map/ppermute | solution.py:27
  69.8 8.0 %collective-permute-start.15 = (f32[32,2176]{1,0:T(8,128)S(1)}, f32[32,2176]{1,0:T(8,128)S(1)}, u32[]{:S(2)}, u32[]{:S(2)}) collective-permute-start(f32[32,2176]{1,0:T(8,128)S(1)} %relay.2.refs_5_), channel_id=1, source_target_pairs={{0,24},{8,0},{16,8},{24,16},{1,25},{9,1},{17,9},{25,17},{2,26},{10... | collective-permute-start | bytes 835592 | tf_op jit(solution)/shard_map/ppermute | solution.py:27
  75.7 7.3 %collective-permute-start.10 = (f32[32,2176]{1,0:T(8,128)S(1)}, f32[32,2176]{1,0:T(8,128)S(1)}, u32[]{:S(2)}, u32[]{:S(2)}) collective-permute-start(f32[32,2176]{1,0:T(8,128)S(1)} %hand_on.9), channel_id=1, source_target_pairs={{0,24},{8,0},{16,8},{24,16},{1,25},{9,1},{17,9},{25,17},{2,26},{10... | collective-permute-start | bytes 835592 | tf_op jit(solution)/shard_map/ppermute | solution.py:27
  75.8 9.2 %collective-permute-start.9 = (f32[32,2176]{1,0:T(8,128)S(1)}, f32[32,2176]{1,0:T(8,128)S(1)}, u32[]{:S(2)}, u32[]{:S(2)}) collective-permute-start(f32[32,2176]{1,0:T(8,128)S(1)} %relay.3), channel_id=1, source_target_pairs={{0,8},{8,16},{16,24},{24,0},{1,9},{9,17},{17,25},{25,1},{2,10},{10... | collective-permute-start | bytes 835592 | tf_op jit(solution)/shard_map/ppermute | solution.py:27
  77.8 8.9 %collective-permute-start.16 = (f32[8,2176]{1,0:T(8,128)S(1)}, f32[8,2176]{1,0:T(8,128)S(1)}, u32[]{:S(2)}, u32[]{:S(2)}) collective-permute-start(f32[8,2176]{1,0:T(8,128)S(1)} %get-tuple-element.51), channel_id=1, source_target_pairs={{0,96},{32,128},{64,160},{96,192},{128,224},{160,0},{192,32},{224,... | collective-permute-start | bytes 208904 | tf_op jit(solution)/shard_map/ppermute | solution.py:27
  78.5 9.0 %collective-permute-start.17 = (f32[8,2176]{1,0:T(8,128)S(1)}, f32[8,2176]{1,0:T(8,128)S(1)}, u32[]{:S(2)}, u32[]{:S(2)}) collective-permute-start(f32[8,2176]{1,0:T(8,128)S(1)} %get-tuple-element.52), channel_id=1, source_target_pairs={{0,160},{32,192},{64,224},{96,0},{128,32},{160,64},{192,96},{224,1... | collective-permute-start | bytes 208904 | tf_op jit(solution)/shard_map/ppermute | solution.py:27
  82.4 7.6 %collective-permute-start.18 = (f32[8,2176]{1,0:T(8,128)S(1)}, f32[8,2176]{1,0:T(8,128)S(1)}, u32[]{:S(2)}, u32[]{:S(2)}) collective-permute-start(f32[8,2176]{1,0:T(8,128)S(1)} %get-tuple-element.53), channel_id=1, source_target_pairs={{0,128},{32,160},{64,192},{96,224},{128,0},{160,32},{192,64},{224,... | collective-permute-start | bytes 208904 | tf_op jit(solution)/shard_map/ppermute | solution.py:27
  83.0 7.5 %collective-permute-start.19 = (f32[8,2176]{1,0:T(8,128)S(1)}, f32[8,2176]{1,0:T(8,128)S(1)}, u32[]{:S(2)}, u32[]{:S(2)}) collective-permute-start(f32[8,2176]{1,0:T(8,128)S(1)} %get-tuple-element.54), channel_id=1, source_target_pairs={{0,64},{32,96},{64,128},{96,160},{128,192},{160,224},{192,0},{224,... | collective-permute-start | bytes 208904 | tf_op jit(solution)/shard_map/ppermute | solution.py:27
  85.1 7.7 %collective-permute-start.11 = (f32[8,2176]{1,0:T(8,128)S(1)}, f32[8,2176]{1,0:T(8,128)S(1)}, u32[]{:S(2)}, u32[]{:S(2)}) collective-permute-start(f32[8,2176]{1,0:T(8,128)S(1)} %get-tuple-element.45), channel_id=1, source_target_pairs={{0,192},{32,224},{64,0},{96,32},{128,64},{160,96},{192,128},{224,1... | collective-permute-start | bytes 208904 | tf_op jit(solution)/shard_map/ppermute | solution.py:27
  86.7 6.2 %collective-permute-start.12 = (f32[8,2176]{1,0:T(8,128)S(1)}, f32[8,2176]{1,0:T(8,128)S(1)}, u32[]{:S(2)}, u32[]{:S(2)}) collective-permute-start(f32[8,2176]{1,0:T(8,128)S(1)} %get-tuple-element.46), channel_id=1, source_target_pairs={{0,32},{32,64},{64,96},{96,128},{128,160},{160,192},{192,224},{224... | collective-permute-start | bytes 208904 | tf_op jit(solution)/shard_map/ppermute | solution.py:27
  87.5 6.4 %collective-permute-start.13 = (f32[8,2176]{1,0:T(8,128)S(1)}, f32[8,2176]{1,0:T(8,128)S(1)}, u32[]{:S(2)}, u32[]{:S(2)}) collective-permute-start(f32[8,2176]{1,0:T(8,128)S(1)} %get-tuple-element.47), channel_id=1, source_target_pairs={{0,224},{32,0},{64,32},{96,64},{128,96},{160,128},{192,160},{224,1... | collective-permute-start | bytes 208904 | tf_op jit(solution)/shard_map/ppermute | solution.py:27
  94.6 3.5 %collective-permute-start.20 = (f32[8,128]{1,0:T(8,128)S(1)}, f32[8,128]{1,0:T(8,128)S(1)}, u32[]{:S(2)}, u32[]{:S(2)}) collective-permute-start(f32[8,128]{1,0:T(8,128)S(1)} %get-tuple-element.60), channel_id=1, source_target_pairs={{0,1},{1,0},{2,3},{3,2},{4,5},{5,4},{6,7},{7,6},{8,9},{9,8},{10,11... | collective-permute-start | bytes 12296 | tf_op jit(solution)/shard_map/ppermute | solution.py:27
  98.1 5.2 %collective-permute-start.21 = (f32[8,128]{1,0:T(8,128)S(1)}, f32[8,128]{1,0:T(8,128)S(1)}, u32[]{:S(2)}, u32[]{:S(2)}) collective-permute-start(f32[8,128]{1,0:T(8,128)S(1)} %add.20.a), channel_id=1, source_target_pairs={{0,2},{2,4},{4,6},{6,0},{1,3},{3,5},{5,7},{7,1},{8,10},{10,12},{12... | collective-permute-start | bytes 12296 | tf_op jit(solution)/shard_map/ppermute | solution.py:27
  99.2 4.2 %collective-permute-start.22 = (f32[8,128]{1,0:T(8,128)S(1)}, f32[8,128]{1,0:T(8,128)S(1)}, u32[]{:S(2)}, u32[]{:S(2)}) collective-permute-start(f32[8,128]{1,0:T(8,128)S(1)} %add.20.a), channel_id=1, source_target_pairs={{0,4},{2,6},{4,0},{6,2},{1,5},{3,7},{5,1},{7,3},{8,12},{10,14},{12... | collective-permute-start | bytes 12296 | tf_op jit(solution)/shard_map/ppermute | solution.py:27
  100.9 2.8 %collective-permute-start.23 = (f32[8,128]{1,0:T(8,128)S(1)}, f32[8,128]{1,0:T(8,128)S(1)}, u32[]{:S(2)}, u32[]{:S(2)}) collective-permute-start(f32[8,128]{1,0:T(8,128)S(1)} %add.20.a), channel_id=1, source_target_pairs={{0,6},{2,0},{4,2},{6,4},{1,7},{3,1},{5,3},{7,5},{8,14},{10,8},{12,... | collective-permute-start | bytes 12296 | tf_op jit(solution)/shard_map/ppermute | solution.py:27
